TPU v7x, 32 devices: a whole 2x2x4 slice. The times are simulated.
32 devices in a mesh: parts: 2 (over x), tile: 8 (over z, y), row: 2 (over core).
Axes of the slice: x: 2, y: 2, z: 4, core: 2. Of those that a mesh axis runs over, the one named last changes fastest.
Arguments:
- directions: bfloat16 [256, 32, 384], P(('parts', 'tile')), parts along dimension 0, may hold values from -6 to 6
- sensitivity: bfloat16 [16, 512, 12288], P(('parts', 'tile'), 'row'), parts along dimension 0, may hold values from -0.0546875 to 0.0546875
- data_weight: float32 [16, 512], P(('parts', 'tile'), 'row'), parts along dimension 0, may hold values from 1 to 4
- foot_list: int32 [16, 32], P(('parts', 'tile')), parts along dimension 0, may hold values from 0 to 127, as said below
- foot_mask: int32 [16, 32], P(('parts', 'tile')), parts along dimension 0, may hold values from 0 to 1, as said below
Outputs:
- gradient: float32 [256, 32, 384], P(('parts', 'tile')), parts along dimension 0
There are 2 independent parts, one for each index of `parts`. A program takes and returns all parts, laid end to end along the dimension named above; each array names one. Nothing has to cross between parts.
Inputs may be any that keep to these rules, and one draw needn't show every extreme that they name: `foot_list`: block b belongs to owner b // 16 of the tile axis. Each tile's list names 32 distinct blocks, exactly 4 from each of 8 owners. `foot_mask`: at least three quarters of each tile's entries are live.
All inputs are finite; a program needn't handle non-finite values.
Results may differ from a plain program's by a relative error of at most 0.0028.
Values may be sent and summed in bfloat16 or wider, within the bound.
No kernel may reach another device: no remote copies, remote signals or barrier semaphores. Data moves between devices by JAX's collectives and lax.ppermute only.
A program may use at most 64 MiB of HBM per device.

v0:
```python
import jax
import jax.numpy as jnp
from jax import lax
from jax.sharding import PartitionSpec as P


def owner_ranks(block_ids, blk_dev):
    owners = block_ids // blk_dev
    positions = jnp.arange(block_ids.shape[-1])
    same_owner = owners[:, None] == owners[None, :]
    before = positions[None, :] < positions[:, None]
    return jnp.sum((same_owner & before).astype(jnp.int32), axis=1)


def on_device(directions, sensitivity, data_weight, foot_list, foot_mask):
    tile_count = lax.axis_size("tile")
    blk_dev, vec_count, block_width = directions.shape
    foot_count = foot_list.shape[1]
    capacity = max(2, foot_count // tile_count)
    all_lists, all_masks = (
        lax.all_gather(foot_list, "tile", axis=0, tiled=True),
        lax.all_gather(foot_mask, "tile", axis=0, tiled=True),
    )
    owner_index = lax.axis_index("tile")
    own_list = foot_list[0]
    own_mask = foot_mask[0]
    own_owner = own_list // blk_dev
    own_rank = owner_ranks(own_list, blk_dev)
    all_rank = jax.vmap(lambda block_ids: owner_ranks(block_ids, blk_dev))(all_lists)
    held_here = all_lists // blk_dev == owner_index
    slot_ids = jnp.arange(capacity)
    slot_match = held_here[:, :, None] & (all_rank[:, :, None] == slot_ids[None, None, :])
    slot_valid = jnp.any(slot_match, axis=1)
    slot_block = jnp.sum(slot_match.astype(jnp.int32) * (all_lists % blk_dev)[:, :, None], axis=1)
    kept_vecs = directions.shape[1]
    outbound = jnp.take(directions, slot_block.reshape(-1), axis=0)
    outbound = outbound * slot_valid.reshape(-1).astype(jnp.bfloat16)[:, None, None]
    outbound = outbound.reshape(tile_count, capacity, kept_vecs, block_width)
    arrived = lax.all_to_all(outbound, "tile", split_axis=0, concat_axis=0, tiled=True)
    block_pool = arrived.reshape(tile_count * capacity, kept_vecs, block_width)
    fetched = jnp.take(block_pool, own_owner * capacity + own_rank, axis=0)
    fetched = fetched * own_mask.astype(jnp.bfloat16)[:, None, None]
    flat_dirs = fetched.transpose(1, 0, 2).reshape(vec_count, foot_count * block_width)
    sens_rows = sensitivity[0]
    predicted = lax.dot_general(
        sens_rows, flat_dirs, (((1,), (1,)), ((), ())), preferred_element_type=jnp.float32
    )
    weights = data_weight[0]
    scaled = ((weights * weights)[:, None] * predicted).astype(jnp.bfloat16)
    summed = lax.psum(
        lax.dot_general(
            scaled, sens_rows, (((0,), (0,)), ((), ())), preferred_element_type=jnp.float32
        ),
        "row",
    )
    foot_grads = summed.reshape(kept_vecs, foot_count, block_width).transpose(1, 0, 2)
    foot_grads = foot_grads * own_mask.astype(jnp.float32)[:, None, None]
    entry_ids = jnp.arange(foot_count)
    back_match = (own_owner[None, None, :] == jnp.arange(tile_count)[:, None, None]) & (
        own_rank[None, None, :] == slot_ids[None, :, None]
    )
    back_valid = jnp.any(back_match, axis=2).reshape(-1)
    back_source = jnp.sum(back_match.astype(jnp.int32) * entry_ids[None, None, :], axis=2).reshape(
        -1
    )
    outgoing = (
        jnp.take(foot_grads, back_source, axis=0) * back_valid.astype(jnp.float32)[:, None, None]
    )
    outgoing = outgoing.reshape(tile_count, capacity, kept_vecs, block_width)
    returned = lax.all_to_all(outgoing, "tile", split_axis=0, concat_axis=0, tiled=True)
    segment_ids = jnp.where(slot_valid, slot_block, blk_dev).reshape(-1)
    local_grad = jax.ops.segment_sum(
        returned.reshape(tile_count * capacity, kept_vecs, block_width),
        segment_ids,
        num_segments=blk_dev + 1,
    )[:blk_dev]
    return local_grad


def solution(mesh):
    in_specs = (
        P(("parts", "tile"), None, None),
        P(("parts", "tile"), "row", None),
        P(("parts", "tile"), "row"),
        P(("parts", "tile"), None),
        P(("parts", "tile"), None),
    )
    out_specs = P(("parts", "tile"), None, None)
    return jax.shard_map(
        on_device, mesh=mesh, in_specs=in_specs, out_specs=out_specs, check_vma=False
    )
```

profile of v0, /device:TPU:0, one launch (start us, length us, event | category | flops | bytes accessed | tf_op | source)
XLA Modules:
  0.0 139.1 jit_solution(12028688723916962680)
XLA Ops:
  6.5 22.4 %all-gather = s32[8,1,32]{2,1,0:T(1,128)S(1)} all-gather(s32[1,1,32]{2,1,0:T(1,128)} %bitcast.77), channel_id=1, replica_groups=mesh['parts'=2,'tile'=8,'row'=2] {'tile'}, dimensions={0}, use_global_device_ids=true | all-gather | bytes 1152 | tf_op jit(solution)/shard_map/all_gather | solution.py:21
  29.0 0.3 convert_reduce_fusion
  29.3 0.2 fusion.15
  29.5 0.1 copy.12
  29.6 0.1 select_reduce_fusion
  29.7 0.1 copy.13
  29.8 0.1 copy.15
  29.9 0.1 reduce_or.21
  30.0 0.1 copy.16
  30.2 0.7 gather_fusion
  31.0 1.1 select_multiply_fusion.1
  32.1 3.5 %all-to-all-start = ((bf16[8,4,32,384]{3,2,1,0:T(8,128)(2,1)}), bf16[8,4,32,384]{3,2,1,0:T(8,128)(2,1)S(1)}, u32[]{:S(2)}, u32[]{:S(2)}) async-start(bf16[8,4,32,384]{3,2,1,0:T(8,128)(2,1)} %select_multiply_fusion.1), calls=%async_computation | async-start | bytes 1572864 | tf_op jit(solution)/shard_map/all_to_all | solution.py:39
  35.7 0.2 convert_reduce_fusion.1
  36.0 0.5 convert_bitcast_fusion
  36.4 15.8 %all-to-all-done = bf16[8,4,32,384]{3,2,1,0:T(8,128)(2,1)S(1)} async-done(((bf16[8,4,32,384]{3,2,1,0:T(8,128)(2,1)}), bf16[8,4,32,384]{3,2,1,0:T(8,128)(2,1)S(1)}, u32[]{:S(2)}, u32[]{:S(2)}) %all-to-all-start) | async-done | bytes 786464 | tf_op jit(solution)/shard_map/all_to_all | solution.py:39
  52.3 0.7 gather_fusion.1
  53.0 0.2 multiply_bitcast_fusion.1
  53.3 9.0 %fusion = f32[32,12288]{1,0:T(8,128)S(1)} fusion(bf16[1,256,12288]{2,1,0:T(8,128)(2,1)} %param.6, bf16[32,12288]{1,0:T(8,128)(2,1)S(1)} %bitcast.73, f32[256]{0:T(256)S(1)} %bitcast.76), kind=kOutput, calls=%fused_computation.4 | convolution fusion | flops 402669568 | bytes 8651776 | tf_op jit(solution)/shard_map/dot_general | solution.py:51
  62.3 1.3 copy.24
  63.7 0.1 fusion.12
  63.8 0.1 copy.19
  63.9 0.1 copy.14
  64.0 0.2 and_reduce_fusion
  64.2 0.1 copy.20
  64.4 18.8 %all-reduce.2.cloned.1.call-done = f32[32,32,384]{2,0,1:T(8,128)} async-done(((f32[32,32,384]{2,0,1:T(8,128)}), f32[32,32,384]{2,0,1:T(8,128)}) %all-reduce.2.cloned.1.call-update) | async-done | bytes 1572880 | tf_op jit(solution)/shard_map/psum | solution.py:50
  83.2 1.6 %multiply_bitcast_fusion = f32[32,32,384]{2,1,0:T(8,128)S(1)} fusion(f32[32,32,384]{2,0,1:T(8,128)} %all-reduce.2.cloned.1.call-done, f32[32]{0:T(128)S(1)} %copy-done.3), kind=kLoop, calls=%fused_computation.10 | loop fusion | flops 393216 | bytes 3145856 | tf_op jit(solution)/shard_map/mul | solution.py:57
  84.7 0.7 gather_fusion.2
  85.4 0.2 select_multiply_fusion
  85.6 43.0 %all_to_all.10 = f32[8,4,32,384]{3,2,1,0:T(8,128)S(1)} all-to-all(f32[8,4,32,384]{3,2,1,0:T(8,128)S(1)} %select_multiply_fusion), channel_id=1, replica_groups=mesh['parts'=2,'tile'=8,'row'=2] {'tile'}, dimensions={0} | all-to-all | bytes 3145728 | tf_op jit(solution)/shard_map/all_to_all | solution.py:70
  128.6 0.1 broadcast_in_dim.32
  128.7 2.6 %scatter_fusion = f32[17,32,384]{2,1,0:T(8,128)S(1)} fusion(f32[17,32,384]{2,1,0:T(8,128)S(1)} %broadcast_in_dim.32, s32[32]{0:T(128)S(1)} %get-tuple-element.10, f32[32,32,384]{2,1,0:T(8,128)S(1)} %bitcast.68), kind=kCustom, calls=%fused_computation.3 | custom fusion | flops 393216 | bytes 4718720 | tf_op jit(solution)/shard_map/scatter-add | solution.py:72
  131.4 0.9 slice.10
  (34 shorter events, 0.5 us)
Async XLA Ops:
  6.5 23.7 %copy-start = (bf16[16,32,384]{2,1,0:T(8,128)(2,1)S(1)}, bf16[16,32,384]{2,1,0:T(8,128)(2,1)}, u32[]{:S(2)}) copy-start(bf16[16,32,384]{2,1,0:T(8,128)(2,1)} %param.5) | copy-start | bytes 1179652
  30.9 4.7 %copy-start.1 = (f32[1,256]{1,0:T(1,128)S(1)}, f32[1,256]{1,0:T(1,128)}, u32[]{:S(2)}) copy-start(f32[1,256]{1,0:T(1,128)} %param.7) | copy-start | bytes 3076
  31.0 4.7 %copy-start.2 = (s32[1,32]{1,0:T(1,128)S(1)}, s32[1,32]{1,0:T(1,128)}, u32[]{:S(2)}) copy-start(s32[1,32]{1,0:T(1,128)} %param.8) | copy-start | bytes 388
  31.0 5.0 %copy-start.4 = (s32[1,32]{1,0:T(1,128)S(1)}, s32[1,32]{1,0:T(1,128)}, u32[]{:S(2)}) copy-start(s32[1,32]{1,0:T(1,128)} %param.9) | copy-start | bytes 388
  32.1 20.2 %all-to-all-start = ((bf16[8,4,32,384]{3,2,1,0:T(8,128)(2,1)}), bf16[8,4,32,384]{3,2,1,0:T(8,128)(2,1)S(1)}, u32[]{:S(2)}, u32[]{:S(2)}) async-start(bf16[8,4,32,384]{3,2,1,0:T(8,128)(2,1)} %select_multiply_fusion.1), calls=%async_computation | async-start | bytes 1572864 | tf_op jit(solution)/shard_map/all_to_all | solution.py:39
  35.6 47.6 %all-reduce.2.cloned.1.call-start = ((), (), s32[]{:S(2)}) async-start(), calls=%async_computation.2 | async-start | bytes 3145728 | tf_op jit(solution)/shard_map/psum | solution.py:50
  63.6 19.5 %copy-start.3 = (f32[32]{0:T(128)S(1)}, f32[32]{0:T(128)}, u32[]{:S(2)}) copy-start(f32[32]{0:T(128)} %get-tuple-element.7) | copy-start | bytes 388
Sparse Core Ops, SparseCore 0:
  63.8 19.3 all-reduce.1
where the time goes:
time: 139 us
  blocking collectives  65.4 us (47%)
  waiting for transfers between devices  34.7 us (25%)
  between operations  13.6 us (10%)
  matrix products  8.98 us (6%)
  other arithmetic  7.43 us (5%)
  local copies, waits for them, and re-layouts  5.44 us (4%)
  starting transfers between devices  3.59 us (3%)
    all_to_all x1, blocking collectives, on_device(): lax.all_to_all(outgoing, 'tile', split_axis=0, concat_axis=0, tiled=True)  43 us
    all_gather x1, blocking collectives, on_device(): lax.all_gather(foot_list, 'tile', axis=0, tiled=True)  22.4 us
    psum x1, waiting for transfers between devices, on_device(): lax.psum(lax.dot_general(scaled, sens_rows, (((0,), (0,)), ((), ())), pre...  18.8 us
    all_to_all x1, waiting for transfers between devices, on_device(): lax.all_to_all(outbound, 'tile', split_axis=0, concat_axis=0, tiled=True)  15.8 us
    dot_general x1, matrix products, on_device(): lax.dot_general(scaled, sens_rows, (((0,), (0,)), ((), ())), preferred_el...  8.98 us
    all_to_all x1, starting transfers between devices, on_device(): lax.all_to_all(outbound, 'tile', split_axis=0, concat_axis=0, tiled=True)  3.55 us
  transfers between devices with their start and end apart: 2, of which 2 were waited for; matrix products, arithmetic and copies ran while one was open for 1% of the time, Pallas kernels for 0%

commit v1 on v0

v1 whole, which is shorter than its diff:
```python
import functools

import jax
import jax.numpy as jnp
from jax import lax
from jax.experimental import pallas as pl
from jax.experimental.pallas import tpu as pltpu
from jax.sharding import PartitionSpec as P

VMEM = pl.BlockSpec(memory_space=pltpu.VMEM)
SMEM = pl.BlockSpec(memory_space=pltpu.SMEM)
ANY = pl.BlockSpec(memory_space=pl.ANY)
PARAMS = pltpu.CompilerParams(vmem_limit_bytes=40 << 20)


def swap_rows(x):
    return lax.ppermute(x, "row", [(0, 1), (1, 0)])


def exchange(x, step):
    tiles = lax.axis_size("tile")
    pairs = [(2 * t + r, 2 * (t ^ (2 * step + r)) + r) for t in range(tiles) for r in range(2)]
    return lax.ppermute(x, ("tile", "row"), pairs)


def select_kernel(steps, capacity, here_ref, *refs):
    lists, dirs_ref = refs[:steps], refs[steps]
    outs, chosen_ref = refs[steps + 1 : 2 * steps + 1], refs[2 * steps + 1]
    slots_ref = refs[2 * steps + 2]
    blocks = dirs_ref.shape[0]
    tile = here_ref[0]
    for p in range(steps):
        count = jnp.int32(0)
        for k in range(lists[p].shape[1]):
            block = lists[p][0, k]
            mine = lax.div(block, blocks) == tile
            slots_ref[jnp.where(mine, count, capacity)] = lax.rem(block, blocks)
            count = count + mine.astype(jnp.int32)
        for c in range(capacity):
            block = slots_ref[c]
            chosen_ref[p * capacity + c] = block
            outs[p][c] = dirs_ref[block]


def find_columns(steps, capacity, blocks, here_ref, list_ref, count_ref, column_ref):
    tile, core = here_ref[0], here_ref[1]
    for p in range(steps):
        count_ref[p] = 0
    for k in range(list_ref.shape[1]):
        apart = lax.div(list_ref[0, k], blocks) ^ tile
        step = lax.div(apart, 2)
        mine = lax.rem(apart, 2) == core
        count = count_ref[step]
        column_ref[jnp.where(mine, step * capacity + count, steps * capacity)] = k
        count_ref[step] = count + mine.astype(jnp.int32)


def column_copies(slots, capacity, width, column_ref, sens_refs, held_ref, sems):
    copies = []
    rows = sens_refs[0].shape[0]
    for place, slot in enumerate(slots):
        start = pl.multiple_of(column_ref[slot] * width, 128)
        for half in range(2):
            copies.append(
                pltpu.make_async_copy(
                    sens_refs[half].at[:, pl.ds(start, width)],
                    held_ref.at[pl.ds(half * rows, rows), pl.ds(place * width, width)],
                    sems.at[2 * place + half],
                )
            )
    return copies


def predict_kernel(
    steps, capacity, blocks, here_ref, list_ref, mask_ref, own_ref, other_ref, *refs
):
    dirs = refs[:steps]
    out_ref, count_ref, column_ref, held_ref, flat_ref, sems = refs[steps:]
    vecs, width = dirs[0].shape[1:]
    rows = own_ref.shape[0]
    find_columns(steps, capacity, blocks, here_ref, list_ref, count_ref, column_ref)
    order = [p * capacity + c for p in range(steps) for c in range(capacity)]
    copies = column_copies(order, capacity, width, column_ref, (own_ref, other_ref), held_ref, sems)
    for copy in copies:
        copy.start()
    for p in range(steps):
        for c in range(capacity):
            slot = p * capacity + c
            live = mask_ref[0, column_ref[slot]].astype(jnp.float32)
            block = dirs[p][c].astype(jnp.float32) * live
            flat_ref[:, slot * width : (slot + 1) * width] = block.astype(jnp.bfloat16)
    total = jnp.zeros((vecs, 2 * rows), jnp.float32)
    for p in range(steps):
        for copy in copies[2 * p * capacity : 2 * (p + 1) * capacity]:
            copy.wait()
        span = slice(p * capacity * width, (p + 1) * capacity * width)
        total += lax.dot_general(
            flat_ref[:, span],
            held_ref[:, span],
            (((1,), (1,)), ((), ())),
            preferred_element_type=jnp.float32,
        )
    out_ref[0] = total[:, :rows]
    out_ref[1] = total[:, rows:]


def back_kernel(
    group, steps, capacity, blocks, here_ref, list_ref, mask_ref, own_ref, other_ref, *refs
):
    mine_ref, theirs_ref, own_weight_ref, other_weight_ref = refs[:4]
    outs = refs[4 : 4 + len(group)]
    count_ref, column_ref, held_ref, sems = refs[4 + len(group) :]
    width = outs[0].shape[2]
    find_columns(steps, capacity, blocks, here_ref, list_ref, count_ref, column_ref)
    order = [p * capacity + c for p in group for c in range(capacity)]
    copies = column_copies(order, capacity, width, column_ref, (own_ref, other_ref), held_ref, sems)
    for copy in copies:
        copy.start()
    own_weight, other_weight = own_weight_ref[...], other_weight_ref[...]
    scaled = jnp.concatenate(
        [
            (own_weight * own_weight) * (mine_ref[0] + theirs_ref[1]),
            (other_weight * other_weight) * (mine_ref[1] + theirs_ref[0]),
        ],
        axis=1,
    ).astype(jnp.bfloat16)
    for place, p in enumerate(group):
        for copy in copies[2 * place * capacity : 2 * (place + 1) * capacity]:
            copy.wait()
        span = slice(place * capacity * width, (place + 1) * capacity * width)
        grads = jnp.dot(scaled, held_ref[:, span], preferred_element_type=jnp.float32)
        for c in range(capacity):
            live = mask_ref[0, column_ref[p * capacity + c]].astype(jnp.float32)
            part = grads[:, c * width : (c + 1) * width] * live
            outs[place][c] = part.astype(jnp.bfloat16)


def sum_kernel(steps, capacity, own_chosen_ref, other_chosen_ref, *refs):
    own, other = refs[:steps], refs[steps : 2 * steps]
    out_ref, held_ref = refs[2 * steps :]
    out_ref[...] = jnp.zeros_like(out_ref)
    held_ref[...] = jnp.zeros_like(held_ref)
    for chosen_ref, chunks, total_ref in (
        (own_chosen_ref, own, out_ref),
        (other_chosen_ref, other, held_ref),
    ):
        for p in range(steps):
            for c in range(capacity):
                total_ref[chosen_ref[p * capacity + c]] += chunks[p][c].astype(jnp.float32)
    out_ref[...] += held_ref[...]


def on_device(directions, sensitivity, data_weight, foot_list, foot_mask):
    tiles = lax.axis_size("tile")
    blocks, vecs, width = directions.shape
    rows = sensitivity.shape[1]
    foot = foot_list.shape[1]
    steps, capacity = tiles // 2, foot // tiles
    here = jnp.stack([lax.axis_index("tile"), lax.axis_index("row")]).astype(jnp.int32)
    far_first = list(reversed(range(steps)))

    own_sens = sensitivity[0]
    other_sens = swap_rows(own_sens)
    other_weight = swap_rows(data_weight)
    lists = {p: exchange(foot_list, p) for p in far_first}

    chunk = jax.ShapeDtypeStruct((capacity, vecs, width), jnp.bfloat16)
    *chunks, chosen = pl.pallas_call(
        functools.partial(select_kernel, steps, capacity),
        out_shape=[chunk] * steps + [jax.ShapeDtypeStruct((steps * capacity,), jnp.int32)],
        in_specs=[SMEM] * (steps + 1) + [VMEM],
        out_specs=[VMEM] * steps + [SMEM],
        scratch_shapes=[pltpu.SMEM((capacity + 1,), jnp.int32)],
        compiler_params=PARAMS,
        name="select_blocks",
    )(here, *[lists[p] for p in range(steps)], directions)
    fetched = {p: exchange(chunks[p], p) for p in far_first}
    other_chosen = swap_rows(chosen)

    span = steps * capacity * width
    partial = pl.pallas_call(
        functools.partial(predict_kernel, steps, capacity, blocks),
        out_shape=jax.ShapeDtypeStruct((2, vecs, rows), jnp.float32),
        in_specs=[SMEM] * 3 + [ANY] * 2 + [VMEM] * steps,
        out_specs=VMEM,
        scratch_shapes=[
            pltpu.SMEM((steps,), jnp.int32),
            pltpu.SMEM((steps * capacity + 1,), jnp.int32),
            pltpu.VMEM((2 * rows, span), jnp.bfloat16),
            pltpu.VMEM((vecs, span), jnp.bfloat16),
            pltpu.SemaphoreType.DMA((2 * steps * capacity,)),
        ],
        compiler_params=PARAMS,
        name="predict",
    )(here, foot_list, foot_mask, own_sens, other_sens, *[fetched[p] for p in range(steps)])
    other_partial = swap_rows(partial)

    half = (steps + 1) // 2
    returned = {}
    for group in (far_first[:half], far_first[half:]):
        grads = pl.pallas_call(
            functools.partial(back_kernel, group, steps, capacity, blocks),
            out_shape=[chunk] * len(group),
            in_specs=[SMEM] * 3 + [ANY] * 2 + [VMEM] * 4,
            out_specs=[VMEM] * len(group),
            scratch_shapes=[
                pltpu.SMEM((steps,), jnp.int32),
                pltpu.SMEM((steps * capacity + 1,), jnp.int32),
                pltpu.VMEM((2 * rows, len(group) * capacity * width), jnp.bfloat16),
                pltpu.SemaphoreType.DMA((2 * len(group) * capacity,)),
            ],
            compiler_params=PARAMS,
            name="back_project",
        )(
            here, foot_list, foot_mask, own_sens, other_sens,
            partial, other_partial, data_weight, other_weight,
        )
        for place, p in enumerate(group):
            returned[p] = exchange(grads[place], p)
    other_returned = {p: swap_rows(returned[p]) for p in far_first}

    return pl.pallas_call(
        functools.partial(sum_kernel, steps, capacity),
        out_shape=jax.ShapeDtypeStruct((blocks, vecs, width), jnp.float32),
        in_specs=[SMEM] * 2 + [VMEM] * (2 * steps),
        out_specs=VMEM,
        scratch_shapes=[pltpu.VMEM((blocks, vecs, width), jnp.float32)],
        compiler_params=PARAMS,
        name="sum_blocks",
    )(
        chosen, other_chosen,
        *[returned[p] for p in range(steps)], *[other_returned[p] for p in range(steps)],
    )


def solution(mesh):
    in_specs = (
        P(("parts", "tile"), None, None),
        P(("parts", "tile"), "row", None),
        P(("parts", "tile"), "row"),
        P(("parts", "tile"), None),
        P(("parts", "tile"), None),
    )
    out_specs = P(("parts", "tile"), None, None)
    return jax.shard_map(
        on_device, mesh=mesh, in_specs=in_specs, out_specs=out_specs, check_vma=False
    )
```

time: 139 us -> 62 us (0.45)
  blocking collectives: 65.4 us -> 0 us
  starting transfers between devices: 3.59 us -> 25.6 us
  waiting for transfers between devices: 34.7 us -> 16.6 us
  Pallas kernels: 0 us -> 14.2 us
  between operations: 13.6 us -> 0.09 us
  matrix products: 8.98 us -> 0 us
  other arithmetic: 7.43 us -> 0.07 us
    all_to_all x1 -> x0, blocking collectives: 43 us -> none  [on_device(): lax.all_to_all(outgoing, 'tile', split_axis=0, concat_axis=0, tiled=True)]
    ppermute x0 -> x20, starting transfers between devices: none -> 25.6 us  [the longest x12 16.8 us: exchange(): return lax.ppermute(x, ('tile', 'row'), pairs)]
    all_gather x1 -> x0, blocking collectives: 22.4 us -> none  [on_device(): lax.all_gather(foot_list, 'tile', axis=0, tiled=True)]
    psum x1 -> x0, waiting for transfers between devices: 18.8 us -> none  [on_device(): lax.psum(lax.dot_general(scaled, sens_rows, (((0,), (0,)), ((), ())), pre...]
    ppermute x0 -> x20, waiting for transfers between devices: none -> 16.6 us  [the longest x12 14.7 us: exchange(): return lax.ppermute(x, ('tile', 'row'), pairs)]
    all_to_all x1 -> x0, waiting for transfers between devices: 15.8 us -> none  [on_device(): lax.all_to_all(outbound, 'tile', split_axis=0, concat_axis=0, tiled=True)]
    pallas_call x0 -> x5, Pallas kernels: none -> 14.2 us  [the longest x2 6.04 us: on_device(): pl.pallas_call(functools.partial(back_kernel, group, steps, capacity, blo...]
    dot_general x1 -> x0, matrix products: 8.98 us -> none  [on_device(): lax.dot_general(scaled, sens_rows, (((0,), (0,)), ((), ())), preferred_el...]
  transfers between devices with their start and end apart: 2 -> 20, of which waited for: 2 -> 8; matrix products, arithmetic and copies ran while one was open for 1% -> 0% of each run, Pallas kernels for 0% -> 8%
where the time goes in v1:
time: 62 us; the launch traced here: 61.6 us
  starting transfers between devices  25.6 us (41%)
  waiting for transfers between devices  16.6 us (27%)
  Pallas kernels  14.2 us (23%)
  local copies, waits for them, and re-layouts  5.09 us (8%)
    ppermute x12, starting transfers between devices, exchange(): return lax.ppermute(x, ('tile', 'row'), pairs)  16.8 us
    ppermute x12, waiting for transfers between devices, exchange(): return lax.ppermute(x, ('tile', 'row'), pairs)  14.7 us
    ppermute x8, starting transfers between devices, swap_rows(): return lax.ppermute(x, 'row', [(0, 1), (1, 0)])  8.84 us
    pallas_call x2, Pallas kernels, on_device(): pl.pallas_call(functools.partial(back_kernel, group, steps, capacity, blo...  6.04 us
    unnamed x10, local copies, waits for them, and re-layouts  5.09 us
    pallas_call x1, Pallas kernels, on_device(): pl.pallas_call(functools.partial(predict_kernel, steps, capacity, blocks)...  4.64 us
    ppermute x8, waiting for transfers between devices, swap_rows(): return lax.ppermute(x, 'row', [(0, 1), (1, 0)])  1.89 us
    pallas_call x1, Pallas kernels, on_device(): pl.pallas_call(functools.partial(select_kernel, steps, capacity), out_sha...  1.8 us
  transfers between devices with their start and end apart: 20, of which 8 were waited for; matrix products, arithmetic and copies ran while one was open for 0% of the time, Pallas kernels for 8%

profile of v1, /device:TPU:0, one launch (start us, length us, event | category | flops | bytes accessed | tf_op | source)
XLA Modules:
  0.0 61.6 jit_solution(8273696606396531109)
XLA Ops:
  0.0 0.5 collective-permute-start.5
  0.5 1.3 %collective-permute-start = (s32[1,32]{1,0:T(1,128)}, s32[1,32]{1,0:T(1,128)S(1)}, u32[]{:S(2)}, u32[]{:S(2)}) collective-permute-start(s32[1,32]{1,0:T(1,128)} %list_ref.5), channel_id=1, source_target_pairs={{0,0},{1,3},{2,2},{3,1},{4,4},{5,7},{6,6},{7,5},{8,8},{9,11},{10,1... | collective-permute-start | bytes 392 | tf_op jit(solution)/shard_map/ppermute | solution.py:23
  1.8 2.6 %collective-permute-start.1 = (s32[1,32]{1,0:T(1,128)}, s32[1,32]{1,0:T(1,128)S(1)}, u32[]{:S(2)}, u32[]{:S(2)}) collective-permute-start(s32[1,32]{1,0:T(1,128)} %list_ref.5), channel_id=1, source_target_pairs={{0,4},{1,7},{2,6},{3,5},{4,0},{5,3},{6,2},{7,1},{8,12},{9,15},{10,... | collective-permute-start | bytes 392 | tf_op jit(solution)/shard_map/ppermute | solution.py:23
  4.3 2.6 %collective-permute-start.2 = (s32[1,32]{1,0:T(1,128)}, s32[1,32]{1,0:T(1,128)S(1)}, u32[]{:S(2)}, u32[]{:S(2)}) collective-permute-start(s32[1,32]{1,0:T(1,128)} %list_ref.5), channel_id=1, source_target_pairs={{0,8},{1,11},{2,10},{3,9},{4,12},{5,15},{6,14},{7,13},{8,0},{9,3},... | collective-permute-start | bytes 392 | tf_op jit(solution)/shard_map/ppermute | solution.py:23
  7.0 1.9 %collective-permute-done.2.refs_2_ = s32[1,32]{1,0:T(1,128)S(1)} collective-permute-done((s32[1,32]{1,0:T(1,128)}, s32[1,32]{1,0:T(1,128)S(1)}, u32[]{:S(2)}, u32[]{:S(2)}) %collective-permute-start.2) | collective-permute-done | bytes 160 | tf_op jit(solution)/shard_map/ppermute | solution.py:23
  8.9 3.5 %collective-permute-done.3.refs_3_ = s32[1,32]{1,0:T(1,128)S(1)} collective-permute-done((s32[1,32]{1,0:T(1,128)}, s32[1,32]{1,0:T(1,128)S(1)}, u32[]{:S(2)}, u32[]{:S(2)}) %collective-permute-start.3) | collective-permute-done | bytes 160 | tf_op jit(solution)/shard_map/ppermute | solution.py:23
  12.4 1.0 %copy-done.1 = bf16[16,32,384]{2,1,0:T(8,128)(2,1)S(1)} copy-done((bf16[16,32,384]{2,1,0:T(8,128)(2,1)S(1)}, bf16[16,32,384]{2,1,0:T(8,128)(2,1)}, u32[]{:S(2)}) %copy-start.1) | copy-done | bytes 393240
  13.4 1.8 %select_blocks.1 = (bf16[4,32,384]{2,1,0:T(8,128)(2,1)S(1)}, bf16[4,32,384]{2,1,0:T(8,128)(2,1)S(1)}, bf16[4,32,384]{2,1,0:T(8,128)(2,1)S(1)}, bf16[4,32,384]{2,1,0:T(8,128)(2,1)S(1)}, s32[16]{0:T(128)S(1)}) custom-call(s32[2]{0:T(128)S(1)} %pad_add_fusion.here_ref, s32[1,32]{1,0:T(1,128)S(1)} %collective-permute-done.refs_0_, ...), custom_call_target="tpu_custom_call" | custom-call | tf_op jit(solution)/shard_map/select_blocks/pallas_call | solution.py:168
  15.2 0.7 %collective-permute-start.6 = (bf16[4,32,384]{2,1,0:T(8,128)(2,1)S(1)}, bf16[4,32,384]{2,1,0:T(8,128)(2,1)S(1)}, u32[]{:S(2)}, u32[]{:S(2)}) collective-permute-start(bf16[4,32,384]{2,1,0:T(8,128)(2,1)S(1)} %get-tuple-element.15), channel_id=1, source_target_pairs={{0,0},{1,3},{2,2},{3,1},{4,4},{5,7},{6,6},{7,5},{8,8},{9,11},{10,1... | collective-permute-start | bytes 294920 | tf_op jit(solution)/shard_map/ppermute | solution.py:23
  16.0 0.6 collective-permute-start.8
  16.5 3.8 %collective-permute-start.9 = (bf16[4,32,384]{2,1,0:T(8,128)(2,1)S(1)}, bf16[4,32,384]{2,1,0:T(8,128)(2,1)S(1)}, u32[]{:S(2)}, u32[]{:S(2)}) collective-permute-start(bf16[4,32,384]{2,1,0:T(8,128)(2,1)S(1)} %get-tuple-element.18), channel_id=1, source_target_pairs={{0,12},{1,15},{2,14},{3,13},{4,8},{5,11},{6,10},{7,9},{8,4},{9,7},... | collective-permute-start | bytes 294920 | tf_op jit(solution)/shard_map/ppermute | solution.py:23
  20.3 0.2 collective-permute-done.7.refs_1_
  20.6 1.0 %collective-permute-done.8.refs_2_ = bf16[4,32,384]{2,1,0:T(8,128)(2,1)S(1)} collective-permute-done((bf16[4,32,384]{2,1,0:T(8,128)(2,1)S(1)}, bf16[4,32,384]{2,1,0:T(8,128)(2,1)S(1)}, u32[]{:S(2)}, u32[]{:S(2)}) %collective-permute-start.8) | collective-permute-done | bytes 98336 | tf_op jit(solution)/shard_map/ppermute | solution.py:23
  21.6 3.1 %collective-permute-done.9.refs_3_ = bf16[4,32,384]{2,1,0:T(8,128)(2,1)S(1)} collective-permute-done((bf16[4,32,384]{2,1,0:T(8,128)(2,1)S(1)}, bf16[4,32,384]{2,1,0:T(8,128)(2,1)S(1)}, u32[]{:S(2)}, u32[]{:S(2)}) %collective-permute-start.9) | collective-permute-done | bytes 98336 | tf_op jit(solution)/shard_map/ppermute | solution.py:23
  24.7 2.8 %copy-done = bf16[1,256,12288]{2,1,0:T(8,128)(2,1)S(1)} copy-done((bf16[1,256,12288]{2,1,0:T(8,128)(2,1)S(1)}, bf16[1,256,12288]{2,1,0:T(8,128)(2,1)}, u32[]{:S(2)}) %copy-start) | copy-done | bytes 6291480
  27.5 0.7 %copy-done.2 = s32[1,32]{1,0:T(1,128)S(1)} copy-done((s32[1,32]{1,0:T(1,128)S(1)}, s32[1,32]{1,0:T(1,128)}, u32[]{:S(2)}) %copy-start.2) | copy-done | bytes 152
  28.2 0.7 %copy-done.3 = s32[1,32]{1,0:T(1,128)S(1)} copy-done((s32[1,32]{1,0:T(1,128)S(1)}, s32[1,32]{1,0:T(1,128)}, u32[]{:S(2)}) %copy-start.3) | copy-done | bytes 152
  28.8 4.6 %predict.1.refs_0_ = f32[2,32,256]{2,1,0:T(8,128)S(1)} custom-call(s32[2]{0:T(128)S(1)} %pad_add_fusion.here_ref, s32[1,32]{1,0:T(1,128)S(1)} %copy-done.2, s32[1,32]{1,0:T(1,128)S(1)} %copy-done.3, bf16[256,12288]{1,0:T(8,128)(2,1)S(1)} %bitcast.4, bf16[256,12288]{1,0:T(8,128)(2,1)} %collective-permute-done.5.other_ref, ...), custom_call_target="tpu_custom_call" | custom-call | tf_op jit(solution)/shard_map/predict/pallas_call | solution.py:181
  33.5 4.0 %collective-permute-start.10 = (f32[2,32,256]{2,1,0:T(8,128)S(1)}, f32[2,32,256]{2,1,0:T(8,128)S(1)}, u32[]{:S(2)}, u32[]{:S(2)}) collective-permute-start(f32[2,32,256]{2,1,0:T(8,128)S(1)} %predict.1.refs_0_), channel_id=1, source_target_pairs={{0,1},{1,0},{2,3},{3,2},{4,5},{5,4},{6,7},{7,6},{8,9},{9,8},{10,11... | collective-permute-start | bytes 196616 | tf_op jit(solution)/shard_map/ppermute | solution.py:17
  37.6 1.1 %collective-permute-done.11.refs_3_ = f32[1,256]{1,0:T(1,128)S(1)} collective-permute-done((f32[1,256]{1,0:T(1,128)S(1)}, f32[1,256]{1,0:T(1,128)S(1)}, u32[]{:S(2)}, u32[]{:S(2)}) %collective-permute-start.11) | collective-permute-done | bytes 1056 | tf_op jit(solution)/shard_map/ppermute | solution.py:17
  38.6 3.0 %back_project.2 = (bf16[4,32,384]{2,1,0:T(8,128)(2,1)S(1)}, bf16[4,32,384]{2,1,0:T(8,128)(2,1)S(1)}) custom-call(s32[2]{0:T(128)S(1)} %pad_add_fusion.here_ref, s32[1,32]{1,0:T(1,128)S(1)} %copy-done.2, s32[1,32]{1,0:T(1,128)S(1)} %copy-done.3, bf16[256,12288]{1,0:T(8,128)(2,1)S(1)} %bitcast.5, bf16[256,12288]{1,0:T(8,128)(2,1)} %collective-permute-done.5.other_ref, ...), custom_call_target="tpu_custom_call" | custom-call | tf_op jit(solution)/shard_map/back_project/pallas_call | solution.py:201
  41.7 0.7 %collective-permute-start.12 = (bf16[4,32,384]{2,1,0:T(8,128)(2,1)S(1)}, bf16[4,32,384]{2,1,0:T(8,128)(2,1)S(1)}, u32[]{:S(2)}, u32[]{:S(2)}) collective-permute-start(bf16[4,32,384]{2,1,0:T(8,128)(2,1)S(1)} %get-tuple-element.19), channel_id=1, source_target_pairs={{0,0},{1,3},{2,2},{3,1},{4,4},{5,7},{6,6},{7,5},{8,8},{9,11},{10,1... | collective-permute-start | bytes 294920 | tf_op jit(solution)/shard_map/ppermute | solution.py:23
  42.3 1.7 %collective-permute-start.13 = (bf16[4,32,384]{2,1,0:T(8,128)(2,1)S(1)}, bf16[4,32,384]{2,1,0:T(8,128)(2,1)S(1)}, u32[]{:S(2)}, u32[]{:S(2)}) collective-permute-start(bf16[4,32,384]{2,1,0:T(8,128)(2,1)S(1)} %get-tuple-element.20), channel_id=1, source_target_pairs={{0,4},{1,7},{2,6},{3,5},{4,0},{5,3},{6,2},{7,1},{8,12},{9,15},{10,... | collective-permute-start | bytes 294920 | tf_op jit(solution)/shard_map/ppermute | solution.py:23
  44.0 3.0 %back_project.3 = (bf16[4,32,384]{2,1,0:T(8,128)(2,1)S(1)}, bf16[4,32,384]{2,1,0:T(8,128)(2,1)S(1)}) custom-call(s32[2]{0:T(128)S(1)} %pad_add_fusion.here_ref, s32[1,32]{1,0:T(1,128)S(1)} %copy-done.2, s32[1,32]{1,0:T(1,128)S(1)} %copy-done.3, bf16[256,12288]{1,0:T(8,128)(2,1)S(1)} %bitcast.6, bf16[256,12288]{1,0:T(8,128)(2,1)} %collective-permute-done.5.other_ref, ...), custom_call_target="tpu_custom_call" | custom-call | tf_op jit(solution)/shard_map/back_project/pallas_call | solution.py:201
  47.0 1.3 %collective-permute-start.14 = (bf16[4,32,384]{2,1,0:T(8,128)(2,1)S(1)}, bf16[4,32,384]{2,1,0:T(8,128)(2,1)S(1)}, u32[]{:S(2)}, u32[]{:S(2)}) collective-permute-start(bf16[4,32,384]{2,1,0:T(8,128)(2,1)S(1)} %get-tuple-element.21), channel_id=1, source_target_pairs={{0,8},{1,11},{2,10},{3,9},{4,12},{5,15},{6,14},{7,13},{8,0},{9,3},... | collective-permute-start | bytes 294920 | tf_op jit(solution)/shard_map/ppermute | solution.py:23
  48.3 1.6 %collective-permute-start.15 = (bf16[4,32,384]{2,1,0:T(8,128)(2,1)S(1)}, bf16[4,32,384]{2,1,0:T(8,128)(2,1)S(1)}, u32[]{:S(2)}, u32[]{:S(2)}) collective-permute-start(bf16[4,32,384]{2,1,0:T(8,128)(2,1)S(1)} %get-tuple-element.22), channel_id=1, source_target_pairs={{0,12},{1,15},{2,14},{3,13},{4,8},{5,11},{6,10},{7,9},{8,4},{9,7},... | collective-permute-start | bytes 294920 | tf_op jit(solution)/shard_map/ppermute | solution.py:23
  49.9 2.7 %collective-permute-start.16 = (bf16[4,32,384]{2,1,0:T(8,128)(2,1)S(1)}, bf16[4,32,384]{2,1,0:T(8,128)(2,1)S(1)}, u32[]{:S(2)}, u32[]{:S(2)}) collective-permute-start(bf16[4,32,384]{2,1,0:T(8,128)(2,1)S(1)} %collective-permute-done.12.refs_0_), channel_id=1, source_target_pairs={{0,1},{1,0},{2,3},{3,2},{4,5},{5,4},{6,7},{7,6},{8,9},{9,8},{10,11... | collective-permute-start | bytes 294920 | tf_op jit(solution)/shard_map/ppermute | solution.py:17
  52.6 4.9 %collective-permute-done.14.refs_2_ = bf16[4,32,384]{2,1,0:T(8,128)(2,1)S(1)} collective-permute-done((bf16[4,32,384]{2,1,0:T(8,128)(2,1)S(1)}, bf16[4,32,384]{2,1,0:T(8,128)(2,1)S(1)}, u32[]{:S(2)}, u32[]{:S(2)}) %collective-permute-start.14) | collective-permute-done | bytes 98336 | tf_op jit(solution)/shard_map/ppermute | solution.py:23
  57.5 1.1 %collective-permute-start.18 = (bf16[4,32,384]{2,1,0:T(8,128)(2,1)S(1)}, bf16[4,32,384]{2,1,0:T(8,128)(2,1)S(1)}, u32[]{:S(2)}, u32[]{:S(2)}) collective-permute-start(bf16[4,32,384]{2,1,0:T(8,128)(2,1)S(1)} %collective-permute-done.14.refs_2_), channel_id=1, source_target_pairs={{0,1},{1,0},{2,3},{3,2},{4,5},{5,4},{6,7},{7,6},{8,9},{9,8},{10,11... | collective-permute-start | bytes 294920 | tf_op jit(solution)/shard_map/ppermute | solution.py:17
  58.5 0.5 collective-permute-start.4
  59.0 0.8 %collective-permute-done.4.other_chosen_ref = s32[16]{0:T(128)S(1)} collective-permute-done((s32[16]{0:T(128)S(1)}, s32[16]{0:T(128)S(1)}, u32[]{:S(2)}, u32[]{:S(2)}) %collective-permute-start.4) | collective-permute-done | bytes 96 | tf_op jit(solution)/shard_map/ppermute | solution.py:17
  59.9 1.7 %sum_blocks.1 = f32[16,32,384]{2,1,0:T(8,128)} custom-call(s32[16]{0:T(128)S(1)} %get-tuple-element.14.own_chosen_ref, s32[16]{0:T(128)S(1)} %collective-permute-done.4.other_chosen_ref, bf16[4,32,384]{2,1,0:T(8,128)(2,1)S(1)} %collective-permute-done.12.refs_0_, bf16[4,32,384]{2,1,0:T(8,128)(2,1)S(1)} %collective-permute-done.13.refs_1_, ...), custom_call_target="tpu_custom_call" | custom-call | tf_op jit(solution)/shard_map/sum_blocks/pallas_call | solution.py:222
  (24 shorter events, 0.3 us)
Async XLA Ops:
  0.0 24.7 %collective-permute-start.5 = (bf16[256,12288]{1,0:T(8,128)(2,1)}, bf16[256,12288]{1,0:T(8,128)(2,1)}, u32[]{:S(2)}, u32[]{:S(2)}) collective-permute-start(bf16[256,12288]{1,0:T(8,128)(2,1)} %bitcast.3), channel_id=1, source_target_pairs={{0,1},{1,0},{2,3},{3,2},{4,5},{5,4},{6,7},{7,6},{8,9},{9,8},{10,11... | collective-permute-start | bytes 18874376 | tf_op jit(solution)/shard_map/ppermute | solution.py:17
  0.5 6.5 %collective-permute-start = (s32[1,32]{1,0:T(1,128)}, s32[1,32]{1,0:T(1,128)S(1)}, u32[]{:S(2)}, u32[]{:S(2)}) collective-permute-start(s32[1,32]{1,0:T(1,128)} %list_ref.5), channel_id=1, source_target_pairs={{0,0},{1,3},{2,2},{3,1},{4,4},{5,7},{6,6},{7,5},{8,8},{9,11},{10,1... | collective-permute-start | bytes 392 | tf_op jit(solution)/shard_map/ppermute | solution.py:23
  1.8 5.2 %collective-permute-start.1 = (s32[1,32]{1,0:T(1,128)}, s32[1,32]{1,0:T(1,128)S(1)}, u32[]{:S(2)}, u32[]{:S(2)}) collective-permute-start(s32[1,32]{1,0:T(1,128)} %list_ref.5), channel_id=1, source_target_pairs={{0,4},{1,7},{2,6},{3,5},{4,0},{5,3},{6,2},{7,1},{8,12},{9,15},{10,... | collective-permute-start | bytes 392 | tf_op jit(solution)/shard_map/ppermute | solution.py:23
  4.3 4.6 %collective-permute-start.2 = (s32[1,32]{1,0:T(1,128)}, s32[1,32]{1,0:T(1,128)S(1)}, u32[]{:S(2)}, u32[]{:S(2)}) collective-permute-start(s32[1,32]{1,0:T(1,128)} %list_ref.5), channel_id=1, source_target_pairs={{0,8},{1,11},{2,10},{3,9},{4,12},{5,15},{6,14},{7,13},{8,0},{9,3},... | collective-permute-start | bytes 392 | tf_op jit(solution)/shard_map/ppermute | solution.py:23
  6.9 5.5 %collective-permute-start.3 = (s32[1,32]{1,0:T(1,128)}, s32[1,32]{1,0:T(1,128)S(1)}, u32[]{:S(2)}, u32[]{:S(2)}) collective-permute-start(s32[1,32]{1,0:T(1,128)} %list_ref.5), channel_id=1, source_target_pairs={{0,12},{1,15},{2,14},{3,13},{4,8},{5,11},{6,10},{7,9},{8,4},{9,7},... | collective-permute-start | bytes 392 | tf_op jit(solution)/shard_map/ppermute | solution.py:23
  12.4 1.0 %copy-start.1 = (bf16[16,32,384]{2,1,0:T(8,128)(2,1)S(1)}, bf16[16,32,384]{2,1,0:T(8,128)(2,1)}, u32[]{:S(2)}) copy-start(bf16[16,32,384]{2,1,0:T(8,128)(2,1)} %refs_4_.1) | copy-start | bytes 1179652
  15.2 5.1 %collective-permute-start.6 = (bf16[4,32,384]{2,1,0:T(8,128)(2,1)S(1)}, bf16[4,32,384]{2,1,0:T(8,128)(2,1)S(1)}, u32[]{:S(2)}, u32[]{:S(2)}) collective-permute-start(bf16[4,32,384]{2,1,0:T(8,128)(2,1)S(1)} %get-tuple-element.15), channel_id=1, source_target_pairs={{0,0},{1,3},{2,2},{3,1},{4,4},{5,7},{6,6},{7,5},{8,8},{9,11},{10,1... | collective-permute-start | bytes 294920 | tf_op jit(solution)/shard_map/ppermute | solution.py:23
  15.9 4.7 %collective-permute-start.7 = (bf16[4,32,384]{2,1,0:T(8,128)(2,1)S(1)}, bf16[4,32,384]{2,1,0:T(8,128)(2,1)S(1)}, u32[]{:S(2)}, u32[]{:S(2)}) collective-permute-start(bf16[4,32,384]{2,1,0:T(8,128)(2,1)S(1)} %get-tuple-element.16), channel_id=1, source_target_pairs={{0,4},{1,7},{2,6},{3,5},{4,0},{5,3},{6,2},{7,1},{8,12},{9,15},{10,... | collective-permute-start | bytes 294920 | tf_op jit(solution)/shard_map/ppermute | solution.py:23
  16.0 5.7 %collective-permute-start.8 = (bf16[4,32,384]{2,1,0:T(8,128)(2,1)S(1)}, bf16[4,32,384]{2,1,0:T(8,128)(2,1)S(1)}, u32[]{:S(2)}, u32[]{:S(2)}) collective-permute-start(bf16[4,32,384]{2,1,0:T(8,128)(2,1)S(1)} %get-tuple-element.17), channel_id=1, source_target_pairs={{0,8},{1,11},{2,10},{3,9},{4,12},{5,15},{6,14},{7,13},{8,0},{9,3},... | collective-permute-start | bytes 294920 | tf_op jit(solution)/shard_map/ppermute | solution.py:23
  16.5 20.9 %copy-start.4 = (f32[1,256]{1,0:T(1,128)S(1)}, f32[1,256]{1,0:T(1,128)}, u32[]{:S(2)}) copy-start(f32[1,256]{1,0:T(1,128)} %refs_2_.3) | copy-start | bytes 3076
  16.5 8.2 %collective-permute-start.9 = (bf16[4,32,384]{2,1,0:T(8,128)(2,1)S(1)}, bf16[4,32,384]{2,1,0:T(8,128)(2,1)S(1)}, u32[]{:S(2)}, u32[]{:S(2)}) collective-permute-start(bf16[4,32,384]{2,1,0:T(8,128)(2,1)S(1)} %get-tuple-element.18), channel_id=1, source_target_pairs={{0,12},{1,15},{2,14},{3,13},{4,8},{5,11},{6,10},{7,9},{8,4},{9,7},... | collective-permute-start | bytes 294920 | tf_op jit(solution)/shard_map/ppermute | solution.py:23
  24.7 2.8 %copy-start = (bf16[1,256,12288]{2,1,0:T(8,128)(2,1)S(1)}, bf16[1,256,12288]{2,1,0:T(8,128)(2,1)}, u32[]{:S(2)}) copy-start(bf16[1,256,12288]{2,1,0:T(8,128)(2,1)} %param.6) | copy-start | bytes 18874372
  27.5 0.7 %copy-start.2 = (s32[1,32]{1,0:T(1,128)S(1)}, s32[1,32]{1,0:T(1,128)}, u32[]{:S(2)}) copy-start(s32[1,32]{1,0:T(1,128)} %list_ref.5) | copy-start | bytes 388
  28.2 0.7 %copy-start.3 = (s32[1,32]{1,0:T(1,128)S(1)}, s32[1,32]{1,0:T(1,128)}, u32[]{:S(2)}) copy-start(s32[1,32]{1,0:T(1,128)} %mask_ref.5) | copy-start | bytes 388
  33.5 5.1 %collective-permute-start.10 = (f32[2,32,256]{2,1,0:T(8,128)S(1)}, f32[2,32,256]{2,1,0:T(8,128)S(1)}, u32[]{:S(2)}, u32[]{:S(2)}) collective-permute-start(f32[2,32,256]{2,1,0:T(8,128)S(1)} %predict.1.refs_0_), channel_id=1, source_target_pairs={{0,1},{1,0},{2,3},{3,2},{4,5},{5,4},{6,7},{7,6},{8,9},{9,8},{10,11... | collective-permute-start | bytes 196616 | tf_op jit(solution)/shard_map/ppermute | solution.py:17
  37.5 1.1 %collective-permute-start.11 = (f32[1,256]{1,0:T(1,128)S(1)}, f32[1,256]{1,0:T(1,128)S(1)}, u32[]{:S(2)}, u32[]{:S(2)}) collective-permute-start(f32[1,256]{1,0:T(1,128)S(1)} %copy-done.4), channel_id=1, source_target_pairs={{0,1},{1,0},{2,3},{3,2},{4,5},{5,4},{6,7},{7,6},{8,9},{9,8},{10,11... | collective-permute-start | bytes 3080 | tf_op jit(solution)/shard_map/ppermute | solution.py:17
  41.7 8.2 %collective-permute-start.12 = (bf16[4,32,384]{2,1,0:T(8,128)(2,1)S(1)}, bf16[4,32,384]{2,1,0:T(8,128)(2,1)S(1)}, u32[]{:S(2)}, u32[]{:S(2)}) collective-permute-start(bf16[4,32,384]{2,1,0:T(8,128)(2,1)S(1)} %get-tuple-element.19), channel_id=1, source_target_pairs={{0,0},{1,3},{2,2},{3,1},{4,4},{5,7},{6,6},{7,5},{8,8},{9,11},{10,1... | collective-permute-start | bytes 294920 | tf_op jit(solution)/shard_map/ppermute | solution.py:23
  42.3 10.2 %collective-permute-start.13 = (bf16[4,32,384]{2,1,0:T(8,128)(2,1)S(1)}, bf16[4,32,384]{2,1,0:T(8,128)(2,1)S(1)}, u32[]{:S(2)}, u32[]{:S(2)}) collective-permute-start(bf16[4,32,384]{2,1,0:T(8,128)(2,1)S(1)} %get-tuple-element.20), channel_id=1, source_target_pairs={{0,4},{1,7},{2,6},{3,5},{4,0},{5,3},{6,2},{7,1},{8,12},{9,15},{10,... | collective-permute-start | bytes 294920 | tf_op jit(solution)/shard_map/ppermute | solution.py:23
  47.0 10.5 %collective-permute-start.14 = (bf16[4,32,384]{2,1,0:T(8,128)(2,1)S(1)}, bf16[4,32,384]{2,1,0:T(8,128)(2,1)S(1)}, u32[]{:S(2)}, u32[]{:S(2)}) collective-permute-start(bf16[4,32,384]{2,1,0:T(8,128)(2,1)S(1)} %get-tuple-element.21), channel_id=1, source_target_pairs={{0,8},{1,11},{2,10},{3,9},{4,12},{5,15},{6,14},{7,13},{8,0},{9,3},... | collective-permute-start | bytes 294920 | tf_op jit(solution)/shard_map/ppermute | solution.py:23
  48.3 10.2 %collective-permute-start.15 = (bf16[4,32,384]{2,1,0:T(8,128)(2,1)S(1)}, bf16[4,32,384]{2,1,0:T(8,128)(2,1)S(1)}, u32[]{:S(2)}, u32[]{:S(2)}) collective-permute-start(bf16[4,32,384]{2,1,0:T(8,128)(2,1)S(1)} %get-tuple-element.22), channel_id=1, source_target_pairs={{0,12},{1,15},{2,14},{3,13},{4,8},{5,11},{6,10},{7,9},{8,4},{9,7},... | collective-permute-start | bytes 294920 | tf_op jit(solution)/shard_map/ppermute | solution.py:23
  49.9 10.0 %collective-permute-start.16 = (bf16[4,32,384]{2,1,0:T(8,128)(2,1)S(1)}, bf16[4,32,384]{2,1,0:T(8,128)(2,1)S(1)}, u32[]{:S(2)}, u32[]{:S(2)}) collective-permute-start(bf16[4,32,384]{2,1,0:T(8,128)(2,1)S(1)} %collective-permute-done.12.refs_0_), channel_id=1, source_target_pairs={{0,1},{1,0},{2,3},{3,2},{4,5},{5,4},{6,7},{7,6},{8,9},{9,8},{10,11... | collective-permute-start | bytes 294920 | tf_op jit(solution)/shard_map/ppermute | solution.py:17
  52.5 7.3 %collective-permute-start.17 = (bf16[4,32,384]{2,1,0:T(8,128)(2,1)S(1)}, bf16[4,32,384]{2,1,0:T(8,128)(2,1)S(1)}, u32[]{:S(2)}, u32[]{:S(2)}) collective-permute-start(bf16[4,32,384]{2,1,0:T(8,128)(2,1)S(1)} %collective-permute-done.13.refs_1_), channel_id=1, source_target_pairs={{0,1},{1,0},{2,3},{3,2},{4,5},{5,4},{6,7},{7,6},{8,9},{9,8},{10,11... | collective-permute-start | bytes 294920 | tf_op jit(solution)/shard_map/ppermute | solution.py:17
  57.5 2.4 %collective-permute-start.18 = (bf16[4,32,384]{2,1,0:T(8,128)(2,1)S(1)}, bf16[4,32,384]{2,1,0:T(8,128)(2,1)S(1)}, u32[]{:S(2)}, u32[]{:S(2)}) collective-permute-start(bf16[4,32,384]{2,1,0:T(8,128)(2,1)S(1)} %collective-permute-done.14.refs_2_), channel_id=1, source_target_pairs={{0,1},{1,0},{2,3},{3,2},{4,5},{5,4},{6,7},{7,6},{8,9},{9,8},{10,11... | collective-permute-start | bytes 294920 | tf_op jit(solution)/shard_map/ppermute | solution.py:17
  58.5 1.3 %collective-permute-start.19 = (bf16[4,32,384]{2,1,0:T(8,128)(2,1)S(1)}, bf16[4,32,384]{2,1,0:T(8,128)(2,1)S(1)}, u32[]{:S(2)}, u32[]{:S(2)}) collective-permute-start(bf16[4,32,384]{2,1,0:T(8,128)(2,1)S(1)} %collective-permute-done.15.refs_3_), channel_id=1, source_target_pairs={{0,1},{1,0},{2,3},{3,2},{4,5},{5,4},{6,7},{7,6},{8,9},{9,8},{10,11... | collective-permute-start | bytes 294920 | tf_op jit(solution)/shard_map/ppermute | solution.py:17
  58.5 1.3 %collective-permute-start.4 = (s32[16]{0:T(128)S(1)}, s32[16]{0:T(128)S(1)}, u32[]{:S(2)}, u32[]{:S(2)}) collective-permute-start(s32[16]{0:T(128)S(1)} %get-tuple-element.14.own_chosen_ref), channel_id=1, source_target_pairs={{0,1},{1,0},{2,3},{3,2},{4,5},{5,4},{6,7},{7,6},{8,9},{9,8},{10,11... | collective-permute-start | bytes 200 | tf_op jit(solution)/shard_map/ppermute | solution.py:17

commit v2 on v0

v2 whole, which is shorter than its diff:
```python
import functools

import jax
import jax.numpy as jnp
from jax import lax
from jax.experimental import pallas as pl
from jax.experimental.pallas import tpu as pltpu
from jax.sharding import PartitionSpec as P

VMEM = pl.BlockSpec(memory_space=pltpu.VMEM)
SMEM = pl.BlockSpec(memory_space=pltpu.SMEM)
HBM = pl.BlockSpec(memory_space=pltpu.HBM)
PARAMS = pltpu.CompilerParams(vmem_limit_bytes=32 << 20)


def swap_rows(x):
    return lax.ppermute(x, "row", [(0, 1), (1, 0)])


def exchange(x, step):
    tiles = lax.axis_size("tile")
    pairs = [(2 * t + r, 2 * (t ^ (2 * step + r)) + r) for t in range(tiles) for r in range(2)]
    return lax.ppermute(x, ("tile", "row"), pairs)


def in_hbm(x):
    return pltpu.with_memory_space_constraint(x, pltpu.HBM)


def cost(moved, flops=0):
    return pl.CostEstimate(flops=flops, bytes_accessed=moved, transcendentals=0)


def plan_kernel(steps, capacity, here_ref, list_ref, mask_ref, dirs_ref, *refs):
    column_ref, live_ref, held_dirs_ref, held_list_ref, held_mask_ref, count_ref, sems = refs
    slots, blocks = steps * capacity, dirs_ref.shape[0]
    pairs = [(list_ref, held_list_ref), (mask_ref, held_mask_ref), (dirs_ref, held_dirs_ref)]
    copies = [pltpu.make_async_copy(*pair, sems.at[i]) for i, pair in enumerate(pairs)]
    for copy in copies:
        copy.start()
    for s in range(2 * steps):
        count_ref[s] = 0
    for copy in copies[:2]:
        copy.wait()
    tile, core = here_ref[0], here_ref[1]
    for k in range(list_ref.shape[1]):
        apart = lax.div(held_list_ref[0, k], blocks) ^ tile
        count = count_ref[apart]
        count_ref[apart] = count + 1
        mine = (apart & 1) == core
        slot = jnp.where(mine, (apart >> 1) * capacity + count, slots)
        column_ref[slot] = k
        live_ref[slot] = held_mask_ref[0, k]
    copies[2].wait()


def stage_kernel(slots, column_ref, own_ref, other_ref, own_out_ref, other_out_ref, sems):
    width = own_out_ref.shape[1] // slots
    copies = []
    for slot in range(slots):
        start = pl.multiple_of(column_ref[slot] * width, 128)
        for half, (sens_ref, out_ref) in enumerate(
            ((own_ref, own_out_ref), (other_ref, other_out_ref))
        ):
            copies.append(
                pltpu.make_async_copy(
                    sens_ref.at[:, pl.ds(start, width)],
                    out_ref.at[:, pl.ds(slot * width, width)],
                    sems.at[2 * slot + half],
                )
            )
            copies[-1].start()
    for copy in copies:
        copy.wait()


def select_kernel(steps, capacity, here_ref, *refs):
    lists, dirs_ref = refs[:steps][::-1], refs[steps]
    outs, (chosen_ref, slots_ref) = refs[steps + 1 : 2 * steps + 1], refs[2 * steps + 1 :]
    blocks = dirs_ref.shape[0]
    first = here_ref[0] * blocks
    for p in range(steps):
        found = jnp.int32(0)
        for k in range(lists[p].shape[1]):
            block = lists[p][0, k] - first
            mine = (block >= 0) & (block < blocks)
            slots_ref[jnp.where(mine, found, capacity)] = block
            found = found + mine.astype(jnp.int32)
        for c in range(capacity):
            block = slots_ref[c]
            chosen_ref[p * capacity + c] = block
            outs[p][c] = dirs_ref[block]


def predict_kernel(order, capacity, live_ref, own_ref, other_ref, weight_ref, *refs):
    dirs, (out_ref, flat_ref) = refs[: len(order)], refs[len(order) :]
    vecs, width = dirs[0].shape[1:]
    size = capacity * width
    for chunk_ref, p in zip(dirs, order):
        for c in range(capacity):
            live = live_ref[p * capacity + c].astype(jnp.float32)
            block = chunk_ref[c].astype(jnp.float32) * live
            start = p * size + c * width
            flat_ref[:, start : start + width] = block.astype(jnp.bfloat16)
    weight = weight_ref[...]
    for half, sens_ref in enumerate((own_ref, other_ref)):
        out_ref[half, :vecs] = lax.dot_general(
            flat_ref[...],
            sens_ref[...],
            (((1,), (1,)), ((), ())),
            preferred_element_type=jnp.float32,
        )
        out_ref[half, vecs:] = jnp.broadcast_to(weight * weight, (8, weight.shape[1]))


def back_kernel(group, capacity, live_ref, own_ref, other_ref, mine_ref, theirs_ref, *outs):
    vecs, width = outs[0].shape[1:]
    own = mine_ref[0, vecs : vecs + 1] * (mine_ref[0, :vecs] + theirs_ref[1, :vecs])
    other = theirs_ref[0, vecs : vecs + 1] * (mine_ref[1, :vecs] + theirs_ref[0, :vecs])
    own, other = own.astype(jnp.bfloat16), other.astype(jnp.bfloat16)
    size = capacity * width
    for place, slot in enumerate(group):
        span = slice(slot * size, (slot + 1) * size)
        grads = jnp.dot(own, own_ref[:, span], preferred_element_type=jnp.float32)
        grads += jnp.dot(other, other_ref[:, span], preferred_element_type=jnp.float32)
        for c in range(capacity):
            live = live_ref[slot * capacity + c].astype(jnp.float32)
            part = grads[:, c * width : (c + 1) * width] * live
            outs[place][c] = part.astype(jnp.bfloat16)


def add_chunk(capacity, chosen_ref, slot, chunk_ref, total_ref):
    for c in range(capacity):
        total_ref[chosen_ref[slot * capacity + c]] += chunk_ref[c].astype(jnp.float32)


def sum_kernel(order, capacity, chosen_ref, *refs):
    out_ref = refs[-1]
    out_ref[...] = jnp.zeros_like(out_ref)
    for slot, chunk_ref in zip(order, refs):
        add_chunk(capacity, chosen_ref, slot, chunk_ref, out_ref)


def finish_kernel(order, capacity, chosen_ref, own_ref, *refs):
    sum_kernel(order, capacity, chosen_ref, *refs)
    refs[-1][...] += own_ref[...]


def on_device(directions, sensitivity, data_weight, foot_list, foot_mask):
    tiles = lax.axis_size("tile")
    blocks, vecs, width = directions.shape
    rows = sensitivity.shape[1]
    foot = foot_list.shape[1]
    steps, capacity = tiles // 2, foot // tiles
    slots = steps * capacity
    here = jnp.stack([lax.axis_index("tile"), lax.axis_index("row")]).astype(jnp.int32)
    half = (steps + 1) // 2
    far, near = list(range(half, steps)), list(range(half))
    order = far + near

    own_sens = in_hbm(sensitivity[0])
    other_sens = in_hbm(swap_rows(sensitivity[0]))
    lists = {p: exchange(foot_list, p) for p in order}
    table = jax.ShapeDtypeStruct((slots + 1,), jnp.int32)
    column, live, held_dirs = pl.pallas_call(
        functools.partial(plan_kernel, steps, capacity),
        out_shape=[table, table, pltpu.VMEM(directions.shape, jnp.bfloat16)],
        in_specs=[SMEM] + [HBM] * 3,
        out_specs=[SMEM] * 2 + [VMEM],
        scratch_shapes=[
            pltpu.SMEM(foot_list.shape, jnp.int32),
            pltpu.SMEM(foot_mask.shape, jnp.int32),
            pltpu.SMEM((tiles,), jnp.int32),
            pltpu.SemaphoreType.DMA((3,)),
        ],
        compiler_params=PARAMS,
        cost_estimate=cost(1),
        name="plan_columns",
    )(here, in_hbm(foot_list), in_hbm(foot_mask), in_hbm(directions))

    chunk = jax.ShapeDtypeStruct((capacity, vecs, width), jnp.bfloat16)
    *chunks, chosen = pl.pallas_call(
        functools.partial(select_kernel, steps, capacity),
        out_shape=[chunk] * steps + [jax.ShapeDtypeStruct((slots,), jnp.int32)],
        in_specs=[SMEM] * (steps + 1) + [VMEM],
        out_specs=[VMEM] * steps + [SMEM],
        scratch_shapes=[pltpu.SMEM((capacity + 1,), jnp.int32)],
        compiler_params=PARAMS,
        cost_estimate=cost(1),
        name="select_blocks",
    )(here, *[lists[p] for p in reversed(range(steps))], held_dirs)
    fetched = {p: exchange(chunks[p], p) for p in order}

    columns = pltpu.VMEM((rows, slots * width), jnp.bfloat16)
    own_sens, other_sens = pl.pallas_call(
        functools.partial(stage_kernel, slots),
        out_shape=[columns] * 2,
        in_specs=[SMEM] + [HBM] * 2,
        out_specs=[VMEM] * 2,
        scratch_shapes=[pltpu.SemaphoreType.DMA((2 * slots,))],
        compiler_params=PARAMS,
        cost_estimate=cost(1),
        name="stage_columns",
    )(column, own_sens, other_sens)

    partial = pl.pallas_call(
        functools.partial(predict_kernel, order, capacity),
        out_shape=jax.ShapeDtypeStruct((2, vecs + 8, rows), jnp.float32),
        in_specs=[SMEM] + [VMEM] * (3 + steps),
        out_specs=VMEM,
        scratch_shapes=[pltpu.VMEM((vecs, slots * width), jnp.bfloat16)],
        compiler_params=PARAMS,
        cost_estimate=cost(1),
        name="predict",
    )(live, own_sens, other_sens, data_weight, *[fetched[p] for p in order])
    partial, chosen = lax.optimization_barrier((partial, chosen))
    other_partial, other_chosen = lax.optimization_barrier((swap_rows(partial), swap_rows(chosen)))

    def back(group, mine):
        return pl.pallas_call(
            functools.partial(back_kernel, group, capacity),
            out_shape=[chunk] * len(group),
            in_specs=[SMEM] + [VMEM] * 4,
            out_specs=[VMEM] * len(group),
            compiler_params=PARAMS,
            cost_estimate=cost(1),
            name="back_project",
        )(live, own_sens, other_sens, mine, other_partial)

    grads = back(order, partial)
    returned = {p: exchange(x, p) for p, x in zip(order, grads)}
    other_returned = {p: swap_rows(returned[p]) for p in order}

    total = jax.ShapeDtypeStruct((blocks, vecs, width), jnp.float32)
    own_sum = pl.pallas_call(
        functools.partial(sum_kernel, order, capacity),
        out_shape=total,
        in_specs=[SMEM] + [VMEM] * len(order),
        out_specs=VMEM,
        compiler_params=PARAMS,
        cost_estimate=cost(1),
        name="sum_blocks",
    )(chosen, *[returned[slot] for slot in order])
    return pl.pallas_call(
        functools.partial(finish_kernel, order, capacity),
        out_shape=total,
        in_specs=[SMEM] + [VMEM] * (1 + len(order)),
        out_specs=VMEM,
        compiler_params=PARAMS,
        cost_estimate=cost(1),
        name="finish_blocks",
    )(other_chosen, own_sum, *[other_returned[slot] for slot in order])


def solution(mesh):
    in_specs = (
        P(("parts", "tile"), None, None),
        P(("parts", "tile"), "row", None),
        P(("parts", "tile"), "row"),
        P(("parts", "tile"), None),
        P(("parts", "tile"), None),
    )
    out_specs = P(("parts", "tile"), None, None)
    return jax.shard_map(
        on_device, mesh=mesh, in_specs=in_specs, out_specs=out_specs, check_vma=False
    )
```

time: 139 us -> 46.8 us (0.34)
  blocking collectives: 65.4 us -> 0 us
  waiting for transfers between devices: 34.7 us -> 11.8 us
  starting transfers between devices: 3.59 us -> 20.6 us
  Pallas kernels: 0 us -> 14.1 us
  between operations: 13.6 us -> 0.11 us
  matrix products: 8.98 us -> 0 us
  other arithmetic: 7.43 us -> 0.07 us
  local copies, waits for them, and re-layouts: 5.44 us -> 0.01 us
    all_to_all x1 -> x0, blocking collectives: 43 us -> none  [on_device(): lax.all_to_all(outgoing, 'tile', split_axis=0, concat_axis=0, tiled=True)]
    all_gather x1 -> x0, blocking collectives: 22.4 us -> none  [on_device(): lax.all_gather(foot_list, 'tile', axis=0, tiled=True)]
    ppermute x0 -> x19, starting transfers between devices: none -> 20.6 us  [the longest x12 15 us: exchange(): return lax.ppermute(x, ('tile', 'row'), pairs)]
    psum x1 -> x0, waiting for transfers between devices: 18.8 us -> none  [on_device(): lax.psum(lax.dot_general(scaled, sens_rows, (((0,), (0,)), ((), ())), pre...]
    all_to_all x1 -> x0, waiting for transfers between devices: 15.8 us -> none  [on_device(): lax.all_to_all(outbound, 'tile', split_axis=0, concat_axis=0, tiled=True)]
    pallas_call x0 -> x7, Pallas kernels: none -> 14.1 us  [the longest x1 3.77 us: on_device(): pl.pallas_call(functools.partial(stage_kernel, slots), out_shape=[columns...]
    ppermute x0 -> x19, waiting for transfers between devices: none -> 11.8 us  [the longest x12 10.5 us: exchange(): return lax.ppermute(x, ('tile', 'row'), pairs)]
    dot_general x1 -> x0, matrix products: 8.98 us -> none  [on_device(): lax.dot_general(scaled, sens_rows, (((0,), (0,)), ((), ())), preferred_el...]
  transfers between devices with their start and end apart: 2 -> 19, of which waited for: 2 -> 8; matrix products, arithmetic and copies ran while one was open for 1% -> 0% of each run, Pallas kernels for 0% -> 18%
where the time goes in v2:
time: 46.8 us; the launch traced here: 46.7 us
  starting transfers between devices  20.6 us (44%)
  Pallas kernels  14.1 us (30%)
  waiting for transfers between devices  11.8 us (25%)
    ppermute x12, starting transfers between devices, exchange(): return lax.ppermute(x, ('tile', 'row'), pairs)  15 us
    ppermute x12, waiting for transfers between devices, exchange(): return lax.ppermute(x, ('tile', 'row'), pairs)  10.5 us
    ppermute x7, starting transfers between devices, swap_rows(): return lax.ppermute(x, 'row', [(0, 1), (1, 0)])  5.57 us
    pallas_call x1, Pallas kernels, on_device(): pl.pallas_call(functools.partial(stage_kernel, slots), out_shape=[columns...  3.77 us
    pallas_call x1, Pallas kernels, on_device(): pl.pallas_call(functools.partial(predict_kernel, order, capacity), out_sh...  2.51 us
    pallas_call x1, Pallas kernels, on_device(): pl.pallas_call(functools.partial(plan_kernel, steps, capacity), out_shape...  2.16 us
    pallas_call x1, Pallas kernels, back(): pl.pallas_call(functools.partial(back_kernel, group, capacity), out_shape...  1.72 us
    pallas_call x1, Pallas kernels, on_device(): pl.pallas_call(functools.partial(finish_kernel, order, capacity), out_sha...  1.66 us
  transfers between devices with their start and end apart: 19, of which 8 were waited for; matrix products, arithmetic and copies ran while one was open for 0% of the time, Pallas kernels for 18%

profile of v2, /device:TPU:0, one launch (start us, length us, event | category | flops | bytes accessed | tf_op | source)
XLA Modules:
  0.0 46.7 jit_solution(16855697777757175088)
XLA Ops:
  0.0 0.5 collective-permute-start
  0.5 3.6 %collective-permute-start.2 = (s32[1,32]{1,0:T(1,128)}, s32[1,32]{1,0:T(1,128)S(1)}, u32[]{:S(2)}, u32[]{:S(2)}) collective-permute-start(s32[1,32]{1,0:T(1,128)} %list_ref.1), channel_id=1, source_target_pairs={{0,8},{1,11},{2,10},{3,9},{4,12},{5,15},{6,14},{7,13},{8,0},{9,3},... | collective-permute-start | bytes 392 | tf_op jit(solution)/shard_map/ppermute | solution.py:23
  4.0 1.3 %collective-permute-start.1 = (s32[1,32]{1,0:T(1,128)}, s32[1,32]{1,0:T(1,128)S(1)}, u32[]{:S(2)}, u32[]{:S(2)}) collective-permute-start(s32[1,32]{1,0:T(1,128)} %list_ref.1), channel_id=1, source_target_pairs={{0,12},{1,15},{2,14},{3,13},{4,8},{5,11},{6,10},{7,9},{8,4},{9,7},... | collective-permute-start | bytes 392 | tf_op jit(solution)/shard_map/ppermute | solution.py:23
  5.4 1.3 %collective-permute-start.4 = (s32[1,32]{1,0:T(1,128)}, s32[1,32]{1,0:T(1,128)S(1)}, u32[]{:S(2)}, u32[]{:S(2)}) collective-permute-start(s32[1,32]{1,0:T(1,128)} %list_ref.1), channel_id=1, source_target_pairs={{0,0},{1,3},{2,2},{3,1},{4,4},{5,7},{6,6},{7,5},{8,8},{9,11},{10,1... | collective-permute-start | bytes 392 | tf_op jit(solution)/shard_map/ppermute | solution.py:23
  6.7 0.2 collective-permute-start.3
  6.9 0.1 pad_add_fusion.here_ref
  7.0 2.2 %plan_columns.1 = (s32[17]{0:T(128)S(1)}, s32[17]{0:T(128)S(1)}, bf16[16,32,384]{2,1,0:T(8,128)(2,1)S(1)}) custom-call(s32[2]{0:T(128)S(1)} %pad_add_fusion.here_ref, s32[1,32]{1,0:T(1,128)} %list_ref.1, s32[1,32]{1,0:T(1,128)} %mask_ref.1, bf16[16,32,384]{2,1,0:T(8,128)(2,1)} %dirs_ref.1), custom_call_target="tpu_custom_call" | custom-call | bytes 1 | tf_op jit(solution)/shard_map/plan_columns/pallas_call | solution.py:165
  9.2 0.3 collective-permute-done.1.refs_0_
  9.5 0.9 %collective-permute-done.3.refs_2_ = s32[1,32]{1,0:T(1,128)S(1)} collective-permute-done((s32[1,32]{1,0:T(1,128)}, s32[1,32]{1,0:T(1,128)S(1)}, u32[]{:S(2)}, u32[]{:S(2)}) %collective-permute-start.3) | collective-permute-done | bytes 160 | tf_op jit(solution)/shard_map/ppermute | solution.py:23
  10.4 1.6 %select_blocks.1 = (bf16[4,32,384]{2,1,0:T(8,128)(2,1)S(1)}, bf16[4,32,384]{2,1,0:T(8,128)(2,1)S(1)}, bf16[4,32,384]{2,1,0:T(8,128)(2,1)S(1)}, bf16[4,32,384]{2,1,0:T(8,128)(2,1)S(1)}, s32[16]{0:T(128)S(1)}) custom-call(s32[2]{0:T(128)S(1)} %pad_add_fusion.here_ref, s32[1,32]{1,0:T(1,128)S(1)} %collective-permute-done.1.refs_0_, ...), custom_call_target="tpu_custom_call" | custom-call | bytes 1 | tf_op jit(solution)/shard_map/select_blocks/pallas_call | solution.py:182
  12.0 1.8 %collective-permute-start.5 = (bf16[4,32,384]{2,1,0:T(8,128)(2,1)S(1)}, bf16[4,32,384]{2,1,0:T(8,128)(2,1)S(1)}, u32[]{:S(2)}, u32[]{:S(2)}) collective-permute-start(bf16[4,32,384]{2,1,0:T(8,128)(2,1)S(1)} %get-tuple-element.28), channel_id=1, source_target_pairs={{0,8},{1,11},{2,10},{3,9},{4,12},{5,15},{6,14},{7,13},{8,0},{9,3},... | collective-permute-start | bytes 294920 | tf_op jit(solution)/shard_map/ppermute | solution.py:23
  13.7 1.3 %collective-permute-start.6 = (bf16[4,32,384]{2,1,0:T(8,128)(2,1)S(1)}, bf16[4,32,384]{2,1,0:T(8,128)(2,1)S(1)}, u32[]{:S(2)}, u32[]{:S(2)}) collective-permute-start(bf16[4,32,384]{2,1,0:T(8,128)(2,1)S(1)} %get-tuple-element.29), channel_id=1, source_target_pairs={{0,12},{1,15},{2,14},{3,13},{4,8},{5,11},{6,10},{7,9},{8,4},{9,7},... | collective-permute-start | bytes 294920 | tf_op jit(solution)/shard_map/ppermute | solution.py:23
  15.0 0.7 %collective-permute-start.7 = (bf16[4,32,384]{2,1,0:T(8,128)(2,1)S(1)}, bf16[4,32,384]{2,1,0:T(8,128)(2,1)S(1)}, u32[]{:S(2)}, u32[]{:S(2)}) collective-permute-start(bf16[4,32,384]{2,1,0:T(8,128)(2,1)S(1)} %get-tuple-element.30), channel_id=1, source_target_pairs={{0,0},{1,3},{2,2},{3,1},{4,4},{5,7},{6,6},{7,5},{8,8},{9,11},{10,1... | collective-permute-start | bytes 294920 | tf_op jit(solution)/shard_map/ppermute | solution.py:23
  15.7 0.5 %collective-permute-start.8 = (bf16[4,32,384]{2,1,0:T(8,128)(2,1)S(1)}, bf16[4,32,384]{2,1,0:T(8,128)(2,1)S(1)}, u32[]{:S(2)}, u32[]{:S(2)}) collective-permute-start(bf16[4,32,384]{2,1,0:T(8,128)(2,1)S(1)} %get-tuple-element.31), channel_id=1, source_target_pairs={{0,4},{1,7},{2,6},{3,5},{4,0},{5,3},{6,2},{7,1},{8,12},{9,15},{10,... | collective-permute-start | bytes 294920 | tf_op jit(solution)/shard_map/ppermute | solution.py:23
  16.3 3.8 %stage_columns.1 = (bf16[256,6144]{1,0:T(8,128)(2,1)S(1)}, bf16[256,6144]{1,0:T(8,128)(2,1)S(1)}) custom-call(s32[17]{0:T(128)S(1)} %get-tuple-element.24.column_ref, bf16[256,12288]{1,0:T(8,128)(2,1)} %bitcast.4, bf16[256,12288]{1,0:T(8,128)(2,1)} %collective-permute-done.other_ref), custom_call_target="tpu_custom_call" | custom-call | bytes 1 | tf_op jit(solution)/shard_map/stage_columns/pallas_call | solution.py:195
  20.0 1.3 %collective-permute-done.5.refs_0_ = bf16[4,32,384]{2,1,0:T(8,128)(2,1)S(1)} collective-permute-done((bf16[4,32,384]{2,1,0:T(8,128)(2,1)S(1)}, bf16[4,32,384]{2,1,0:T(8,128)(2,1)S(1)}, u32[]{:S(2)}, u32[]{:S(2)}) %collective-permute-start.5) | collective-permute-done | bytes 98336 | tf_op jit(solution)/shard_map/ppermute | solution.py:23
  21.4 0.6 %collective-permute-done.8.refs_3_ = bf16[4,32,384]{2,1,0:T(8,128)(2,1)S(1)} collective-permute-done((bf16[4,32,384]{2,1,0:T(8,128)(2,1)S(1)}, bf16[4,32,384]{2,1,0:T(8,128)(2,1)S(1)}, u32[]{:S(2)}, u32[]{:S(2)}) %collective-permute-start.8) | collective-permute-done | bytes 98336 | tf_op jit(solution)/shard_map/ppermute | solution.py:23
  22.0 2.5 %predict.1.mine_ref = f32[2,40,256]{2,1,0:T(8,128)S(1)} custom-call(s32[17]{0:T(128)S(1)} %get-tuple-element.23.live_ref, bf16[256,6144]{1,0:T(8,128)(2,1)S(1)} %get-tuple-element.25.own_ref, bf16[256,6144]{1,0:T(8,128)(2,1)S(1)} %get-tuple-element.26.other_ref, f32[1,256]{1,0:T(1,128)S(1)} %copy-done, ...), custom_call_target="tpu_custom_call" | custom-call | bytes 1 | tf_op jit(solution)/shard_map/predict/pallas_call | solution.py:206
  24.5 3.8 %collective-permute-start.9 = (f32[2,40,256]{2,1,0:T(8,128)S(1)}, f32[2,40,256]{2,1,0:T(8,128)S(1)}, u32[]{:S(2)}, u32[]{:S(2)}) collective-permute-start(f32[2,40,256]{2,1,0:T(8,128)S(1)} %predict.1.mine_ref), channel_id=1, source_target_pairs={{0,1},{1,0},{2,3},{3,2},{4,5},{5,4},{6,7},{7,6},{8,9},{9,8},{10,11... | collective-permute-start | bytes 245768 | tf_op jit(solution)/shard_map/ppermute | solution.py:17
  28.4 1.0 %collective-permute-done.10.chosen_ref = s32[16]{0:T(128)S(1)} collective-permute-done((s32[16]{0:T(128)S(1)}, s32[16]{0:T(128)S(1)}, u32[]{:S(2)}, u32[]{:S(2)}) %collective-permute-start.10) | collective-permute-done | bytes 96 | tf_op jit(solution)/shard_map/ppermute | solution.py:17
  29.4 1.7 %back_project.1 = (bf16[4,32,384]{2,1,0:T(8,128)(2,1)S(1)}, bf16[4,32,384]{2,1,0:T(8,128)(2,1)S(1)}, bf16[4,32,384]{2,1,0:T(8,128)(2,1)S(1)}, bf16[4,32,384]{2,1,0:T(8,128)(2,1)S(1)}) custom-call(s32[17]{0:T(128)S(1)} %get-tuple-element.23.live_ref, bf16[256,6144]{1,0:T(8,128)(2,1)S(1)} %get-tuple-element.25.own_ref, ...), custom_call_target="tpu_custom_call" | custom-call | bytes 1 | tf_op jit(solution)/shard_map/back_project/pallas_call | solution.py:220
  31.1 2.0 %collective-permute-start.11 = (bf16[4,32,384]{2,1,0:T(8,128)(2,1)S(1)}, bf16[4,32,384]{2,1,0:T(8,128)(2,1)S(1)}, u32[]{:S(2)}, u32[]{:S(2)}) collective-permute-start(bf16[4,32,384]{2,1,0:T(8,128)(2,1)S(1)} %get-tuple-element.37), channel_id=1, source_target_pairs={{0,8},{1,11},{2,10},{3,9},{4,12},{5,15},{6,14},{7,13},{8,0},{9,3},... | collective-permute-start | bytes 294920 | tf_op jit(solution)/shard_map/ppermute | solution.py:23
  33.1 1.2 %collective-permute-start.12 = (bf16[4,32,384]{2,1,0:T(8,128)(2,1)S(1)}, bf16[4,32,384]{2,1,0:T(8,128)(2,1)S(1)}, u32[]{:S(2)}, u32[]{:S(2)}) collective-permute-start(bf16[4,32,384]{2,1,0:T(8,128)(2,1)S(1)} %get-tuple-element.38), channel_id=1, source_target_pairs={{0,12},{1,15},{2,14},{3,13},{4,8},{5,11},{6,10},{7,9},{8,4},{9,7},... | collective-permute-start | bytes 294920 | tf_op jit(solution)/shard_map/ppermute | solution.py:23
  34.4 0.7 %collective-permute-start.13 = (bf16[4,32,384]{2,1,0:T(8,128)(2,1)S(1)}, bf16[4,32,384]{2,1,0:T(8,128)(2,1)S(1)}, u32[]{:S(2)}, u32[]{:S(2)}) collective-permute-start(bf16[4,32,384]{2,1,0:T(8,128)(2,1)S(1)} %get-tuple-element.39), channel_id=1, source_target_pairs={{0,0},{1,3},{2,2},{3,1},{4,4},{5,7},{6,6},{7,5},{8,8},{9,11},{10,1... | collective-permute-start | bytes 294920 | tf_op jit(solution)/shard_map/ppermute | solution.py:23
  35.0 0.4 collective-permute-start.14
  35.4 6.5 %collective-permute-done.11.refs_0_ = bf16[4,32,384]{2,1,0:T(8,128)(2,1)S(1)} collective-permute-done((bf16[4,32,384]{2,1,0:T(8,128)(2,1)S(1)}, bf16[4,32,384]{2,1,0:T(8,128)(2,1)S(1)}, u32[]{:S(2)}, u32[]{:S(2)}) %collective-permute-start.11) | collective-permute-done | bytes 98336 | tf_op jit(solution)/shard_map/ppermute | solution.py:23
  42.0 0.5 %collective-permute-start.16 = (bf16[4,32,384]{2,1,0:T(8,128)(2,1)S(1)}, bf16[4,32,384]{2,1,0:T(8,128)(2,1)S(1)}, u32[]{:S(2)}, u32[]{:S(2)}) collective-permute-start(bf16[4,32,384]{2,1,0:T(8,128)(2,1)S(1)} %collective-permute-done.12.refs_1_), channel_id=1, source_target_pairs={{0,1},{1,0},{2,3},{3,2},{4,5},{5,4},{6,7},{7,6},{8,9},{9,8},{10,11... | collective-permute-start | bytes 294920 | tf_op jit(solution)/shard_map/ppermute | solution.py:17
  42.6 0.8 %collective-permute-done.14.refs_3_ = bf16[4,32,384]{2,1,0:T(8,128)(2,1)S(1)} collective-permute-done((bf16[4,32,384]{2,1,0:T(8,128)(2,1)S(1)}, bf16[4,32,384]{2,1,0:T(8,128)(2,1)S(1)}, u32[]{:S(2)}, u32[]{:S(2)}) %collective-permute-start.14) | collective-permute-done | bytes 98336 | tf_op jit(solution)/shard_map/ppermute | solution.py:23
  43.4 0.7 %collective-permute-start.18 = (bf16[4,32,384]{2,1,0:T(8,128)(2,1)S(1)}, bf16[4,32,384]{2,1,0:T(8,128)(2,1)S(1)}, u32[]{:S(2)}, u32[]{:S(2)}) collective-permute-start(bf16[4,32,384]{2,1,0:T(8,128)(2,1)S(1)} %collective-permute-done.14.refs_3_), channel_id=1, source_target_pairs={{0,1},{1,0},{2,3},{3,2},{4,5},{5,4},{6,7},{7,6},{8,9},{9,8},{10,11... | collective-permute-start | bytes 294920 | tf_op jit(solution)/shard_map/ppermute | solution.py:17
  44.1 0.7 %sum_blocks.1.own_ref = f32[16,32,384]{2,1,0:T(8,128)S(1)} custom-call(s32[16]{0:T(128)S(1)} %get-tuple-element.34.chosen_ref, bf16[4,32,384]{2,1,0:T(8,128)(2,1)S(1)} %collective-permute-done.11.refs_0_, bf16[4,32,384]{2,1,0:T(8,128)(2,1)S(1)} %collective-permute-done.12.refs_1_, bf16[4,32,384]{2,1,0:T(8,128)(2,1)S(1)} %collective-permute-done.13.refs_2_, ...), custom_call_target="tpu_custom_call" | custom-call | bytes 1 | tf_op jit(solution)/shard_map/sum_blocks/pallas_call | solution.py:235
  44.8 0.2 collective-permute-done.18.refs_3_
  45.0 1.7 %finish_blocks.1 = f32[16,32,384]{2,1,0:T(8,128)} custom-call(s32[16]{0:T(128)S(1)} %collective-permute-done.10.chosen_ref, f32[16,32,384]{2,1,0:T(8,128)S(1)} %sum_blocks.1.own_ref, bf16[4,32,384]{2,1,0:T(8,128)(2,1)S(1)} %collective-permute-done.15.refs_0_, bf16[4,32,384]{2,1,0:T(8,128)(2,1)S(1)} %collective-permute-done.16.refs_1_, ...), custom_call_target="tpu_custom_call" | custom-call | bytes 1 | tf_op jit(solution)/shard_map/finish_blocks/pallas_call | solution.py:244
  (16 shorter events, 0.2 us)
Async XLA Ops:
  0.0 16.3 %collective-permute-start = (bf16[256,12288]{1,0:T(8,128)(2,1)}, bf16[256,12288]{1,0:T(8,128)(2,1)}, u32[]{:S(2)}, u32[]{:S(2)}) collective-permute-start(bf16[256,12288]{1,0:T(8,128)(2,1)} %bitcast.3), channel_id=1, source_target_pairs={{0,1},{1,0},{2,3},{3,2},{4,5},{5,4},{6,7},{7,6},{8,9},{9,8},{10,11... | collective-permute-start | bytes 18874376 | tf_op jit(solution)/shard_map/ppermute | solution.py:17
  0.5 8.7 %collective-permute-start.2 = (s32[1,32]{1,0:T(1,128)}, s32[1,32]{1,0:T(1,128)S(1)}, u32[]{:S(2)}, u32[]{:S(2)}) collective-permute-start(s32[1,32]{1,0:T(1,128)} %list_ref.1), channel_id=1, source_target_pairs={{0,8},{1,11},{2,10},{3,9},{4,12},{5,15},{6,14},{7,13},{8,0},{9,3},... | collective-permute-start | bytes 392 | tf_op jit(solution)/shard_map/ppermute | solution.py:23
  4.0 5.5 %collective-permute-start.1 = (s32[1,32]{1,0:T(1,128)}, s32[1,32]{1,0:T(1,128)S(1)}, u32[]{:S(2)}, u32[]{:S(2)}) collective-permute-start(s32[1,32]{1,0:T(1,128)} %list_ref.1), channel_id=1, source_target_pairs={{0,12},{1,15},{2,14},{3,13},{4,8},{5,11},{6,10},{7,9},{8,4},{9,7},... | collective-permute-start | bytes 392 | tf_op jit(solution)/shard_map/ppermute | solution.py:23
  5.4 4.1 %collective-permute-start.4 = (s32[1,32]{1,0:T(1,128)}, s32[1,32]{1,0:T(1,128)S(1)}, u32[]{:S(2)}, u32[]{:S(2)}) collective-permute-start(s32[1,32]{1,0:T(1,128)} %list_ref.1), channel_id=1, source_target_pairs={{0,0},{1,3},{2,2},{3,1},{4,4},{5,7},{6,6},{7,5},{8,8},{9,11},{10,1... | collective-permute-start | bytes 392 | tf_op jit(solution)/shard_map/ppermute | solution.py:23
  6.7 3.7 %collective-permute-start.3 = (s32[1,32]{1,0:T(1,128)}, s32[1,32]{1,0:T(1,128)S(1)}, u32[]{:S(2)}, u32[]{:S(2)}) collective-permute-start(s32[1,32]{1,0:T(1,128)} %list_ref.1), channel_id=1, source_target_pairs={{0,4},{1,7},{2,6},{3,5},{4,0},{5,3},{6,2},{7,1},{8,12},{9,15},{10,... | collective-permute-start | bytes 392 | tf_op jit(solution)/shard_map/ppermute | solution.py:23
  12.0 9.4 %collective-permute-start.5 = (bf16[4,32,384]{2,1,0:T(8,128)(2,1)S(1)}, bf16[4,32,384]{2,1,0:T(8,128)(2,1)S(1)}, u32[]{:S(2)}, u32[]{:S(2)}) collective-permute-start(bf16[4,32,384]{2,1,0:T(8,128)(2,1)S(1)} %get-tuple-element.28), channel_id=1, source_target_pairs={{0,8},{1,11},{2,10},{3,9},{4,12},{5,15},{6,14},{7,13},{8,0},{9,3},... | collective-permute-start | bytes 294920 | tf_op jit(solution)/shard_map/ppermute | solution.py:23
  13.7 7.6 %collective-permute-start.6 = (bf16[4,32,384]{2,1,0:T(8,128)(2,1)S(1)}, bf16[4,32,384]{2,1,0:T(8,128)(2,1)S(1)}, u32[]{:S(2)}, u32[]{:S(2)}) collective-permute-start(bf16[4,32,384]{2,1,0:T(8,128)(2,1)S(1)} %get-tuple-element.29), channel_id=1, source_target_pairs={{0,12},{1,15},{2,14},{3,13},{4,8},{5,11},{6,10},{7,9},{8,4},{9,7},... | collective-permute-start | bytes 294920 | tf_op jit(solution)/shard_map/ppermute | solution.py:23
  15.0 6.3 %collective-permute-start.7 = (bf16[4,32,384]{2,1,0:T(8,128)(2,1)S(1)}, bf16[4,32,384]{2,1,0:T(8,128)(2,1)S(1)}, u32[]{:S(2)}, u32[]{:S(2)}) collective-permute-start(bf16[4,32,384]{2,1,0:T(8,128)(2,1)S(1)} %get-tuple-element.30), channel_id=1, source_target_pairs={{0,0},{1,3},{2,2},{3,1},{4,4},{5,7},{6,6},{7,5},{8,8},{9,11},{10,1... | collective-permute-start | bytes 294920 | tf_op jit(solution)/shard_map/ppermute | solution.py:23
  15.7 6.3 %collective-permute-start.8 = (bf16[4,32,384]{2,1,0:T(8,128)(2,1)S(1)}, bf16[4,32,384]{2,1,0:T(8,128)(2,1)S(1)}, u32[]{:S(2)}, u32[]{:S(2)}) collective-permute-start(bf16[4,32,384]{2,1,0:T(8,128)(2,1)S(1)} %get-tuple-element.31), channel_id=1, source_target_pairs={{0,4},{1,7},{2,6},{3,5},{4,0},{5,3},{6,2},{7,1},{8,12},{9,15},{10,... | collective-permute-start | bytes 294920 | tf_op jit(solution)/shard_map/ppermute | solution.py:23
  16.3 5.7 %copy-start = (f32[1,256]{1,0:T(1,128)S(1)}, f32[1,256]{1,0:T(1,128)}, u32[]{:S(2)}) copy-start(f32[1,256]{1,0:T(1,128)} %weight_ref.1) | copy-start | bytes 3076
  24.5 4.9 %collective-permute-start.9 = (f32[2,40,256]{2,1,0:T(8,128)S(1)}, f32[2,40,256]{2,1,0:T(8,128)S(1)}, u32[]{:S(2)}, u32[]{:S(2)}) collective-permute-start(f32[2,40,256]{2,1,0:T(8,128)S(1)} %predict.1.mine_ref), channel_id=1, source_target_pairs={{0,1},{1,0},{2,3},{3,2},{4,5},{5,4},{6,7},{7,6},{8,9},{9,8},{10,11... | collective-permute-start | bytes 245768 | tf_op jit(solution)/shard_map/ppermute | solution.py:17
  28.3 1.1 %collective-permute-start.10 = (s32[16]{0:T(128)S(1)}, s32[16]{0:T(128)S(1)}, u32[]{:S(2)}, u32[]{:S(2)}) collective-permute-start(s32[16]{0:T(128)S(1)} %get-tuple-element.34.chosen_ref), channel_id=1, source_target_pairs={{0,1},{1,0},{2,3},{3,2},{4,5},{5,4},{6,7},{7,6},{8,9},{9,8},{10,11... | collective-permute-start | bytes 200 | tf_op jit(solution)/shard_map/ppermute | solution.py:17
  31.1 10.8 %collective-permute-start.11 = (bf16[4,32,384]{2,1,0:T(8,128)(2,1)S(1)}, bf16[4,32,384]{2,1,0:T(8,128)(2,1)S(1)}, u32[]{:S(2)}, u32[]{:S(2)}) collective-permute-start(bf16[4,32,384]{2,1,0:T(8,128)(2,1)S(1)} %get-tuple-element.37), channel_id=1, source_target_pairs={{0,8},{1,11},{2,10},{3,9},{4,12},{5,15},{6,14},{7,13},{8,0},{9,3},... | collective-permute-start | bytes 294920 | tf_op jit(solution)/shard_map/ppermute | solution.py:23
  33.1 8.9 %collective-permute-start.12 = (bf16[4,32,384]{2,1,0:T(8,128)(2,1)S(1)}, bf16[4,32,384]{2,1,0:T(8,128)(2,1)S(1)}, u32[]{:S(2)}, u32[]{:S(2)}) collective-permute-start(bf16[4,32,384]{2,1,0:T(8,128)(2,1)S(1)} %get-tuple-element.38), channel_id=1, source_target_pairs={{0,12},{1,15},{2,14},{3,13},{4,8},{5,11},{6,10},{7,9},{8,4},{9,7},... | collective-permute-start | bytes 294920 | tf_op jit(solution)/shard_map/ppermute | solution.py:23
  34.4 8.1 %collective-permute-start.13 = (bf16[4,32,384]{2,1,0:T(8,128)(2,1)S(1)}, bf16[4,32,384]{2,1,0:T(8,128)(2,1)S(1)}, u32[]{:S(2)}, u32[]{:S(2)}) collective-permute-start(bf16[4,32,384]{2,1,0:T(8,128)(2,1)S(1)} %get-tuple-element.39), channel_id=1, source_target_pairs={{0,0},{1,3},{2,2},{3,1},{4,4},{5,7},{6,6},{7,5},{8,8},{9,11},{10,1... | collective-permute-start | bytes 294920 | tf_op jit(solution)/shard_map/ppermute | solution.py:23
  35.0 8.4 %collective-permute-start.14 = (bf16[4,32,384]{2,1,0:T(8,128)(2,1)S(1)}, bf16[4,32,384]{2,1,0:T(8,128)(2,1)S(1)}, u32[]{:S(2)}, u32[]{:S(2)}) collective-permute-start(bf16[4,32,384]{2,1,0:T(8,128)(2,1)S(1)} %get-tuple-element.40), channel_id=1, source_target_pairs={{0,4},{1,7},{2,6},{3,5},{4,0},{5,3},{6,2},{7,1},{8,12},{9,15},{10,... | collective-permute-start | bytes 294920 | tf_op jit(solution)/shard_map/ppermute | solution.py:23
  42.0 2.8 %collective-permute-start.15 = (bf16[4,32,384]{2,1,0:T(8,128)(2,1)S(1)}, bf16[4,32,384]{2,1,0:T(8,128)(2,1)S(1)}, u32[]{:S(2)}, u32[]{:S(2)}) collective-permute-start(bf16[4,32,384]{2,1,0:T(8,128)(2,1)S(1)} %collective-permute-done.11.refs_0_), channel_id=1, source_target_pairs={{0,1},{1,0},{2,3},{3,2},{4,5},{5,4},{6,7},{7,6},{8,9},{9,8},{10,11... | collective-permute-start | bytes 294920 | tf_op jit(solution)/shard_map/ppermute | solution.py:17
  42.0 2.7 %collective-permute-start.16 = (bf16[4,32,384]{2,1,0:T(8,128)(2,1)S(1)}, bf16[4,32,384]{2,1,0:T(8,128)(2,1)S(1)}, u32[]{:S(2)}, u32[]{:S(2)}) collective-permute-start(bf16[4,32,384]{2,1,0:T(8,128)(2,1)S(1)} %collective-permute-done.12.refs_1_), channel_id=1, source_target_pairs={{0,1},{1,0},{2,3},{3,2},{4,5},{5,4},{6,7},{7,6},{8,9},{9,8},{10,11... | collective-permute-start | bytes 294920 | tf_op jit(solution)/shard_map/ppermute | solution.py:17
  42.5 2.3 %collective-permute-start.17 = (bf16[4,32,384]{2,1,0:T(8,128)(2,1)S(1)}, bf16[4,32,384]{2,1,0:T(8,128)(2,1)S(1)}, u32[]{:S(2)}, u32[]{:S(2)}) collective-permute-start(bf16[4,32,384]{2,1,0:T(8,128)(2,1)S(1)} %collective-permute-done.13.refs_2_), channel_id=1, source_target_pairs={{0,1},{1,0},{2,3},{3,2},{4,5},{5,4},{6,7},{7,6},{8,9},{9,8},{10,11... | collective-permute-start | bytes 294920 | tf_op jit(solution)/shard_map/ppermute | solution.py:17
  43.4 1.6 %collective-permute-start.18 = (bf16[4,32,384]{2,1,0:T(8,128)(2,1)S(1)}, bf16[4,32,384]{2,1,0:T(8,128)(2,1)S(1)}, u32[]{:S(2)}, u32[]{:S(2)}) collective-permute-start(bf16[4,32,384]{2,1,0:T(8,128)(2,1)S(1)} %collective-permute-done.14.refs_3_), channel_id=1, source_target_pairs={{0,1},{1,0},{2,3},{3,2},{4,5},{5,4},{6,7},{7,6},{8,9},{9,8},{10,11... | collective-permute-start | bytes 294920 | tf_op jit(solution)/shard_map/ppermute | solution.py:17

commit v3 on v2

v3 whole, which is shorter than its diff:
```python
import functools

import jax
import jax.numpy as jnp
from jax import lax
from jax.experimental import pallas as pl
from jax.experimental.pallas import tpu as pltpu
from jax.sharding import PartitionSpec as P

VMEM = pl.BlockSpec(memory_space=pltpu.VMEM)
SMEM = pl.BlockSpec(memory_space=pltpu.SMEM)
HBM = pl.BlockSpec(memory_space=pltpu.HBM)
ANY = pl.BlockSpec(memory_space=pl.ANY)
PARAMS = pltpu.CompilerParams(vmem_limit_bytes=32 << 20)


def swap_rows(x):
    return lax.ppermute(x, "row", [(0, 1), (1, 0)])


def exchange(x, apart):
    tiles = lax.axis_size("tile")
    pairs = [(2 * t + r, 2 * (t ^ apart[r]) + r) for t in range(tiles) for r in apart]
    return lax.ppermute(x, ("tile", "row"), pairs)


def in_hbm(x):
    return pltpu.with_memory_space_constraint(x, pltpu.HBM)


def cost(moved, flops=0):
    return pl.CostEstimate(flops=flops, bytes_accessed=moved, transcendentals=0)


def column_copies(slots, column_ref, sens_ref, out_ref, sems):
    width = out_ref.shape[1] // slots
    copies = []
    for slot in range(slots):
        start = pl.multiple_of(column_ref[slot] * width, 128)
        copies.append(
            pltpu.make_async_copy(
                sens_ref.at[:, pl.ds(start, width)],
                out_ref.at[:, pl.ds(slot * width, width)],
                sems.at[slot],
            )
        )
        copies[-1].start()
    return copies


def find_asked(list_ref, owner, blocks, slot, ids_ref):
    first, spare = owner * blocks, ids_ref.shape[0] - 1
    for k in range(list_ref.shape[1]):
        block = list_ref[0, k] - first
        mine = (block >= 0) & (block < blocks)
        ids_ref[jnp.where(mine, slot, spare)] = block
        slot = slot + mine.astype(jnp.int32)


def plan_kernel(tiles, capacity, blocks, here_ref, list_ref, mask_ref, sens_ref, *refs):
    column_ref, live_ref, own_ids_ref, out_ref = refs[:4]
    held_list_ref, held_mask_ref, count_ref, sems = refs[4:]
    steps = tiles // 2
    slots = steps * capacity
    pairs = [(list_ref, held_list_ref), (mask_ref, held_mask_ref)]
    copies = [pltpu.make_async_copy(*pair, sems.at[slots + i]) for i, pair in enumerate(pairs)]
    for copy in copies:
        copy.start()
    for s in range(tiles):
        count_ref[s] = 0
    for copy in copies:
        copy.wait()
    tile, core = here_ref[0], here_ref[1]
    mirror = tile ^ (tiles - 2)
    seen_from = jnp.where(core == 0, tile, mirror)
    for k in range(list_ref.shape[1]):
        apart = lax.div(held_list_ref[0, k], blocks) ^ seen_from
        count = count_ref[apart]
        count_ref[apart] = count + 1
        slot = (steps - 1 - apart) * capacity + count
        slot = jnp.where(apart < steps, slot, slots)
        column_ref[slot] = k
        live_ref[slot] = held_mask_ref[0, k]
    copies = column_copies(slots, column_ref, sens_ref, out_ref, sems)
    find_asked(held_list_ref, tile, blocks, 0, own_ids_ref)
    find_asked(held_list_ref, mirror, blocks, capacity, own_ids_ref)
    for copy in copies:
        copy.wait()


def stage_kernel(slots, column_ref, sens_ref, out_ref, sems):
    for copy in column_copies(slots, column_ref, sens_ref, out_ref, sems):
        copy.wait()


def search_kernel(tiles, capacity, blocks, here_ref, own_ids_ref, *refs):
    *lists, ids_ref = refs
    steps, tile = tiles // 2, here_ref[0]
    slots = steps * capacity
    for part, owner in enumerate((tile, tile ^ (tiles - 2))):
        for turn, list_ref in enumerate(lists):
            find_asked(list_ref, owner, blocks, part * slots + turn * capacity, ids_ref)
        for c in range(capacity):
            ids_ref[part * slots + (steps - 1) * capacity + c] = own_ids_ref[part * capacity + c]


def select_kernel(capacity, here_ref, ids_ref, own_ref, mirror_ref, *refs):
    *outs, dirs_ref, sem = refs
    core = here_ref[1]

    @pl.when(core == 0)
    def _():
        pltpu.make_async_copy(own_ref, dirs_ref, sem.at[0]).start()

    @pl.when(core != 0)
    def _():
        pltpu.make_async_copy(mirror_ref, dirs_ref, sem.at[0]).start()

    pltpu.make_async_copy(own_ref, dirs_ref, sem.at[0]).wait()
    start = core * (len(outs) * capacity)
    for turn, out_ref in enumerate(outs):
        for c in range(capacity):
            out_ref[c] = dirs_ref[ids_ref[start + turn * capacity + c]]


def predict_kernel(capacity, live_ref, own_ref, other_ref, weight_ref, *refs):
    *chunks, out_ref, flat_ref = refs
    vecs, width = chunks[0].shape[1:]
    for turn, chunk_ref in enumerate(chunks):
        for c in range(capacity):
            slot = turn * capacity + c
            live = live_ref[slot].astype(jnp.float32)
            block = chunk_ref[c].astype(jnp.float32) * live
            flat_ref[:, slot * width : (slot + 1) * width] = block.astype(jnp.bfloat16)
    weight = weight_ref[...]
    for side, sens_ref in enumerate((own_ref, other_ref)):
        product = lax.dot_general(
            sens_ref[...],
            flat_ref[...],
            (((1,), (1,)), ((), ())),
            preferred_element_type=jnp.float32,
        )
        out_ref[side, :vecs] = product.T
        out_ref[side, vecs:] = jnp.broadcast_to(weight * weight, (8, weight.shape[1]))


def back_kernel(capacity, live_ref, own_ref, other_ref, mine_ref, theirs_ref, *outs):
    vecs, width = outs[0].shape[1:]
    own = mine_ref[0, vecs : vecs + 1] * (mine_ref[0, :vecs] + theirs_ref[1, :vecs])
    other = theirs_ref[0, vecs : vecs + 1] * (mine_ref[1, :vecs] + theirs_ref[0, :vecs])
    own, other = own.astype(jnp.bfloat16), other.astype(jnp.bfloat16)
    for turn, out_ref in enumerate(outs):
        span = slice(turn * capacity * width, (turn + 1) * capacity * width)
        grads = jnp.dot(own, own_ref[:, span], preferred_element_type=jnp.float32)
        grads += jnp.dot(other, other_ref[:, span], preferred_element_type=jnp.float32)
        for c in range(capacity):
            live = live_ref[turn * capacity + c].astype(jnp.float32)
            part = grads[:, c * width : (c + 1) * width] * live
            out_ref[c] = part.astype(jnp.bfloat16)


def add_chunks(capacity, places, chunks, out_ref):
    out_ref[...] = jnp.zeros_like(out_ref)
    for turn, chunk_ref in enumerate(chunks):
        for c in range(capacity):
            out_ref[places(turn * capacity + c)] += chunk_ref[c].astype(jnp.float32)


def sum_kernel(capacity, here_ref, near_ref, far_ref, *refs):
    *chunks, out_ref = refs
    core, slots = here_ref[1], len(chunks) * capacity
    add_chunks(
        capacity,
        lambda slot: jnp.where(core == 0, near_ref[slot], far_ref[slots + slot]),
        chunks,
        out_ref,
    )


def finish_kernel(capacity, here_ref, near_ref, far_ref, own_ref, *refs):
    *chunks, out_ref = refs
    core, slots = here_ref[1], len(chunks) * capacity
    add_chunks(
        capacity,
        lambda slot: jnp.where(core == 0, far_ref[slots + slot], near_ref[slot]),
        chunks,
        out_ref,
    )
    out_ref[...] += own_ref[...]


def on_device(directions, sensitivity, data_weight, foot_list, foot_mask):
    tiles = lax.axis_size("tile")
    blocks, vecs, width = directions.shape
    rows = sensitivity.shape[1]
    foot = foot_list.shape[1]
    steps, capacity = tiles // 2, foot // tiles
    slots, mirror = steps * capacity, tiles - 2
    here = jnp.stack([lax.axis_index("tile"), lax.axis_index("row")]).astype(jnp.int32)
    order = list(reversed(range(steps)))

    own_sens = in_hbm(sensitivity[0])
    other_sens = in_hbm(swap_rows(sensitivity[0]))
    mirrored = exchange(directions, {1: mirror})
    lists = [exchange(foot_list, {0: s, 1: s}) for s in order[:-1]]

    table = jax.ShapeDtypeStruct((slots + 1,), jnp.int32)
    columns = pltpu.VMEM((rows, slots * width), jnp.bfloat16)
    column, live, own_ids, own_sens = pl.pallas_call(
        functools.partial(plan_kernel, tiles, capacity, blocks),
        out_shape=[table] * 2 + [jax.ShapeDtypeStruct((2 * capacity + 1,), jnp.int32), columns],
        in_specs=[SMEM] + [HBM] * 3,
        out_specs=[SMEM] * 3 + [VMEM],
        scratch_shapes=[
            pltpu.SMEM(foot_list.shape, jnp.int32),
            pltpu.SMEM(foot_mask.shape, jnp.int32),
            pltpu.SMEM((tiles,), jnp.int32),
            pltpu.SemaphoreType.DMA((slots + 2,)),
        ],
        compiler_params=PARAMS,
        cost_estimate=cost(1),
        name="plan_columns",
    )(here, in_hbm(foot_list), in_hbm(foot_mask), own_sens)

    chunk = jax.ShapeDtypeStruct((capacity, vecs, width), jnp.bfloat16)
    ids = pl.pallas_call(
        functools.partial(search_kernel, tiles, capacity, blocks),
        out_shape=jax.ShapeDtypeStruct((2 * slots + 1,), jnp.int32),
        in_specs=[SMEM] * (1 + steps),
        out_specs=SMEM,
        compiler_params=PARAMS,
        cost_estimate=cost(1),
        name="search_lists",
    )(here, own_ids, *lists)
    chunks = pl.pallas_call(
        functools.partial(select_kernel, capacity),
        out_shape=[chunk] * steps,
        in_specs=[SMEM] * 2 + [HBM, ANY],
        out_specs=[VMEM] * steps,
        scratch_shapes=[
            pltpu.VMEM(directions.shape, jnp.bfloat16),
            pltpu.SemaphoreType.DMA((1,)),
        ],
        compiler_params=PARAMS,
        cost_estimate=cost(1),
        name="select_blocks",
    )(here, ids, in_hbm(directions), mirrored)
    fetched = [exchange(x, {0: s, 1: s}) for s, x in zip(order[:-1], chunks)] + [chunks[-1]]

    other_sens = pl.pallas_call(
        functools.partial(stage_kernel, slots),
        out_shape=columns,
        in_specs=[SMEM, HBM],
        out_specs=VMEM,
        scratch_shapes=[pltpu.SemaphoreType.DMA((slots,))],
        compiler_params=PARAMS,
        cost_estimate=cost(1),
        name="stage_columns",
    )(column, other_sens)

    partial = pl.pallas_call(
        functools.partial(predict_kernel, capacity),
        out_shape=jax.ShapeDtypeStruct((2, vecs + 8, rows), jnp.float32),
        in_specs=[SMEM] + [VMEM] * (3 + steps),
        out_specs=VMEM,
        scratch_shapes=[pltpu.VMEM((vecs, slots * width), jnp.bfloat16)],
        compiler_params=PARAMS,
        cost_estimate=cost(1),
        name="predict",
    )(live, own_sens, other_sens, data_weight, *fetched)
    other_partial = swap_rows(partial)

    grads = pl.pallas_call(
        functools.partial(back_kernel, capacity),
        out_shape=[chunk] * steps,
        in_specs=[SMEM] + [VMEM] * 4,
        out_specs=[VMEM] * steps,
        compiler_params=PARAMS,
        cost_estimate=cost(1),
        name="back_project",
    )(live, own_sens, other_sens, partial, other_partial)
    returned = [exchange(x, {0: s, 1: s ^ mirror}) for s, x in zip(order, grads)]

    far_ids = exchange(ids, {0: mirror})
    returned[0], passed_ids = lax.optimization_barrier((returned[0], swap_rows(far_ids)))
    other_returned = [swap_rows(x) for x in returned]

    total = jax.ShapeDtypeStruct((blocks, vecs, width), jnp.float32)
    own_sum = pl.pallas_call(
        functools.partial(sum_kernel, capacity),
        out_shape=total,
        in_specs=[SMEM] * 3 + [VMEM] * steps,
        out_specs=VMEM,
        compiler_params=PARAMS,
        cost_estimate=cost(1),
        name="sum_blocks",
    )(here, ids, passed_ids, *returned)
    return pl.pallas_call(
        functools.partial(finish_kernel, capacity),
        out_shape=total,
        in_specs=[SMEM] * 3 + [VMEM] * (1 + steps),
        out_specs=VMEM,
        compiler_params=PARAMS,
        cost_estimate=cost(1),
        name="finish_blocks",
    )(here, ids, far_ids, own_sum, *other_returned)


def solution(mesh):
    in_specs = (
        P(("parts", "tile"), None, None),
        P(("parts", "tile"), "row", None),
        P(("parts", "tile"), "row"),
        P(("parts", "tile"), None),
        P(("parts", "tile"), None),
    )
    out_specs = P(("parts", "tile"), None, None)
    return jax.shard_map(
        on_device, mesh=mesh, in_specs=in_specs, out_specs=out_specs, check_vma=False
    )
```

time: 46.8 us -> 44.7 us (0.955)
  waiting for transfers between devices: 11.8 us -> 7.5 us
  Pallas kernels: 14.1 us -> 16.7 us
  starting transfers between devices: 20.6 us -> 19.9 us
    ppermute x12, waiting for transfers between devices: 10.5 us -> 5.19 us  [exchange(): return lax.ppermute(x, ('tile', 'row'), pairs)]
    ppermute x7, starting transfers between devices: 5.57 us -> 2.26 us  [swap_rows(): return lax.ppermute(x, 'row', [(0, 1), (1, 0)])]
    ppermute x12, starting transfers between devices: 15 us -> 17.7 us  [exchange(): return lax.ppermute(x, ('tile', 'row'), pairs)]
    pallas_call x7 -> x8, Pallas kernels: 14.1 us -> 16.7 us  [the longest x1 4.27 us: on_device(): pl.pallas_call(functools.partial(plan_kernel, tiles, capacity, blocks), o...]
    ppermute x7, waiting for transfers between devices: 1.28 us -> 2.32 us  [swap_rows(): return lax.ppermute(x, 'row', [(0, 1), (1, 0)])]
  transfers between devices with their start and end apart: 19 -> 19, of which waited for: 8 -> 7; matrix products, arithmetic and copies ran while one was open for 0% -> 0% of each run, Pallas kernels for 18% -> 25%
where the time goes in v3:
time: 44.7 us; the launch traced here: 44.4 us
  starting transfers between devices  19.9 us (45%)
  Pallas kernels  16.7 us (37%)
  waiting for transfers between devices  7.5 us (17%)
    ppermute x12, starting transfers between devices, exchange(): return lax.ppermute(x, ('tile', 'row'), pairs)  17.7 us
    ppermute x12, waiting for transfers between devices, exchange(): return lax.ppermute(x, ('tile', 'row'), pairs)  5.19 us
    pallas_call x1, Pallas kernels, on_device(): pl.pallas_call(functools.partial(plan_kernel, tiles, capacity, blocks), o...  4.27 us
    pallas_call x1, Pallas kernels, on_device(): pl.pallas_call(functools.partial(stage_kernel, slots), out_shape=columns,...  2.65 us
    pallas_call x1, Pallas kernels, on_device(): pl.pallas_call(functools.partial(predict_kernel, capacity), out_shape=jax...  2.37 us
    ppermute x7, waiting for transfers between devices, swap_rows(): return lax.ppermute(x, 'row', [(0, 1), (1, 0)])  2.32 us
    ppermute x7, starting transfers between devices, swap_rows(): return lax.ppermute(x, 'row', [(0, 1), (1, 0)])  2.26 us
    pallas_call x1, Pallas kernels, on_device(): pl.pallas_call(functools.partial(search_kernel, tiles, capacity, blocks),...  1.77 us
  transfers between devices with their start and end apart: 19, of which 7 were waited for; matrix products, arithmetic and copies ran while one was open for 0% of the time, Pallas kernels for 25%

profile of v3, /device:TPU:0, one launch (start us, length us, event | category | flops | bytes accessed | tf_op | source)
XLA Modules:
  0.0 44.4 jit_solution(16548167592814118872)
XLA Ops:
  0.0 0.5 %collective-permute-start.4 = (bf16[256,12288]{1,0:T(8,128)(2,1)}, bf16[256,12288]{1,0:T(8,128)(2,1)}, u32[]{:S(2)}, u32[]{:S(2)}) collective-permute-start(bf16[256,12288]{1,0:T(8,128)(2,1)} %bitcast.3), channel_id=1, source_target_pairs={{0,1},{1,0},{2,3},{3,2},{4,5},{5,4},{6,7},{7,6},{8,9},{9,8},{10,11... | collective-permute-start | bytes 18874376 | tf_op jit(solution)/shard_map/ppermute | solution.py:18
  0.5 0.7 %collective-permute-start.5 = (bf16[16,32,384]{2,1,0:T(8,128)(2,1)}, bf16[16,32,384]{2,1,0:T(8,128)(2,1)S(1)}, u32[]{:S(2)}, u32[]{:S(2)}) collective-permute-start(bf16[16,32,384]{2,1,0:T(8,128)(2,1)} %own_ref.1), channel_id=1, source_target_pairs={{1,13},{3,15},{5,9},{7,11},{9,5},{11,7},{13,1},{15,3},{17,29},{19,... | collective-permute-start | bytes 1179656 | tf_op jit(solution)/shard_map/ppermute | solution.py:24
  1.1 3.6 %collective-permute-start = (s32[1,32]{1,0:T(1,128)}, s32[1,32]{1,0:T(1,128)S(1)}, u32[]{:S(2)}, u32[]{:S(2)}) collective-permute-start(s32[1,32]{1,0:T(1,128)} %list_ref.1), channel_id=1, source_target_pairs={{0,6},{1,7},{2,4},{3,5},{4,2},{5,3},{6,0},{7,1},{8,14},{9,15},{10,... | collective-permute-start | bytes 392 | tf_op jit(solution)/shard_map/ppermute | solution.py:24
  4.7 0.4 %collective-permute-start.1 = (s32[1,32]{1,0:T(1,128)}, s32[1,32]{1,0:T(1,128)S(1)}, u32[]{:S(2)}, u32[]{:S(2)}) collective-permute-start(s32[1,32]{1,0:T(1,128)} %list_ref.1), channel_id=1, source_target_pairs={{0,4},{1,5},{2,6},{3,7},{4,0},{5,1},{6,2},{7,3},{8,12},{9,13},{10,... | collective-permute-start | bytes 392 | tf_op jit(solution)/shard_map/ppermute | solution.py:24
  5.2 0.2 collective-permute-start.2
  5.5 4.3 %plan_columns.1 = (s32[17]{0:T(128)S(1)}, s32[17]{0:T(128)S(1)}, s32[9]{0:T(128)S(1)}, bf16[256,6144]{1,0:T(8,128)(2,1)S(1)}) custom-call(s32[2]{0:T(128)S(1)} %pad_add_fusion.here_ref, s32[1,32]{1,0:T(1,128)} %list_ref.1, s32[1,32]{1,0:T(1,128)} %mask_ref.1, bf16[256,12288]{1,0:T(8,128)(2,1)} %bitcast.4), custom_call_target="tpu_custom_call" | custom-call | bytes 1 | tf_op jit(solution)/shard_map/plan_columns/pallas_call | solution.py:209
  9.8 1.8 %search_lists.1.ids_ref.near_ref = s32[33]{0:T(128)S(1)} custom-call(s32[2]{0:T(128)S(1)} %pad_add_fusion.here_ref, s32[9]{0:T(128)S(1)} %get-tuple-element.19.own_ids_ref, s32[1,32]{1,0:T(1,128)S(1)} %collective-permute-done.refs_0_, s32[1,32]{1,0:T(1,128)S(1)} %collective-permute-done.1.refs_1_, s32[1,32]{1,0:T(1,128)S(1)} %collective-permute-done.2.refs_2_), custom_call_target="tpu_custom_call" | custom-call | bytes 1 | tf_op jit(solution)/shard_map/search_lists/pallas_call | solution.py:226
  11.6 1.6 %select_blocks.1 = (bf16[4,32,384]{2,1,0:T(8,128)(2,1)S(1)}, bf16[4,32,384]{2,1,0:T(8,128)(2,1)S(1)}, bf16[4,32,384]{2,1,0:T(8,128)(2,1)S(1)}, bf16[4,32,384]{2,1,0:T(8,128)(2,1)S(1)}) custom-call(s32[2]{0:T(128)S(1)} %pad_add_fusion.here_ref, s32[33]{0:T(128)S(1)} %search_lists.1.ids_ref.near_ref, bf16[16,32,384]{2,1,0:T(8,128)(2,1)} %own_ref.1, ...), custom_call_target="tpu_custom_call" | custom-call | bytes 1 | tf_op jit(solution)/shard_map/select_blocks/pallas_call | solution.py:235
  13.2 2.9 %collective-permute-start.6 = (bf16[4,32,384]{2,1,0:T(8,128)(2,1)S(1)}, bf16[4,32,384]{2,1,0:T(8,128)(2,1)S(1)}, u32[]{:S(2)}, u32[]{:S(2)}) collective-permute-start(bf16[4,32,384]{2,1,0:T(8,128)(2,1)S(1)} %get-tuple-element.23), channel_id=1, source_target_pairs={{0,6},{1,7},{2,4},{3,5},{4,2},{5,3},{6,0},{7,1},{8,14},{9,15},{10,... | collective-permute-start | bytes 294920 | tf_op jit(solution)/shard_map/ppermute | solution.py:24
  16.1 0.4 %collective-permute-start.7 = (bf16[4,32,384]{2,1,0:T(8,128)(2,1)S(1)}, bf16[4,32,384]{2,1,0:T(8,128)(2,1)S(1)}, u32[]{:S(2)}, u32[]{:S(2)}) collective-permute-start(bf16[4,32,384]{2,1,0:T(8,128)(2,1)S(1)} %get-tuple-element.24), channel_id=1, source_target_pairs={{0,4},{1,5},{2,6},{3,7},{4,0},{5,1},{6,2},{7,3},{8,12},{9,13},{10,... | collective-permute-start | bytes 294920 | tf_op jit(solution)/shard_map/ppermute | solution.py:24
  16.5 0.2 collective-permute-start.8
  16.7 2.7 %stage_columns.1.other_ref = bf16[256,6144]{1,0:T(8,128)(2,1)S(1)} custom-call(s32[17]{0:T(128)S(1)} %get-tuple-element.22.column_ref, bf16[256,12288]{1,0:T(8,128)(2,1)} %collective-permute-done.4.sens_ref), custom_call_target="tpu_custom_call" | custom-call | bytes 1 | tf_op jit(solution)/shard_map/stage_columns/pallas_call | solution.py:250
  19.4 1.5 %collective-permute-done.7.refs_1_ = bf16[4,32,384]{2,1,0:T(8,128)(2,1)S(1)} collective-permute-done((bf16[4,32,384]{2,1,0:T(8,128)(2,1)S(1)}, bf16[4,32,384]{2,1,0:T(8,128)(2,1)S(1)}, u32[]{:S(2)}, u32[]{:S(2)}) %collective-permute-start.7) | collective-permute-done | bytes 98336 | tf_op jit(solution)/shard_map/ppermute | solution.py:24
  20.9 1.4 %collective-permute-done.8.refs_2_ = bf16[4,32,384]{2,1,0:T(8,128)(2,1)S(1)} collective-permute-done((bf16[4,32,384]{2,1,0:T(8,128)(2,1)S(1)}, bf16[4,32,384]{2,1,0:T(8,128)(2,1)S(1)}, u32[]{:S(2)}, u32[]{:S(2)}) %collective-permute-start.8) | collective-permute-done | bytes 98336 | tf_op jit(solution)/shard_map/ppermute | solution.py:24
  22.3 2.4 %predict.1.mine_ref = f32[2,40,256]{2,1,0:T(8,128)S(1)} custom-call(s32[17]{0:T(128)S(1)} %get-tuple-element.20.live_ref, bf16[256,6144]{1,0:T(8,128)(2,1)S(1)} %get-tuple-element.21.own_ref, bf16[256,6144]{1,0:T(8,128)(2,1)S(1)} %stage_columns.1.other_ref, f32[1,256]{1,0:T(1,128)S(1)} %copy-done, bf16[4,32,384]{2,1,0:T(8,128)(2,1)S(1)} %collective-permute-done.6.refs_0_, ...), custom_call_target="tpu_custom_call" | custom-call | bytes 1 | tf_op jit(solution)/shard_map/predict/pallas_call | solution.py:261
  24.7 0.8 %collective-permute-start.9 = (f32[2,40,256]{2,1,0:T(8,128)S(1)}, f32[2,40,256]{2,1,0:T(8,128)S(1)}, u32[]{:S(2)}, u32[]{:S(2)}) collective-permute-start(f32[2,40,256]{2,1,0:T(8,128)S(1)} %predict.1.mine_ref), channel_id=1, source_target_pairs={{0,1},{1,0},{2,3},{3,2},{4,5},{5,4},{6,7},{7,6},{8,9},{9,8},{10,11... | collective-permute-start | bytes 245768 | tf_op jit(solution)/shard_map/ppermute | solution.py:18
  25.5 0.9 %collective-permute-done.9.theirs_ref = f32[2,40,256]{2,1,0:T(8,128)S(1)} collective-permute-done((f32[2,40,256]{2,1,0:T(8,128)S(1)}, f32[2,40,256]{2,1,0:T(8,128)S(1)}, u32[]{:S(2)}, u32[]{:S(2)}) %collective-permute-start.9) | collective-permute-done | bytes 81952 | tf_op jit(solution)/shard_map/ppermute | solution.py:18
  26.4 1.7 %back_project.1 = (bf16[4,32,384]{2,1,0:T(8,128)(2,1)S(1)}, bf16[4,32,384]{2,1,0:T(8,128)(2,1)S(1)}, bf16[4,32,384]{2,1,0:T(8,128)(2,1)S(1)}, bf16[4,32,384]{2,1,0:T(8,128)(2,1)S(1)}) custom-call(s32[17]{0:T(128)S(1)} %get-tuple-element.20.live_ref, bf16[256,6144]{1,0:T(8,128)(2,1)S(1)} %get-tuple-element.21.own_ref, ...), custom_call_target="tpu_custom_call" | custom-call | bytes 1 | tf_op jit(solution)/shard_map/back_project/pallas_call | solution.py:273
  28.1 1.6 %collective-permute-start.10 = (bf16[4,32,384]{2,1,0:T(8,128)(2,1)S(1)}, bf16[4,32,384]{2,1,0:T(8,128)(2,1)S(1)}, u32[]{:S(2)}, u32[]{:S(2)}) collective-permute-start(bf16[4,32,384]{2,1,0:T(8,128)(2,1)S(1)} %get-tuple-element.27), channel_id=1, source_target_pairs={{0,6},{1,11},{2,4},{3,9},{4,2},{5,15},{6,0},{7,13},{8,14},{9,3},{1... | collective-permute-start | bytes 294920 | tf_op jit(solution)/shard_map/ppermute | solution.py:24
  29.7 1.0 %collective-permute-start.12 = (bf16[4,32,384]{2,1,0:T(8,128)(2,1)S(1)}, bf16[4,32,384]{2,1,0:T(8,128)(2,1)S(1)}, u32[]{:S(2)}, u32[]{:S(2)}) collective-permute-start(bf16[4,32,384]{2,1,0:T(8,128)(2,1)S(1)} %get-tuple-element.30), channel_id=1, source_target_pairs={{0,4},{1,9},{2,6},{3,11},{4,0},{5,13},{6,2},{7,15},{8,12},{9,1},{1... | collective-permute-start | bytes 294920 | tf_op jit(solution)/shard_map/ppermute | solution.py:24
  30.7 1.0 %collective-permute-start.13 = (bf16[4,32,384]{2,1,0:T(8,128)(2,1)S(1)}, bf16[4,32,384]{2,1,0:T(8,128)(2,1)S(1)}, u32[]{:S(2)}, u32[]{:S(2)}) collective-permute-start(bf16[4,32,384]{2,1,0:T(8,128)(2,1)S(1)} %get-tuple-element.31), channel_id=1, source_target_pairs={{0,2},{1,15},{2,0},{3,13},{4,6},{5,11},{6,4},{7,9},{8,10},{9,7},{1... | collective-permute-start | bytes 294920 | tf_op jit(solution)/shard_map/ppermute | solution.py:24
  31.7 0.7 %collective-permute-start.14 = (bf16[4,32,384]{2,1,0:T(8,128)(2,1)S(1)}, bf16[4,32,384]{2,1,0:T(8,128)(2,1)S(1)}, u32[]{:S(2)}, u32[]{:S(2)}) collective-permute-start(bf16[4,32,384]{2,1,0:T(8,128)(2,1)S(1)} %get-tuple-element.32), channel_id=1, source_target_pairs={{0,0},{1,13},{2,2},{3,15},{4,4},{5,9},{6,6},{7,11},{8,8},{9,5},{10... | collective-permute-start | bytes 294920 | tf_op jit(solution)/shard_map/ppermute | solution.py:24
  32.4 5.0 %collective-permute-start.3 = (s32[33]{0:T(128)S(1)}, s32[33]{0:T(128)S(1)}, u32[]{:S(2)}, u32[]{:S(2)}) collective-permute-start(s32[33]{0:T(128)S(1)} %search_lists.1.ids_ref.near_ref), channel_id=1, source_target_pairs={{0,12},{2,14},{4,8},{6,10},{8,4},{10,6},{12,0},{14,2},{16,28},{18,... | collective-permute-start | bytes 404 | tf_op jit(solution)/shard_map/ppermute | solution.py:24
  37.4 2.2 %collective-permute-done.3.far_ref = s32[33]{0:T(128)S(1)} collective-permute-done((s32[33]{0:T(128)S(1)}, s32[33]{0:T(128)S(1)}, u32[]{:S(2)}, u32[]{:S(2)}) %collective-permute-start.3) | collective-permute-done | bytes 164 | tf_op jit(solution)/shard_map/ppermute | solution.py:24
  39.6 1.1 %collective-permute-done.11.far_ref = s32[33]{0:T(128)S(1)} collective-permute-done((s32[33]{0:T(128)S(1)}, s32[33]{0:T(128)S(1)}, u32[]{:S(2)}, u32[]{:S(2)}) %collective-permute-start.11) | collective-permute-done | bytes 164 | tf_op jit(solution)/shard_map/ppermute | solution.py:18
  40.7 0.2 collective-permute-start.15
  40.9 0.3 collective-permute-start.16
  41.2 0.2 collective-permute-start.17
  41.5 0.3 collective-permute-start.18
  41.8 0.7 %sum_blocks.1.own_ref = f32[16,32,384]{2,1,0:T(8,128)S(1)} custom-call(s32[2]{0:T(128)S(1)} %pad_add_fusion.here_ref, s32[33]{0:T(128)S(1)} %search_lists.1.ids_ref.near_ref, s32[33]{0:T(128)S(1)} %collective-permute-done.11.far_ref, bf16[4,32,384]{2,1,0:T(8,128)(2,1)S(1)} %collective-permute-done.10.refs_0_, ...), custom_call_target="tpu_custom_call" | custom-call | bytes 1 | tf_op jit(solution)/shard_map/sum_blocks/pallas_call | solution.py:289
  42.5 0.2 collective-permute-done.18.refs_3_
  42.8 1.7 %finish_blocks.1 = f32[16,32,384]{2,1,0:T(8,128)} custom-call(s32[2]{0:T(128)S(1)} %pad_add_fusion.here_ref, s32[33]{0:T(128)S(1)} %search_lists.1.ids_ref.near_ref, s32[33]{0:T(128)S(1)} %collective-permute-done.3.far_ref, f32[16,32,384]{2,1,0:T(8,128)S(1)} %sum_blocks.1.own_ref, bf16[4,32,384]{2,1,0:T(8,128)(2,1)S(1)} %collective-permute-done.15.refs_0_, ...), custom_call_target="tpu_custom_call" | custom-call | bytes 1 | tf_op jit(solution)/shard_map/finish_blocks/pallas_call | solution.py:298
  (17 shorter events, 0.2 us)
Async XLA Ops:
  0.0 16.7 %collective-permute-start.4 = (bf16[256,12288]{1,0:T(8,128)(2,1)}, bf16[256,12288]{1,0:T(8,128)(2,1)}, u32[]{:S(2)}, u32[]{:S(2)}) collective-permute-start(bf16[256,12288]{1,0:T(8,128)(2,1)} %bitcast.3), channel_id=1, source_target_pairs={{0,1},{1,0},{2,3},{3,2},{4,5},{5,4},{6,7},{7,6},{8,9},{9,8},{10,11... | collective-permute-start | bytes 18874376 | tf_op jit(solution)/shard_map/ppermute | solution.py:18
  0.5 11.1 %collective-permute-start.5 = (bf16[16,32,384]{2,1,0:T(8,128)(2,1)}, bf16[16,32,384]{2,1,0:T(8,128)(2,1)S(1)}, u32[]{:S(2)}, u32[]{:S(2)}) collective-permute-start(bf16[16,32,384]{2,1,0:T(8,128)(2,1)} %own_ref.1), channel_id=1, source_target_pairs={{1,13},{3,15},{5,9},{7,11},{9,5},{11,7},{13,1},{15,3},{17,29},{19,... | collective-permute-start | bytes 1179656 | tf_op jit(solution)/shard_map/ppermute | solution.py:24
  1.1 8.6 %collective-permute-start = (s32[1,32]{1,0:T(1,128)}, s32[1,32]{1,0:T(1,128)S(1)}, u32[]{:S(2)}, u32[]{:S(2)}) collective-permute-start(s32[1,32]{1,0:T(1,128)} %list_ref.1), channel_id=1, source_target_pairs={{0,6},{1,7},{2,4},{3,5},{4,2},{5,3},{6,0},{7,1},{8,14},{9,15},{10,... | collective-permute-start | bytes 392 | tf_op jit(solution)/shard_map/ppermute | solution.py:24
  4.7 5.0 %collective-permute-start.1 = (s32[1,32]{1,0:T(1,128)}, s32[1,32]{1,0:T(1,128)S(1)}, u32[]{:S(2)}, u32[]{:S(2)}) collective-permute-start(s32[1,32]{1,0:T(1,128)} %list_ref.1), channel_id=1, source_target_pairs={{0,4},{1,5},{2,6},{3,7},{4,0},{5,1},{6,2},{7,3},{8,12},{9,13},{10,... | collective-permute-start | bytes 392 | tf_op jit(solution)/shard_map/ppermute | solution.py:24
  5.2 4.6 %collective-permute-start.2 = (s32[1,32]{1,0:T(1,128)}, s32[1,32]{1,0:T(1,128)S(1)}, u32[]{:S(2)}, u32[]{:S(2)}) collective-permute-start(s32[1,32]{1,0:T(1,128)} %list_ref.1), channel_id=1, source_target_pairs={{0,2},{1,3},{2,0},{3,1},{4,6},{5,7},{6,4},{7,5},{8,10},{9,11},{10,... | collective-permute-start | bytes 392 | tf_op jit(solution)/shard_map/ppermute | solution.py:24
  9.7 12.6 %copy-start = (f32[1,256]{1,0:T(1,128)S(1)}, f32[1,256]{1,0:T(1,128)}, u32[]{:S(2)}) copy-start(f32[1,256]{1,0:T(1,128)} %weight_ref.1) | copy-start | bytes 3076
  13.2 6.2 %collective-permute-start.6 = (bf16[4,32,384]{2,1,0:T(8,128)(2,1)S(1)}, bf16[4,32,384]{2,1,0:T(8,128)(2,1)S(1)}, u32[]{:S(2)}, u32[]{:S(2)}) collective-permute-start(bf16[4,32,384]{2,1,0:T(8,128)(2,1)S(1)} %get-tuple-element.23), channel_id=1, source_target_pairs={{0,6},{1,7},{2,4},{3,5},{4,2},{5,3},{6,0},{7,1},{8,14},{9,15},{10,... | collective-permute-start | bytes 294920 | tf_op jit(solution)/shard_map/ppermute | solution.py:24
  16.1 4.8 %collective-permute-start.7 = (bf16[4,32,384]{2,1,0:T(8,128)(2,1)S(1)}, bf16[4,32,384]{2,1,0:T(8,128)(2,1)S(1)}, u32[]{:S(2)}, u32[]{:S(2)}) collective-permute-start(bf16[4,32,384]{2,1,0:T(8,128)(2,1)S(1)} %get-tuple-element.24), channel_id=1, source_target_pairs={{0,4},{1,5},{2,6},{3,7},{4,0},{5,1},{6,2},{7,3},{8,12},{9,13},{10,... | collective-permute-start | bytes 294920 | tf_op jit(solution)/shard_map/ppermute | solution.py:24
  16.5 5.8 %collective-permute-start.8 = (bf16[4,32,384]{2,1,0:T(8,128)(2,1)S(1)}, bf16[4,32,384]{2,1,0:T(8,128)(2,1)S(1)}, u32[]{:S(2)}, u32[]{:S(2)}) collective-permute-start(bf16[4,32,384]{2,1,0:T(8,128)(2,1)S(1)} %get-tuple-element.25), channel_id=1, source_target_pairs={{0,2},{1,3},{2,0},{3,1},{4,6},{5,7},{6,4},{7,5},{8,10},{9,11},{10,... | collective-permute-start | bytes 294920 | tf_op jit(solution)/shard_map/ppermute | solution.py:24
  24.7 1.7 %collective-permute-start.9 = (f32[2,40,256]{2,1,0:T(8,128)S(1)}, f32[2,40,256]{2,1,0:T(8,128)S(1)}, u32[]{:S(2)}, u32[]{:S(2)}) collective-permute-start(f32[2,40,256]{2,1,0:T(8,128)S(1)} %predict.1.mine_ref), channel_id=1, source_target_pairs={{0,1},{1,0},{2,3},{3,2},{4,5},{5,4},{6,7},{7,6},{8,9},{9,8},{10,11... | collective-permute-start | bytes 245768 | tf_op jit(solution)/shard_map/ppermute | solution.py:18
  28.1 12.6 %collective-permute-start.10 = (bf16[4,32,384]{2,1,0:T(8,128)(2,1)S(1)}, bf16[4,32,384]{2,1,0:T(8,128)(2,1)S(1)}, u32[]{:S(2)}, u32[]{:S(2)}) collective-permute-start(bf16[4,32,384]{2,1,0:T(8,128)(2,1)S(1)} %get-tuple-element.27), channel_id=1, source_target_pairs={{0,6},{1,11},{2,4},{3,9},{4,2},{5,15},{6,0},{7,13},{8,14},{9,3},{1... | collective-permute-start | bytes 294920 | tf_op jit(solution)/shard_map/ppermute | solution.py:24
  29.7 11.2 %collective-permute-start.12 = (bf16[4,32,384]{2,1,0:T(8,128)(2,1)S(1)}, bf16[4,32,384]{2,1,0:T(8,128)(2,1)S(1)}, u32[]{:S(2)}, u32[]{:S(2)}) collective-permute-start(bf16[4,32,384]{2,1,0:T(8,128)(2,1)S(1)} %get-tuple-element.30), channel_id=1, source_target_pairs={{0,4},{1,9},{2,6},{3,11},{4,0},{5,13},{6,2},{7,15},{8,12},{9,1},{1... | collective-permute-start | bytes 294920 | tf_op jit(solution)/shard_map/ppermute | solution.py:24
  30.7 10.6 %collective-permute-start.13 = (bf16[4,32,384]{2,1,0:T(8,128)(2,1)S(1)}, bf16[4,32,384]{2,1,0:T(8,128)(2,1)S(1)}, u32[]{:S(2)}, u32[]{:S(2)}) collective-permute-start(bf16[4,32,384]{2,1,0:T(8,128)(2,1)S(1)} %get-tuple-element.31), channel_id=1, source_target_pairs={{0,2},{1,15},{2,0},{3,13},{4,6},{5,11},{6,4},{7,9},{8,10},{9,7},{1... | collective-permute-start | bytes 294920 | tf_op jit(solution)/shard_map/ppermute | solution.py:24
  31.7 9.8 %collective-permute-start.14 = (bf16[4,32,384]{2,1,0:T(8,128)(2,1)S(1)}, bf16[4,32,384]{2,1,0:T(8,128)(2,1)S(1)}, u32[]{:S(2)}, u32[]{:S(2)}) collective-permute-start(bf16[4,32,384]{2,1,0:T(8,128)(2,1)S(1)} %get-tuple-element.32), channel_id=1, source_target_pairs={{0,0},{1,13},{2,2},{3,15},{4,4},{5,9},{6,6},{7,11},{8,8},{9,5},{10... | collective-permute-start | bytes 294920 | tf_op jit(solution)/shard_map/ppermute | solution.py:24
  32.4 7.2 %collective-permute-start.3 = (s32[33]{0:T(128)S(1)}, s32[33]{0:T(128)S(1)}, u32[]{:S(2)}, u32[]{:S(2)}) collective-permute-start(s32[33]{0:T(128)S(1)} %search_lists.1.ids_ref.near_ref), channel_id=1, source_target_pairs={{0,12},{2,14},{4,8},{6,10},{8,4},{10,6},{12,0},{14,2},{16,28},{18,... | collective-permute-start | bytes 404 | tf_op jit(solution)/shard_map/ppermute | solution.py:24
  39.6 1.1 %collective-permute-start.11 = (s32[33]{0:T(128)S(1)}, s32[33]{0:T(128)S(1)}, u32[]{:S(2)}, u32[]{:S(2)}) collective-permute-start(s32[33]{0:T(128)S(1)} %collective-permute-done.3.far_ref), channel_id=1, source_target_pairs={{0,1},{1,0},{2,3},{3,2},{4,5},{5,4},{6,7},{7,6},{8,9},{9,8},{10,11... | collective-permute-start | bytes 404 | tf_op jit(solution)/shard_map/ppermute | solution.py:18
  40.7 1.7 %collective-permute-start.15 = (bf16[4,32,384]{2,1,0:T(8,128)(2,1)S(1)}, bf16[4,32,384]{2,1,0:T(8,128)(2,1)S(1)}, u32[]{:S(2)}, u32[]{:S(2)}) collective-permute-start(bf16[4,32,384]{2,1,0:T(8,128)(2,1)S(1)} %collective-permute-done.10.refs_0_), channel_id=1, source_target_pairs={{0,1},{1,0},{2,3},{3,2},{4,5},{5,4},{6,7},{7,6},{8,9},{9,8},{10,11... | collective-permute-start | bytes 294920 | tf_op jit(solution)/shard_map/ppermute | solution.py:18
  40.9 1.5 %collective-permute-start.16 = (bf16[4,32,384]{2,1,0:T(8,128)(2,1)S(1)}, bf16[4,32,384]{2,1,0:T(8,128)(2,1)S(1)}, u32[]{:S(2)}, u32[]{:S(2)}) collective-permute-start(bf16[4,32,384]{2,1,0:T(8,128)(2,1)S(1)} %collective-permute-done.12.refs_1_), channel_id=1, source_target_pairs={{0,1},{1,0},{2,3},{3,2},{4,5},{5,4},{6,7},{7,6},{8,9},{9,8},{10,11... | collective-permute-start | bytes 294920 | tf_op jit(solution)/shard_map/ppermute | solution.py:18
  41.2 1.3 %collective-permute-start.17 = (bf16[4,32,384]{2,1,0:T(8,128)(2,1)S(1)}, bf16[4,32,384]{2,1,0:T(8,128)(2,1)S(1)}, u32[]{:S(2)}, u32[]{:S(2)}) collective-permute-start(bf16[4,32,384]{2,1,0:T(8,128)(2,1)S(1)} %collective-permute-done.13.refs_2_), channel_id=1, source_target_pairs={{0,1},{1,0},{2,3},{3,2},{4,5},{5,4},{6,7},{7,6},{8,9},{9,8},{10,11... | collective-permute-start | bytes 294920 | tf_op jit(solution)/shard_map/ppermute | solution.py:18
  41.5 1.3 %collective-permute-start.18 = (bf16[4,32,384]{2,1,0:T(8,128)(2,1)S(1)}, bf16[4,32,384]{2,1,0:T(8,128)(2,1)S(1)}, u32[]{:S(2)}, u32[]{:S(2)}) collective-permute-start(bf16[4,32,384]{2,1,0:T(8,128)(2,1)S(1)} %collective-permute-done.14.refs_3_), channel_id=1, source_target_pairs={{0,1},{1,0},{2,3},{3,2},{4,5},{5,4},{6,7},{7,6},{8,9},{9,8},{10,11... | collective-permute-start | bytes 294920 | tf_op jit(solution)/shard_map/ppermute | solution.py:18

commit v4 on v3

--- a/solution.py
+++ b/solution.py
@@ -159,17 +159,18 @@
             out_ref[c] = part.astype(jnp.bfloat16)
 
 
-def add_chunks(capacity, places, chunks, out_ref):
+def add_chunks(turns, capacity, places, chunks, out_ref):
     out_ref[...] = jnp.zeros_like(out_ref)
-    for turn, chunk_ref in enumerate(chunks):
+    for turn, chunk_ref in zip(turns, chunks):
         for c in range(capacity):
             out_ref[places(turn * capacity + c)] += chunk_ref[c].astype(jnp.float32)
 
 
-def sum_kernel(capacity, here_ref, near_ref, far_ref, *refs):
+def sum_kernel(turns, capacity, here_ref, near_ref, far_ref, *refs):
     *chunks, out_ref = refs
     core, slots = here_ref[1], len(chunks) * capacity
     add_chunks(
+        turns,
         capacity,
         lambda slot: jnp.where(core == 0, near_ref[slot], far_ref[slots + slot]),
         chunks,
@@ -177,16 +178,26 @@
     )
 
 
-def finish_kernel(capacity, here_ref, near_ref, far_ref, own_ref, *refs):
-    *chunks, out_ref = refs
+def finish_kernel(turns, capacity, here_ref, near_ref, far_ref, own_ref, *refs):
+    *chunks, out_ref, total_ref, sems = refs
     core, slots = here_ref[1], len(chunks) * capacity
     add_chunks(
+        turns,
         capacity,
         lambda slot: jnp.where(core == 0, far_ref[slots + slot], near_ref[slot]),
         chunks,
-        out_ref,
+        total_ref,
     )
-    out_ref[...] += own_ref[...]
+    parts = sems.shape[0]
+    size = out_ref.shape[0] // parts
+    copies = []
+    for i in range(parts):
+        span = pl.ds(i * size, size)
+        total_ref[span] += own_ref[span]
+        copies.append(pltpu.make_async_copy(total_ref.at[span], out_ref.at[span], sems.at[i]))
+        copies[-1].start()
+    for copy in copies:
+        copy.wait()
 
 
 def on_device(directions, sensitivity, data_weight, foot_list, foot_mask):
@@ -258,6 +269,7 @@
         name="stage_columns",
     )(column, other_sens)
 
+    far_ids = exchange(ids, {0: mirror, 1: mirror})
     partial = pl.pallas_call(
         functools.partial(predict_kernel, capacity),
         out_shape=jax.ShapeDtypeStruct((2, vecs + 8, rows), jnp.float32),
@@ -268,6 +280,7 @@
         cost_estimate=cost(1),
         name="predict",
     )(live, own_sens, other_sens, data_weight, *fetched)
+    partial, far_ids = lax.optimization_barrier((partial, far_ids))
     other_partial = swap_rows(partial)
 
     grads = pl.pallas_call(
@@ -279,27 +292,30 @@
         cost_estimate=cost(1),
         name="back_project",
     )(live, own_sens, other_sens, partial, other_partial)
-    returned = [exchange(x, {0: s, 1: s ^ mirror}) for s, x in zip(order, grads)]
-
-    far_ids = exchange(ids, {0: mirror})
-    returned[0], passed_ids = lax.optimization_barrier((returned[0], swap_rows(far_ids)))
+    turns = list(range(0, steps, 2)) + list(range(1, steps, 2))
+    returned = [exchange(grads[i], {0: order[i], 1: order[i] ^ mirror}) for i in turns]
+
     other_returned = [swap_rows(x) for x in returned]
 
     total = jax.ShapeDtypeStruct((blocks, vecs, width), jnp.float32)
     own_sum = pl.pallas_call(
-        functools.partial(sum_kernel, capacity),
+        functools.partial(sum_kernel, turns, capacity),
         out_shape=total,
         in_specs=[SMEM] * 3 + [VMEM] * steps,
         out_specs=VMEM,
         compiler_params=PARAMS,
         cost_estimate=cost(1),
         name="sum_blocks",
-    )(here, ids, passed_ids, *returned)
+    )(here, ids, far_ids, *returned)
     return pl.pallas_call(
-        functools.partial(finish_kernel, capacity),
+        functools.partial(finish_kernel, turns, capacity),
         out_shape=total,
         in_specs=[SMEM] * 3 + [VMEM] * (1 + steps),
-        out_specs=VMEM,
+        out_specs=HBM,
+        scratch_shapes=[
+            pltpu.VMEM((blocks, vecs, width), jnp.float32),
+            pltpu.SemaphoreType.DMA((4,)),
+        ],
         compiler_params=PARAMS,
         cost_estimate=cost(1),
         name="finish_blocks",

time: 44.7 us -> 43.6 us (0.975)
  waiting for transfers between devices: 7.5 us -> 4.99 us
  starting transfers between devices: 19.9 us -> 21.4 us
    ppermute x7 -> x6, starting transfers between devices: 2.26 us -> 4.86 us  [swap_rows(): return lax.ppermute(x, 'row', [(0, 1), (1, 0)])]
    ppermute x12, waiting for transfers between devices: 5.19 us -> 3.51 us  [exchange(): return lax.ppermute(x, ('tile', 'row'), pairs)]
    ppermute x12, starting transfers between devices: 17.7 us -> 16.6 us  [exchange(): return lax.ppermute(x, ('tile', 'row'), pairs)]
    ppermute x7 -> x6, waiting for transfers between devices: 2.32 us -> 1.48 us  [swap_rows(): return lax.ppermute(x, 'row', [(0, 1), (1, 0)])]
  transfers between devices with their start and end apart: 19 -> 18, of which waited for: 7 -> 5; matrix products, arithmetic and copies ran while one was open for 0% -> 0% of each run, Pallas kernels for 25% -> 31%
where the time goes in v4:
time: 43.6 us; the launch traced here: 43.4 us
  starting transfers between devices  21.4 us (49%)
  Pallas kernels  16.7 us (38%)
  waiting for transfers between devices  4.99 us (11%)
    ppermute x12, starting transfers between devices, exchange(): return lax.ppermute(x, ('tile', 'row'), pairs)  16.6 us
    ppermute x6, starting transfers between devices, swap_rows(): return lax.ppermute(x, 'row', [(0, 1), (1, 0)])  4.86 us
    pallas_call x1, Pallas kernels, on_device(): pl.pallas_call(functools.partial(plan_kernel, tiles, capacity, blocks), o...  4.27 us
    ppermute x12, waiting for transfers between devices, exchange(): return lax.ppermute(x, ('tile', 'row'), pairs)  3.51 us
    pallas_call x1, Pallas kernels, on_device(): pl.pallas_call(functools.partial(stage_kernel, slots), out_shape=columns,...  2.65 us
    pallas_call x1, Pallas kernels, on_device(): pl.pallas_call(functools.partial(predict_kernel, capacity), out_shape=jax...  2.39 us
    pallas_call x1, Pallas kernels, on_device(): pl.pallas_call(functools.partial(search_kernel, tiles, capacity, blocks),...  1.77 us
    pallas_call x1, Pallas kernels, on_device(): pl.pallas_call(functools.partial(back_kernel, capacity), out_shape=[chunk...  1.72 us
  transfers between devices with their start and end apart: 18, of which 5 were waited for; matrix products, arithmetic and copies ran while one was open for 0% of the time, Pallas kernels for 31%

profile of v4, /device:TPU:0, one launch (start us, length us, event | category | flops | bytes accessed | tf_op | source)
XLA Modules:
  0.0 43.4 jit_solution(15550930492380938853)
XLA Ops:
  0.0 0.5 %collective-permute-start.3 = (bf16[256,12288]{1,0:T(8,128)(2,1)}, bf16[256,12288]{1,0:T(8,128)(2,1)}, u32[]{:S(2)}, u32[]{:S(2)}) collective-permute-start(bf16[256,12288]{1,0:T(8,128)(2,1)} %bitcast.3), channel_id=1, source_target_pairs={{0,1},{1,0},{2,3},{3,2},{4,5},{5,4},{6,7},{7,6},{8,9},{9,8},{10,11... | collective-permute-start | bytes 18874376 | tf_op jit(solution)/shard_map/ppermute | solution.py:18
  0.5 0.7 %collective-permute-start.4 = (bf16[16,32,384]{2,1,0:T(8,128)(2,1)}, bf16[16,32,384]{2,1,0:T(8,128)(2,1)S(1)}, u32[]{:S(2)}, u32[]{:S(2)}) collective-permute-start(bf16[16,32,384]{2,1,0:T(8,128)(2,1)} %own_ref.1), channel_id=1, source_target_pairs={{1,13},{3,15},{5,9},{7,11},{9,5},{11,7},{13,1},{15,3},{17,29},{19,... | collective-permute-start | bytes 1179656 | tf_op jit(solution)/shard_map/ppermute | solution.py:24
  1.1 3.6 %collective-permute-start = (s32[1,32]{1,0:T(1,128)}, s32[1,32]{1,0:T(1,128)S(1)}, u32[]{:S(2)}, u32[]{:S(2)}) collective-permute-start(s32[1,32]{1,0:T(1,128)} %list_ref.1), channel_id=1, source_target_pairs={{0,6},{1,7},{2,4},{3,5},{4,2},{5,3},{6,0},{7,1},{8,14},{9,15},{10,... | collective-permute-start | bytes 392 | tf_op jit(solution)/shard_map/ppermute | solution.py:24
  4.7 0.4 %collective-permute-start.1 = (s32[1,32]{1,0:T(1,128)}, s32[1,32]{1,0:T(1,128)S(1)}, u32[]{:S(2)}, u32[]{:S(2)}) collective-permute-start(s32[1,32]{1,0:T(1,128)} %list_ref.1), channel_id=1, source_target_pairs={{0,4},{1,5},{2,6},{3,7},{4,0},{5,1},{6,2},{7,3},{8,12},{9,13},{10,... | collective-permute-start | bytes 392 | tf_op jit(solution)/shard_map/ppermute | solution.py:24
  5.2 0.2 collective-permute-start.2
  5.4 0.1 pad_add_fusion.here_ref
  5.5 4.3 %plan_columns.1 = (s32[17]{0:T(128)S(1)}, s32[17]{0:T(128)S(1)}, s32[9]{0:T(128)S(1)}, bf16[256,6144]{1,0:T(8,128)(2,1)S(1)}) custom-call(s32[2]{0:T(128)S(1)} %pad_add_fusion.here_ref, s32[1,32]{1,0:T(1,128)} %list_ref.1, s32[1,32]{1,0:T(1,128)} %mask_ref.1, bf16[256,12288]{1,0:T(8,128)(2,1)} %bitcast.4), custom_call_target="tpu_custom_call" | custom-call | bytes 1 | tf_op jit(solution)/shard_map/plan_columns/pallas_call | solution.py:220
  9.7 0.0 copy-start
  9.8 1.8 %search_lists.1.ids_ref.near_ref = s32[33]{0:T(128)S(1)} custom-call(s32[2]{0:T(128)S(1)} %pad_add_fusion.here_ref, s32[9]{0:T(128)S(1)} %get-tuple-element.19.own_ids_ref, s32[1,32]{1,0:T(1,128)S(1)} %collective-permute-done.refs_0_, s32[1,32]{1,0:T(1,128)S(1)} %collective-permute-done.1.refs_1_, s32[1,32]{1,0:T(1,128)S(1)} %collective-permute-done.2.refs_2_), custom_call_target="tpu_custom_call" | custom-call | bytes 1 | tf_op jit(solution)/shard_map/search_lists/pallas_call | solution.py:237
  11.6 1.6 %select_blocks.1 = (bf16[4,32,384]{2,1,0:T(8,128)(2,1)S(1)}, bf16[4,32,384]{2,1,0:T(8,128)(2,1)S(1)}, bf16[4,32,384]{2,1,0:T(8,128)(2,1)S(1)}, bf16[4,32,384]{2,1,0:T(8,128)(2,1)S(1)}) custom-call(s32[2]{0:T(128)S(1)} %pad_add_fusion.here_ref, s32[33]{0:T(128)S(1)} %search_lists.1.ids_ref.near_ref, bf16[16,32,384]{2,1,0:T(8,128)(2,1)} %own_ref.1, ...), custom_call_target="tpu_custom_call" | custom-call | bytes 1 | tf_op jit(solution)/shard_map/select_blocks/pallas_call | solution.py:246
  13.2 2.9 %collective-permute-start.5 = (bf16[4,32,384]{2,1,0:T(8,128)(2,1)S(1)}, bf16[4,32,384]{2,1,0:T(8,128)(2,1)S(1)}, u32[]{:S(2)}, u32[]{:S(2)}) collective-permute-start(bf16[4,32,384]{2,1,0:T(8,128)(2,1)S(1)} %get-tuple-element.23), channel_id=1, source_target_pairs={{0,6},{1,7},{2,4},{3,5},{4,2},{5,3},{6,0},{7,1},{8,14},{9,15},{10,... | collective-permute-start | bytes 294920 | tf_op jit(solution)/shard_map/ppermute | solution.py:24
  16.1 0.4 %collective-permute-start.6 = (bf16[4,32,384]{2,1,0:T(8,128)(2,1)S(1)}, bf16[4,32,384]{2,1,0:T(8,128)(2,1)S(1)}, u32[]{:S(2)}, u32[]{:S(2)}) collective-permute-start(bf16[4,32,384]{2,1,0:T(8,128)(2,1)S(1)} %get-tuple-element.24), channel_id=1, source_target_pairs={{0,4},{1,5},{2,6},{3,7},{4,0},{5,1},{6,2},{7,3},{8,12},{9,13},{10,... | collective-permute-start | bytes 294920 | tf_op jit(solution)/shard_map/ppermute | solution.py:24
  16.5 0.2 collective-permute-start.7
  16.7 3.9 %collective-permute-start.8 = (s32[33]{0:T(128)S(1)}, s32[33]{0:T(128)S(1)}, u32[]{:S(2)}, u32[]{:S(2)}) collective-permute-start(s32[33]{0:T(128)S(1)} %search_lists.1.ids_ref.near_ref), channel_id=1, source_target_pairs={{0,12},{1,13},{2,14},{3,15},{4,8},{5,9},{6,10},{7,11},{8,4},{9,5},... | collective-permute-start | bytes 404 | tf_op jit(solution)/shard_map/ppermute | solution.py:24
  20.6 2.7 %stage_columns.1.other_ref = bf16[256,6144]{1,0:T(8,128)(2,1)S(1)} custom-call(s32[17]{0:T(128)S(1)} %get-tuple-element.22.column_ref, bf16[256,12288]{1,0:T(8,128)(2,1)} %collective-permute-done.3.sens_ref), custom_call_target="tpu_custom_call" | custom-call | bytes 1 | tf_op jit(solution)/shard_map/stage_columns/pallas_call | solution.py:261
  23.3 2.4 %predict.1.mine_ref = f32[2,40,256]{2,1,0:T(8,128)S(1)} custom-call(s32[17]{0:T(128)S(1)} %get-tuple-element.20.live_ref, bf16[256,6144]{1,0:T(8,128)(2,1)S(1)} %get-tuple-element.21.own_ref, bf16[256,6144]{1,0:T(8,128)(2,1)S(1)} %stage_columns.1.other_ref, f32[1,256]{1,0:T(1,128)S(1)} %copy-done, bf16[4,32,384]{2,1,0:T(8,128)(2,1)S(1)} %collective-permute-done.5.refs_0_, ...), custom_call_target="tpu_custom_call" | custom-call | bytes 1 | tf_op jit(solution)/shard_map/predict/pallas_call | solution.py:273
  25.7 0.1 collective-permute-start.9
  25.8 1.3 %collective-permute-done.9.theirs_ref = f32[2,40,256]{2,1,0:T(8,128)S(1)} collective-permute-done((f32[2,40,256]{2,1,0:T(8,128)S(1)}, f32[2,40,256]{2,1,0:T(8,128)S(1)}, u32[]{:S(2)}, u32[]{:S(2)}) %collective-permute-start.9) | collective-permute-done | bytes 81952 | tf_op jit(solution)/shard_map/ppermute | solution.py:18
  27.1 1.7 %back_project.1 = (bf16[4,32,384]{2,1,0:T(8,128)(2,1)S(1)}, bf16[4,32,384]{2,1,0:T(8,128)(2,1)S(1)}, bf16[4,32,384]{2,1,0:T(8,128)(2,1)S(1)}, bf16[4,32,384]{2,1,0:T(8,128)(2,1)S(1)}) custom-call(s32[17]{0:T(128)S(1)} %get-tuple-element.20.live_ref, bf16[256,6144]{1,0:T(8,128)(2,1)S(1)} %get-tuple-element.21.own_ref, ...), custom_call_target="tpu_custom_call" | custom-call | bytes 1 | tf_op jit(solution)/shard_map/back_project/pallas_call | solution.py:286
  28.8 1.3 %collective-permute-start.10 = (bf16[4,32,384]{2,1,0:T(8,128)(2,1)S(1)}, bf16[4,32,384]{2,1,0:T(8,128)(2,1)S(1)}, u32[]{:S(2)}, u32[]{:S(2)}) collective-permute-start(bf16[4,32,384]{2,1,0:T(8,128)(2,1)S(1)} %get-tuple-element.29), channel_id=1, source_target_pairs={{0,6},{1,11},{2,4},{3,9},{4,2},{5,15},{6,0},{7,13},{8,14},{9,3},{1... | collective-permute-start | bytes 294920 | tf_op jit(solution)/shard_map/ppermute | solution.py:24
  30.1 1.4 %collective-permute-start.11 = (bf16[4,32,384]{2,1,0:T(8,128)(2,1)S(1)}, bf16[4,32,384]{2,1,0:T(8,128)(2,1)S(1)}, u32[]{:S(2)}, u32[]{:S(2)}) collective-permute-start(bf16[4,32,384]{2,1,0:T(8,128)(2,1)S(1)} %get-tuple-element.30), channel_id=1, source_target_pairs={{0,2},{1,15},{2,0},{3,13},{4,6},{5,11},{6,4},{7,9},{8,10},{9,7},{1... | collective-permute-start | bytes 294920 | tf_op jit(solution)/shard_map/ppermute | solution.py:24
  31.5 0.8 %collective-permute-start.12 = (bf16[4,32,384]{2,1,0:T(8,128)(2,1)S(1)}, bf16[4,32,384]{2,1,0:T(8,128)(2,1)S(1)}, u32[]{:S(2)}, u32[]{:S(2)}) collective-permute-start(bf16[4,32,384]{2,1,0:T(8,128)(2,1)S(1)} %get-tuple-element.31), channel_id=1, source_target_pairs={{0,4},{1,9},{2,6},{3,11},{4,0},{5,13},{6,2},{7,15},{8,12},{9,1},{1... | collective-permute-start | bytes 294920 | tf_op jit(solution)/shard_map/ppermute | solution.py:24
  32.4 0.7 %collective-permute-start.13 = (bf16[4,32,384]{2,1,0:T(8,128)(2,1)S(1)}, bf16[4,32,384]{2,1,0:T(8,128)(2,1)S(1)}, u32[]{:S(2)}, u32[]{:S(2)}) collective-permute-start(bf16[4,32,384]{2,1,0:T(8,128)(2,1)S(1)} %get-tuple-element.32), channel_id=1, source_target_pairs={{0,0},{1,13},{2,2},{3,15},{4,4},{5,9},{6,6},{7,11},{8,8},{9,5},{10... | collective-permute-start | bytes 294920 | tf_op jit(solution)/shard_map/ppermute | solution.py:24
  33.0 2.5 %collective-permute-done.10.refs_0_ = bf16[4,32,384]{2,1,0:T(8,128)(2,1)S(1)} collective-permute-done((bf16[4,32,384]{2,1,0:T(8,128)(2,1)S(1)}, bf16[4,32,384]{2,1,0:T(8,128)(2,1)S(1)}, u32[]{:S(2)}, u32[]{:S(2)}) %collective-permute-start.10) | collective-permute-done | bytes 98336 | tf_op jit(solution)/shard_map/ppermute | solution.py:24
  35.5 1.1 %collective-permute-start.14 = (bf16[4,32,384]{2,1,0:T(8,128)(2,1)S(1)}, bf16[4,32,384]{2,1,0:T(8,128)(2,1)S(1)}, u32[]{:S(2)}, u32[]{:S(2)}) collective-permute-start(bf16[4,32,384]{2,1,0:T(8,128)(2,1)S(1)} %collective-permute-done.10.refs_0_), channel_id=1, source_target_pairs={{0,1},{1,0},{2,3},{3,2},{4,5},{5,4},{6,7},{7,6},{8,9},{9,8},{10,11... | collective-permute-start | bytes 294920 | tf_op jit(solution)/shard_map/ppermute | solution.py:18
  36.6 0.9 %collective-permute-done.11.refs_1_ = bf16[4,32,384]{2,1,0:T(8,128)(2,1)S(1)} collective-permute-done((bf16[4,32,384]{2,1,0:T(8,128)(2,1)S(1)}, bf16[4,32,384]{2,1,0:T(8,128)(2,1)S(1)}, u32[]{:S(2)}, u32[]{:S(2)}) %collective-permute-start.11) | collective-permute-done | bytes 98336 | tf_op jit(solution)/shard_map/ppermute | solution.py:24
  37.5 0.1 collective-permute-done.12.refs_2_
  37.6 1.9 %collective-permute-start.16 = (bf16[4,32,384]{2,1,0:T(8,128)(2,1)S(1)}, bf16[4,32,384]{2,1,0:T(8,128)(2,1)S(1)}, u32[]{:S(2)}, u32[]{:S(2)}) collective-permute-start(bf16[4,32,384]{2,1,0:T(8,128)(2,1)S(1)} %collective-permute-done.12.refs_2_), channel_id=1, source_target_pairs={{0,1},{1,0},{2,3},{3,2},{4,5},{5,4},{6,7},{7,6},{8,9},{9,8},{10,11... | collective-permute-start | bytes 294920 | tf_op jit(solution)/shard_map/ppermute | solution.py:18
  39.5 1.3 %collective-permute-start.17 = (bf16[4,32,384]{2,1,0:T(8,128)(2,1)S(1)}, bf16[4,32,384]{2,1,0:T(8,128)(2,1)S(1)}, u32[]{:S(2)}, u32[]{:S(2)}) collective-permute-start(bf16[4,32,384]{2,1,0:T(8,128)(2,1)S(1)} %collective-permute-done.13.refs_3_), channel_id=1, source_target_pairs={{0,1},{1,0},{2,3},{3,2},{4,5},{5,4},{6,7},{7,6},{8,9},{9,8},{10,11... | collective-permute-start | bytes 294920 | tf_op jit(solution)/shard_map/ppermute | solution.py:18
  40.8 0.7 %sum_blocks.1.own_ref = f32[16,32,384]{2,1,0:T(8,128)S(1)} custom-call(s32[2]{0:T(128)S(1)} %pad_add_fusion.here_ref, s32[33]{0:T(128)S(1)} %search_lists.1.ids_ref.near_ref, s32[33]{0:T(128)S(1)} %collective-permute-done.8.far_ref, bf16[4,32,384]{2,1,0:T(8,128)(2,1)S(1)} %collective-permute-done.10.refs_0_, ...), custom_call_target="tpu_custom_call" | custom-call | bytes 1 | tf_op jit(solution)/shard_map/sum_blocks/pallas_call | solution.py:301
  41.6 0.2 collective-permute-done.17.refs_3_
  41.8 1.6 %finish_blocks.1 = f32[16,32,384]{2,1,0:T(8,128)} custom-call(s32[2]{0:T(128)S(1)} %pad_add_fusion.here_ref, s32[33]{0:T(128)S(1)} %search_lists.1.ids_ref.near_ref, s32[33]{0:T(128)S(1)} %collective-permute-done.8.far_ref, f32[16,32,384]{2,1,0:T(8,128)S(1)} %sum_blocks.1.own_ref, bf16[4,32,384]{2,1,0:T(8,128)(2,1)S(1)} %collective-permute-done.14.refs_0_, ...), custom_call_target="tpu_custom_call" | custom-call | bytes 1 | tf_op jit(solution)/shard_map/finish_blocks/pallas_call | solution.py:310
  (15 shorter events, 0.0 us)
Async XLA Ops:
  0.0 20.6 %collective-permute-start.3 = (bf16[256,12288]{1,0:T(8,128)(2,1)}, bf16[256,12288]{1,0:T(8,128)(2,1)}, u32[]{:S(2)}, u32[]{:S(2)}) collective-permute-start(bf16[256,12288]{1,0:T(8,128)(2,1)} %bitcast.3), channel_id=1, source_target_pairs={{0,1},{1,0},{2,3},{3,2},{4,5},{5,4},{6,7},{7,6},{8,9},{9,8},{10,11... | collective-permute-start | bytes 18874376 | tf_op jit(solution)/shard_map/ppermute | solution.py:18
  0.5 11.1 %collective-permute-start.4 = (bf16[16,32,384]{2,1,0:T(8,128)(2,1)}, bf16[16,32,384]{2,1,0:T(8,128)(2,1)S(1)}, u32[]{:S(2)}, u32[]{:S(2)}) collective-permute-start(bf16[16,32,384]{2,1,0:T(8,128)(2,1)} %own_ref.1), channel_id=1, source_target_pairs={{1,13},{3,15},{5,9},{7,11},{9,5},{11,7},{13,1},{15,3},{17,29},{19,... | collective-permute-start | bytes 1179656 | tf_op jit(solution)/shard_map/ppermute | solution.py:24
  1.1 8.6 %collective-permute-start = (s32[1,32]{1,0:T(1,128)}, s32[1,32]{1,0:T(1,128)S(1)}, u32[]{:S(2)}, u32[]{:S(2)}) collective-permute-start(s32[1,32]{1,0:T(1,128)} %list_ref.1), channel_id=1, source_target_pairs={{0,6},{1,7},{2,4},{3,5},{4,2},{5,3},{6,0},{7,1},{8,14},{9,15},{10,... | collective-permute-start | bytes 392 | tf_op jit(solution)/shard_map/ppermute | solution.py:24
  4.7 5.0 %collective-permute-start.1 = (s32[1,32]{1,0:T(1,128)}, s32[1,32]{1,0:T(1,128)S(1)}, u32[]{:S(2)}, u32[]{:S(2)}) collective-permute-start(s32[1,32]{1,0:T(1,128)} %list_ref.1), channel_id=1, source_target_pairs={{0,4},{1,5},{2,6},{3,7},{4,0},{5,1},{6,2},{7,3},{8,12},{9,13},{10,... | collective-permute-start | bytes 392 | tf_op jit(solution)/shard_map/ppermute | solution.py:24
  5.2 4.6 %collective-permute-start.2 = (s32[1,32]{1,0:T(1,128)}, s32[1,32]{1,0:T(1,128)S(1)}, u32[]{:S(2)}, u32[]{:S(2)}) collective-permute-start(s32[1,32]{1,0:T(1,128)} %list_ref.1), channel_id=1, source_target_pairs={{0,2},{1,3},{2,0},{3,1},{4,6},{5,7},{6,4},{7,5},{8,10},{9,11},{10,... | collective-permute-start | bytes 392 | tf_op jit(solution)/shard_map/ppermute | solution.py:24
  9.7 13.6 %copy-start = (f32[1,256]{1,0:T(1,128)S(1)}, f32[1,256]{1,0:T(1,128)}, u32[]{:S(2)}) copy-start(f32[1,256]{1,0:T(1,128)} %weight_ref.1) | copy-start | bytes 3076
  13.2 10.1 %collective-permute-start.5 = (bf16[4,32,384]{2,1,0:T(8,128)(2,1)S(1)}, bf16[4,32,384]{2,1,0:T(8,128)(2,1)S(1)}, u32[]{:S(2)}, u32[]{:S(2)}) collective-permute-start(bf16[4,32,384]{2,1,0:T(8,128)(2,1)S(1)} %get-tuple-element.23), channel_id=1, source_target_pairs={{0,6},{1,7},{2,4},{3,5},{4,2},{5,3},{6,0},{7,1},{8,14},{9,15},{10,... | collective-permute-start | bytes 294920 | tf_op jit(solution)/shard_map/ppermute | solution.py:24
  16.1 7.2 %collective-permute-start.6 = (bf16[4,32,384]{2,1,0:T(8,128)(2,1)S(1)}, bf16[4,32,384]{2,1,0:T(8,128)(2,1)S(1)}, u32[]{:S(2)}, u32[]{:S(2)}) collective-permute-start(bf16[4,32,384]{2,1,0:T(8,128)(2,1)S(1)} %get-tuple-element.24), channel_id=1, source_target_pairs={{0,4},{1,5},{2,6},{3,7},{4,0},{5,1},{6,2},{7,3},{8,12},{9,13},{10,... | collective-permute-start | bytes 294920 | tf_op jit(solution)/shard_map/ppermute | solution.py:24
  16.5 6.8 %collective-permute-start.7 = (bf16[4,32,384]{2,1,0:T(8,128)(2,1)S(1)}, bf16[4,32,384]{2,1,0:T(8,128)(2,1)S(1)}, u32[]{:S(2)}, u32[]{:S(2)}) collective-permute-start(bf16[4,32,384]{2,1,0:T(8,128)(2,1)S(1)} %get-tuple-element.25), channel_id=1, source_target_pairs={{0,2},{1,3},{2,0},{3,1},{4,6},{5,7},{6,4},{7,5},{8,10},{9,11},{10,... | collective-permute-start | bytes 294920 | tf_op jit(solution)/shard_map/ppermute | solution.py:24
  16.7 9.0 %collective-permute-start.8 = (s32[33]{0:T(128)S(1)}, s32[33]{0:T(128)S(1)}, u32[]{:S(2)}, u32[]{:S(2)}) collective-permute-start(s32[33]{0:T(128)S(1)} %search_lists.1.ids_ref.near_ref), channel_id=1, source_target_pairs={{0,12},{1,13},{2,14},{3,15},{4,8},{5,9},{6,10},{7,11},{8,4},{9,5},... | collective-permute-start | bytes 404 | tf_op jit(solution)/shard_map/ppermute | solution.py:24
  25.7 1.3 %collective-permute-start.9 = (f32[2,40,256]{2,1,0:T(8,128)S(1)}, f32[2,40,256]{2,1,0:T(8,128)S(1)}, u32[]{:S(2)}, u32[]{:S(2)}) collective-permute-start(f32[2,40,256]{2,1,0:T(8,128)S(1)} %predict.1.mine_ref), channel_id=1, source_target_pairs={{0,1},{1,0},{2,3},{3,2},{4,5},{5,4},{6,7},{7,6},{8,9},{9,8},{10,11... | collective-permute-start | bytes 245768 | tf_op jit(solution)/shard_map/ppermute | solution.py:18
  28.8 6.7 %collective-permute-start.10 = (bf16[4,32,384]{2,1,0:T(8,128)(2,1)S(1)}, bf16[4,32,384]{2,1,0:T(8,128)(2,1)S(1)}, u32[]{:S(2)}, u32[]{:S(2)}) collective-permute-start(bf16[4,32,384]{2,1,0:T(8,128)(2,1)S(1)} %get-tuple-element.29), channel_id=1, source_target_pairs={{0,6},{1,11},{2,4},{3,9},{4,2},{5,15},{6,0},{7,13},{8,14},{9,3},{1... | collective-permute-start | bytes 294920 | tf_op jit(solution)/shard_map/ppermute | solution.py:24
  30.1 7.4 %collective-permute-start.11 = (bf16[4,32,384]{2,1,0:T(8,128)(2,1)S(1)}, bf16[4,32,384]{2,1,0:T(8,128)(2,1)S(1)}, u32[]{:S(2)}, u32[]{:S(2)}) collective-permute-start(bf16[4,32,384]{2,1,0:T(8,128)(2,1)S(1)} %get-tuple-element.30), channel_id=1, source_target_pairs={{0,2},{1,15},{2,0},{3,13},{4,6},{5,11},{6,4},{7,9},{8,10},{9,7},{1... | collective-permute-start | bytes 294920 | tf_op jit(solution)/shard_map/ppermute | solution.py:24
  31.5 6.1 %collective-permute-start.12 = (bf16[4,32,384]{2,1,0:T(8,128)(2,1)S(1)}, bf16[4,32,384]{2,1,0:T(8,128)(2,1)S(1)}, u32[]{:S(2)}, u32[]{:S(2)}) collective-permute-start(bf16[4,32,384]{2,1,0:T(8,128)(2,1)S(1)} %get-tuple-element.31), channel_id=1, source_target_pairs={{0,4},{1,9},{2,6},{3,11},{4,0},{5,13},{6,2},{7,15},{8,12},{9,1},{1... | collective-permute-start | bytes 294920 | tf_op jit(solution)/shard_map/ppermute | solution.py:24
  32.4 7.2 %collective-permute-start.13 = (bf16[4,32,384]{2,1,0:T(8,128)(2,1)S(1)}, bf16[4,32,384]{2,1,0:T(8,128)(2,1)S(1)}, u32[]{:S(2)}, u32[]{:S(2)}) collective-permute-start(bf16[4,32,384]{2,1,0:T(8,128)(2,1)S(1)} %get-tuple-element.32), channel_id=1, source_target_pairs={{0,0},{1,13},{2,2},{3,15},{4,4},{5,9},{6,6},{7,11},{8,8},{9,5},{10... | collective-permute-start | bytes 294920 | tf_op jit(solution)/shard_map/ppermute | solution.py:24
  35.5 6.0 %collective-permute-start.14 = (bf16[4,32,384]{2,1,0:T(8,128)(2,1)S(1)}, bf16[4,32,384]{2,1,0:T(8,128)(2,1)S(1)}, u32[]{:S(2)}, u32[]{:S(2)}) collective-permute-start(bf16[4,32,384]{2,1,0:T(8,128)(2,1)S(1)} %collective-permute-done.10.refs_0_), channel_id=1, source_target_pairs={{0,1},{1,0},{2,3},{3,2},{4,5},{5,4},{6,7},{7,6},{8,9},{9,8},{10,11... | collective-permute-start | bytes 294920 | tf_op jit(solution)/shard_map/ppermute | solution.py:18
  37.5 4.0 %collective-permute-start.15 = (bf16[4,32,384]{2,1,0:T(8,128)(2,1)S(1)}, bf16[4,32,384]{2,1,0:T(8,128)(2,1)S(1)}, u32[]{:S(2)}, u32[]{:S(2)}) collective-permute-start(bf16[4,32,384]{2,1,0:T(8,128)(2,1)S(1)} %collective-permute-done.11.refs_1_), channel_id=1, source_target_pairs={{0,1},{1,0},{2,3},{3,2},{4,5},{5,4},{6,7},{7,6},{8,9},{9,8},{10,11... | collective-permute-start | bytes 294920 | tf_op jit(solution)/shard_map/ppermute | solution.py:18
  37.6 4.0 %collective-permute-start.16 = (bf16[4,32,384]{2,1,0:T(8,128)(2,1)S(1)}, bf16[4,32,384]{2,1,0:T(8,128)(2,1)S(1)}, u32[]{:S(2)}, u32[]{:S(2)}) collective-permute-start(bf16[4,32,384]{2,1,0:T(8,128)(2,1)S(1)} %collective-permute-done.12.refs_2_), channel_id=1, source_target_pairs={{0,1},{1,0},{2,3},{3,2},{4,5},{5,4},{6,7},{7,6},{8,9},{9,8},{10,11... | collective-permute-start | bytes 294920 | tf_op jit(solution)/shard_map/ppermute | solution.py:18
  39.5 2.2 %collective-permute-start.17 = (bf16[4,32,384]{2,1,0:T(8,128)(2,1)S(1)}, bf16[4,32,384]{2,1,0:T(8,128)(2,1)S(1)}, u32[]{:S(2)}, u32[]{:S(2)}) collective-permute-start(bf16[4,32,384]{2,1,0:T(8,128)(2,1)S(1)} %collective-permute-done.13.refs_3_), channel_id=1, source_target_pairs={{0,1},{1,0},{2,3},{3,2},{4,5},{5,4},{6,7},{7,6},{8,9},{9,8},{10,11... | collective-permute-start | bytes 294920 | tf_op jit(solution)/shard_map/ppermute | solution.py:18

commit v5 on v4

--- a/solution.py
+++ b/solution.py
@@ -159,32 +159,39 @@
             out_ref[c] = part.astype(jnp.bfloat16)
 
 
-def add_chunks(turns, capacity, places, chunks, out_ref):
+def add_chunks(turns, capacity, places, kept, kept_ref, chunks, out_ref):
     out_ref[...] = jnp.zeros_like(out_ref)
     for turn, chunk_ref in zip(turns, chunks):
         for c in range(capacity):
-            out_ref[places(turn * capacity + c)] += chunk_ref[c].astype(jnp.float32)
+            block = chunk_ref[c]
+            if turn == len(turns) - 1:
+                block = jnp.where(kept, kept_ref[c], block)
+            out_ref[places(turn * capacity + c)] += block.astype(jnp.float32)
 
 
 def sum_kernel(turns, capacity, here_ref, near_ref, far_ref, *refs):
-    *chunks, out_ref = refs
+    kept_ref, *chunks, out_ref = refs
     core, slots = here_ref[1], len(chunks) * capacity
     add_chunks(
         turns,
         capacity,
         lambda slot: jnp.where(core == 0, near_ref[slot], far_ref[slots + slot]),
+        core == 0,
+        kept_ref,
         chunks,
         out_ref,
     )
 
 
 def finish_kernel(turns, capacity, here_ref, near_ref, far_ref, own_ref, *refs):
-    *chunks, out_ref, total_ref, sems = refs
+    kept_ref, *chunks, out_ref, total_ref, sems = refs
     core, slots = here_ref[1], len(chunks) * capacity
     add_chunks(
         turns,
         capacity,
         lambda slot: jnp.where(core == 0, far_ref[slots + slot], near_ref[slot]),
+        core != 0,
+        kept_ref,
         chunks,
         total_ref,
     )
@@ -212,7 +219,7 @@
 
     own_sens = in_hbm(sensitivity[0])
     other_sens = in_hbm(swap_rows(sensitivity[0]))
-    mirrored = exchange(directions, {1: mirror})
+    mirrored = exchange(directions, {0: 1, 1: mirror})
     lists = [exchange(foot_list, {0: s, 1: s}) for s in order[:-1]]
 
     table = jax.ShapeDtypeStruct((slots + 1,), jnp.int32)
@@ -269,7 +276,7 @@
         name="stage_columns",
     )(column, other_sens)
 
-    far_ids = exchange(ids, {0: mirror, 1: mirror})
+    far_ids = exchange(ids, {0: 1, 1: mirror})
     partial = pl.pallas_call(
         functools.partial(predict_kernel, capacity),
         out_shape=jax.ShapeDtypeStruct((2, vecs + 8, rows), jnp.float32),
@@ -292,25 +299,27 @@
         cost_estimate=cost(1),
         name="back_project",
     )(live, own_sens, other_sens, partial, other_partial)
-    turns = list(range(0, steps, 2)) + list(range(1, steps, 2))
-    returned = [exchange(grads[i], {0: order[i], 1: order[i] ^ mirror}) for i in turns]
-
+    turns = list(range(steps))
+    returned = [exchange(grads[i], {0: order[i] or 1, 1: order[i] ^ mirror}) for i in turns]
+    own_grads = grads[steps - 1]
+    returned[0], passed_ids = lax.optimization_barrier((returned[0], swap_rows(far_ids)))
     other_returned = [swap_rows(x) for x in returned]
+    other_grads = swap_rows(own_grads)
 
     total = jax.ShapeDtypeStruct((blocks, vecs, width), jnp.float32)
     own_sum = pl.pallas_call(
         functools.partial(sum_kernel, turns, capacity),
         out_shape=total,
-        in_specs=[SMEM] * 3 + [VMEM] * steps,
+        in_specs=[SMEM] * 3 + [VMEM] * (1 + steps),
         out_specs=VMEM,
         compiler_params=PARAMS,
         cost_estimate=cost(1),
         name="sum_blocks",
-    )(here, ids, far_ids, *returned)
+    )(here, ids, far_ids, own_grads, *returned)
     return pl.pallas_call(
         functools.partial(finish_kernel, turns, capacity),
         out_shape=total,
-        in_specs=[SMEM] * 3 + [VMEM] * (1 + steps),
+        in_specs=[SMEM] * 3 + [VMEM] * (2 + steps),
         out_specs=HBM,
         scratch_shapes=[
             pltpu.VMEM((blocks, vecs, width), jnp.float32),
@@ -319,7 +328,7 @@
         compiler_params=PARAMS,
         cost_estimate=cost(1),
         name="finish_blocks",
-    )(here, ids, far_ids, own_sum, *other_returned)
+    )(here, ids, passed_ids, own_sum, other_grads, *other_returned)
 
 
 def solution(mesh):

time: 43.6 us -> 41.6 us (0.954)
  starting transfers between devices: 21.4 us -> 20.3 us
  waiting for transfers between devices: 4.99 us -> 4.18 us
    ppermute x12, starting transfers between devices: 16.6 us -> 13.9 us  [exchange(): return lax.ppermute(x, ('tile', 'row'), pairs)]
    ppermute x6 -> x8, starting transfers between devices: 4.86 us -> 6.4 us  [swap_rows(): return lax.ppermute(x, 'row', [(0, 1), (1, 0)])]
    ppermute x12, waiting for transfers between devices: 3.51 us -> 2.01 us  [exchange(): return lax.ppermute(x, ('tile', 'row'), pairs)]
    ppermute x6 -> x8, waiting for transfers between devices: 1.48 us -> 2.17 us  [swap_rows(): return lax.ppermute(x, 'row', [(0, 1), (1, 0)])]
  transfers between devices with their start and end apart: 18 -> 20, of which waited for: 5 -> 6; matrix products, arithmetic and copies ran while one was open for 0% -> 0% of each run, Pallas kernels for 31% -> 32%
where the time goes in v5:
time: 41.6 us; the launch traced here: 41.4 us
  starting transfers between devices  20.3 us (49%)
  Pallas kernels  16.7 us (40%)
  waiting for transfers between devices  4.18 us (10%)
    ppermute x12, starting transfers between devices, exchange(): return lax.ppermute(x, ('tile', 'row'), pairs)  13.9 us
    ppermute x8, starting transfers between devices, swap_rows(): return lax.ppermute(x, 'row', [(0, 1), (1, 0)])  6.4 us
    pallas_call x1, Pallas kernels, on_device(): pl.pallas_call(functools.partial(plan_kernel, tiles, capacity, blocks), o...  4.27 us
    pallas_call x1, Pallas kernels, on_device(): pl.pallas_call(functools.partial(stage_kernel, slots), out_shape=columns,...  2.65 us
    pallas_call x1, Pallas kernels, on_device(): pl.pallas_call(functools.partial(predict_kernel, capacity), out_shape=jax...  2.38 us
    ppermute x8, waiting for transfers between devices, swap_rows(): return lax.ppermute(x, 'row', [(0, 1), (1, 0)])  2.17 us
    ppermute x12, waiting for transfers between devices, exchange(): return lax.ppermute(x, ('tile', 'row'), pairs)  2.01 us
    pallas_call x1, Pallas kernels, on_device(): pl.pallas_call(functools.partial(search_kernel, tiles, capacity, blocks),...  1.77 us
  transfers between devices with their start and end apart: 20, of which 6 were waited for; matrix products, arithmetic and copies ran while one was open for 0% of the time, Pallas kernels for 32%

profile of v5, /device:TPU:0, one launch (start us, length us, event | category | flops | bytes accessed | tf_op | source)
XLA Modules:
  0.0 41.4 jit_solution(18267679669463054366)
XLA Ops:
  0.0 0.5 %collective-permute-start.3 = (bf16[256,12288]{1,0:T(8,128)(2,1)}, bf16[256,12288]{1,0:T(8,128)(2,1)}, u32[]{:S(2)}, u32[]{:S(2)}) collective-permute-start(bf16[256,12288]{1,0:T(8,128)(2,1)} %bitcast.3), channel_id=1, source_target_pairs={{0,1},{1,0},{2,3},{3,2},{4,5},{5,4},{6,7},{7,6},{8,9},{9,8},{10,11... | collective-permute-start | bytes 18874376 | tf_op jit(solution)/shard_map/ppermute | solution.py:18
  0.5 2.5 %collective-permute-start.4 = (bf16[16,32,384]{2,1,0:T(8,128)(2,1)}, bf16[16,32,384]{2,1,0:T(8,128)(2,1)S(1)}, u32[]{:S(2)}, u32[]{:S(2)}) collective-permute-start(bf16[16,32,384]{2,1,0:T(8,128)(2,1)} %own_ref.1), channel_id=1, source_target_pairs={{0,2},{1,13},{2,0},{3,15},{4,6},{5,9},{6,4},{7,11},{8,10},{9,5},{1... | collective-permute-start | bytes 1179656 | tf_op jit(solution)/shard_map/ppermute | solution.py:24
  3.0 1.5 %collective-permute-start = (s32[1,32]{1,0:T(1,128)}, s32[1,32]{1,0:T(1,128)S(1)}, u32[]{:S(2)}, u32[]{:S(2)}) collective-permute-start(s32[1,32]{1,0:T(1,128)} %list_ref.1), channel_id=1, source_target_pairs={{0,6},{1,7},{2,4},{3,5},{4,2},{5,3},{6,0},{7,1},{8,14},{9,15},{10,... | collective-permute-start | bytes 392 | tf_op jit(solution)/shard_map/ppermute | solution.py:24
  4.6 1.9 %collective-permute-start.2 = (s32[1,32]{1,0:T(1,128)}, s32[1,32]{1,0:T(1,128)S(1)}, u32[]{:S(2)}, u32[]{:S(2)}) collective-permute-start(s32[1,32]{1,0:T(1,128)} %list_ref.1), channel_id=1, source_target_pairs={{0,2},{1,3},{2,0},{3,1},{4,6},{5,7},{6,4},{7,5},{8,10},{9,11},{10,... | collective-permute-start | bytes 392 | tf_op jit(solution)/shard_map/ppermute | solution.py:24
  6.5 4.3 %plan_columns.1 = (s32[17]{0:T(128)S(1)}, s32[17]{0:T(128)S(1)}, s32[9]{0:T(128)S(1)}, bf16[256,6144]{1,0:T(8,128)(2,1)S(1)}) custom-call(s32[2]{0:T(128)S(1)} %pad_add_fusion.here_ref, s32[1,32]{1,0:T(1,128)} %list_ref.1, s32[1,32]{1,0:T(1,128)} %mask_ref.1, bf16[256,12288]{1,0:T(8,128)(2,1)} %bitcast.4), custom_call_target="tpu_custom_call" | custom-call | bytes 1 | tf_op jit(solution)/shard_map/plan_columns/pallas_call | solution.py:227
  10.9 1.8 %search_lists.1.ids_ref.near_ref = s32[33]{0:T(128)S(1)} custom-call(s32[2]{0:T(128)S(1)} %pad_add_fusion.here_ref, s32[9]{0:T(128)S(1)} %get-tuple-element.21.own_ids_ref, s32[1,32]{1,0:T(1,128)S(1)} %collective-permute-done.refs_0_, s32[1,32]{1,0:T(1,128)S(1)} %collective-permute-done.1.refs_1_, s32[1,32]{1,0:T(1,128)S(1)} %collective-permute-done.2.refs_2_), custom_call_target="tpu_custom_call" | custom-call | bytes 1 | tf_op jit(solution)/shard_map/search_lists/pallas_call | solution.py:244
  12.6 1.6 %select_blocks.1 = (bf16[4,32,384]{2,1,0:T(8,128)(2,1)S(1)}, bf16[4,32,384]{2,1,0:T(8,128)(2,1)S(1)}, bf16[4,32,384]{2,1,0:T(8,128)(2,1)S(1)}, bf16[4,32,384]{2,1,0:T(8,128)(2,1)S(1)}) custom-call(s32[2]{0:T(128)S(1)} %pad_add_fusion.here_ref, s32[33]{0:T(128)S(1)} %search_lists.1.ids_ref.near_ref, bf16[16,32,384]{2,1,0:T(8,128)(2,1)} %own_ref.1, ...), custom_call_target="tpu_custom_call" | custom-call | bytes 1 | tf_op jit(solution)/shard_map/select_blocks/pallas_call | solution.py:253
  14.2 1.6 %collective-permute-start.5 = (bf16[4,32,384]{2,1,0:T(8,128)(2,1)S(1)}, bf16[4,32,384]{2,1,0:T(8,128)(2,1)S(1)}, u32[]{:S(2)}, u32[]{:S(2)}) collective-permute-start(bf16[4,32,384]{2,1,0:T(8,128)(2,1)S(1)} %get-tuple-element.25), channel_id=1, source_target_pairs={{0,6},{1,7},{2,4},{3,5},{4,2},{5,3},{6,0},{7,1},{8,14},{9,15},{10,... | collective-permute-start | bytes 294920 | tf_op jit(solution)/shard_map/ppermute | solution.py:24
  16.0 1.9 %collective-permute-start.7 = (bf16[4,32,384]{2,1,0:T(8,128)(2,1)S(1)}, bf16[4,32,384]{2,1,0:T(8,128)(2,1)S(1)}, u32[]{:S(2)}, u32[]{:S(2)}) collective-permute-start(bf16[4,32,384]{2,1,0:T(8,128)(2,1)S(1)} %get-tuple-element.27), channel_id=1, source_target_pairs={{0,2},{1,3},{2,0},{3,1},{4,6},{5,7},{6,4},{7,5},{8,10},{9,11},{10,... | collective-permute-start | bytes 294920 | tf_op jit(solution)/shard_map/ppermute | solution.py:24
  17.8 0.2 collective-permute-start.8
  18.0 2.7 %stage_columns.1.other_ref = bf16[256,6144]{1,0:T(8,128)(2,1)S(1)} custom-call(s32[17]{0:T(128)S(1)} %get-tuple-element.24.column_ref, bf16[256,12288]{1,0:T(8,128)(2,1)} %collective-permute-done.3.sens_ref), custom_call_target="tpu_custom_call" | custom-call | bytes 1 | tf_op jit(solution)/shard_map/stage_columns/pallas_call | solution.py:268
  20.7 0.2 collective-permute-done.5.refs_0_
  20.9 0.6 %collective-permute-done.6.refs_1_ = bf16[4,32,384]{2,1,0:T(8,128)(2,1)S(1)} collective-permute-done((bf16[4,32,384]{2,1,0:T(8,128)(2,1)S(1)}, bf16[4,32,384]{2,1,0:T(8,128)(2,1)S(1)}, u32[]{:S(2)}, u32[]{:S(2)}) %collective-permute-start.6) | collective-permute-done | bytes 98336 | tf_op jit(solution)/shard_map/ppermute | solution.py:24
  21.5 1.2 %collective-permute-done.7.refs_2_ = bf16[4,32,384]{2,1,0:T(8,128)(2,1)S(1)} collective-permute-done((bf16[4,32,384]{2,1,0:T(8,128)(2,1)S(1)}, bf16[4,32,384]{2,1,0:T(8,128)(2,1)S(1)}, u32[]{:S(2)}, u32[]{:S(2)}) %collective-permute-start.7) | collective-permute-done | bytes 98336 | tf_op jit(solution)/shard_map/ppermute | solution.py:24
  22.6 2.4 %predict.1.mine_ref = f32[2,40,256]{2,1,0:T(8,128)S(1)} custom-call(s32[17]{0:T(128)S(1)} %get-tuple-element.22.live_ref, bf16[256,6144]{1,0:T(8,128)(2,1)S(1)} %get-tuple-element.23.own_ref, bf16[256,6144]{1,0:T(8,128)(2,1)S(1)} %stage_columns.1.other_ref, f32[1,256]{1,0:T(1,128)S(1)} %copy-done, bf16[4,32,384]{2,1,0:T(8,128)(2,1)S(1)} %collective-permute-done.5.refs_0_, ...), custom_call_target="tpu_custom_call" | custom-call | bytes 1 | tf_op jit(solution)/shard_map/predict/pallas_call | solution.py:280
  25.0 0.2 collective-permute-start.9
  25.2 1.2 %collective-permute-done.9.theirs_ref = f32[2,40,256]{2,1,0:T(8,128)S(1)} collective-permute-done((f32[2,40,256]{2,1,0:T(8,128)S(1)}, f32[2,40,256]{2,1,0:T(8,128)S(1)}, u32[]{:S(2)}, u32[]{:S(2)}) %collective-permute-start.9) | collective-permute-done | bytes 81952 | tf_op jit(solution)/shard_map/ppermute | solution.py:18
  26.4 1.7 %back_project.1 = (bf16[4,32,384]{2,1,0:T(8,128)(2,1)S(1)}, bf16[4,32,384]{2,1,0:T(8,128)(2,1)S(1)}, bf16[4,32,384]{2,1,0:T(8,128)(2,1)S(1)}, bf16[4,32,384]{2,1,0:T(8,128)(2,1)S(1)}) custom-call(s32[17]{0:T(128)S(1)} %get-tuple-element.22.live_ref, bf16[256,6144]{1,0:T(8,128)(2,1)S(1)} %get-tuple-element.23.own_ref, ...), custom_call_target="tpu_custom_call" | custom-call | bytes 1 | tf_op jit(solution)/shard_map/back_project/pallas_call | solution.py:293
  28.1 1.5 %collective-permute-start.10 = (bf16[4,32,384]{2,1,0:T(8,128)(2,1)S(1)}, bf16[4,32,384]{2,1,0:T(8,128)(2,1)S(1)}, u32[]{:S(2)}, u32[]{:S(2)}) collective-permute-start(bf16[4,32,384]{2,1,0:T(8,128)(2,1)S(1)} %get-tuple-element.30), channel_id=1, source_target_pairs={{0,6},{1,11},{2,4},{3,9},{4,2},{5,15},{6,0},{7,13},{8,14},{9,3},{1... | collective-permute-start | bytes 294920 | tf_op jit(solution)/shard_map/ppermute | solution.py:24
  29.6 0.6 %collective-permute-start.12 = (bf16[4,32,384]{2,1,0:T(8,128)(2,1)S(1)}, bf16[4,32,384]{2,1,0:T(8,128)(2,1)S(1)}, u32[]{:S(2)}, u32[]{:S(2)}) collective-permute-start(bf16[4,32,384]{2,1,0:T(8,128)(2,1)S(1)} %get-tuple-element.35), channel_id=1, source_target_pairs={{0,4},{1,9},{2,6},{3,11},{4,0},{5,13},{6,2},{7,15},{8,12},{9,1},{1... | collective-permute-start | bytes 294920 | tf_op jit(solution)/shard_map/ppermute | solution.py:24
  30.2 1.4 %collective-permute-start.13 = (bf16[4,32,384]{2,1,0:T(8,128)(2,1)S(1)}, bf16[4,32,384]{2,1,0:T(8,128)(2,1)S(1)}, u32[]{:S(2)}, u32[]{:S(2)}) collective-permute-start(bf16[4,32,384]{2,1,0:T(8,128)(2,1)S(1)} %get-tuple-element.36), channel_id=1, source_target_pairs={{0,2},{1,15},{2,0},{3,13},{4,6},{5,11},{6,4},{7,9},{8,10},{9,7},{1... | collective-permute-start | bytes 294920 | tf_op jit(solution)/shard_map/ppermute | solution.py:24
  31.7 0.6 %collective-permute-start.14 = (bf16[4,32,384]{2,1,0:T(8,128)(2,1)S(1)}, bf16[4,32,384]{2,1,0:T(8,128)(2,1)S(1)}, u32[]{:S(2)}, u32[]{:S(2)}) collective-permute-start(bf16[4,32,384]{2,1,0:T(8,128)(2,1)S(1)} %get-tuple-element.33.refs_0_), channel_id=1, source_target_pairs={{0,2},{1,13},{2,0},{3,15},{4,6},{5,9},{6,4},{7,11},{8,10},{9,5},{1... | collective-permute-start | bytes 294920 | tf_op jit(solution)/shard_map/ppermute | solution.py:24
  32.3 2.6 %collective-permute-start.11 = (s32[33]{0:T(128)S(1)}, s32[33]{0:T(128)S(1)}, u32[]{:S(2)}, u32[]{:S(2)}) collective-permute-start(s32[33]{0:T(128)S(1)} %collective-permute-done.8.far_ref), channel_id=1, source_target_pairs={{0,1},{1,0},{2,3},{3,2},{4,5},{5,4},{6,7},{7,6},{8,9},{9,8},{10,11... | collective-permute-start | bytes 404 | tf_op jit(solution)/shard_map/ppermute | solution.py:18
  34.8 0.8 %collective-permute-done.11.far_ref = s32[33]{0:T(128)S(1)} collective-permute-done((s32[33]{0:T(128)S(1)}, s32[33]{0:T(128)S(1)}, u32[]{:S(2)}, u32[]{:S(2)}) %collective-permute-start.11) | collective-permute-done | bytes 164 | tf_op jit(solution)/shard_map/ppermute | solution.py:18
  35.7 0.3 collective-permute-start.15
  36.0 0.2 collective-permute-start.16
  36.2 0.3 collective-permute-start.17
  36.5 1.8 %collective-permute-start.18 = (bf16[4,32,384]{2,1,0:T(8,128)(2,1)S(1)}, bf16[4,32,384]{2,1,0:T(8,128)(2,1)S(1)}, u32[]{:S(2)}, u32[]{:S(2)}) collective-permute-start(bf16[4,32,384]{2,1,0:T(8,128)(2,1)S(1)} %collective-permute-done.13.refs_3_), channel_id=1, source_target_pairs={{0,1},{1,0},{2,3},{3,2},{4,5},{5,4},{6,7},{7,6},{8,9},{9,8},{10,11... | collective-permute-start | bytes 294920 | tf_op jit(solution)/shard_map/ppermute | solution.py:18
  38.3 0.5 %collective-permute-start.19 = (bf16[4,32,384]{2,1,0:T(8,128)(2,1)S(1)}, bf16[4,32,384]{2,1,0:T(8,128)(2,1)S(1)}, u32[]{:S(2)}, u32[]{:S(2)}) collective-permute-start(bf16[4,32,384]{2,1,0:T(8,128)(2,1)S(1)} %collective-permute-done.14.refs_4_), channel_id=1, source_target_pairs={{0,1},{1,0},{2,3},{3,2},{4,5},{5,4},{6,7},{7,6},{8,9},{9,8},{10,11... | collective-permute-start | bytes 294920 | tf_op jit(solution)/shard_map/ppermute | solution.py:18
  38.9 0.7 %sum_blocks.1.own_ref = f32[16,32,384]{2,1,0:T(8,128)S(1)} custom-call(s32[2]{0:T(128)S(1)} %pad_add_fusion.here_ref, s32[33]{0:T(128)S(1)} %search_lists.1.ids_ref.near_ref, s32[33]{0:T(128)S(1)} %collective-permute-done.8.far_ref, bf16[4,32,384]{2,1,0:T(8,128)(2,1)S(1)} %get-tuple-element.33.refs_0_, ...), custom_call_target="tpu_custom_call" | custom-call | bytes 1 | tf_op jit(solution)/shard_map/sum_blocks/pallas_call | solution.py:310
  39.6 0.2 collective-permute-done.19.refs_4_
  39.8 1.6 %finish_blocks.1 = f32[16,32,384]{2,1,0:T(8,128)} custom-call(s32[2]{0:T(128)S(1)} %pad_add_fusion.here_ref, s32[33]{0:T(128)S(1)} %search_lists.1.ids_ref.near_ref, s32[33]{0:T(128)S(1)} %collective-permute-done.11.far_ref, f32[16,32,384]{2,1,0:T(8,128)S(1)} %sum_blocks.1.own_ref, bf16[4,32,384]{2,1,0:T(8,128)(2,1)S(1)} %collective-permute-done.15.refs_0_, ...), custom_call_target="tpu_custom_call" | custom-call | bytes 1 | tf_op jit(solution)/shard_map/finish_blocks/pallas_call | solution.py:319
  (19 shorter events, 0.3 us)
Async XLA Ops:
  0.0 18.0 %collective-permute-start.3 = (bf16[256,12288]{1,0:T(8,128)(2,1)}, bf16[256,12288]{1,0:T(8,128)(2,1)}, u32[]{:S(2)}, u32[]{:S(2)}) collective-permute-start(bf16[256,12288]{1,0:T(8,128)(2,1)} %bitcast.3), channel_id=1, source_target_pairs={{0,1},{1,0},{2,3},{3,2},{4,5},{5,4},{6,7},{7,6},{8,9},{9,8},{10,11... | collective-permute-start | bytes 18874376 | tf_op jit(solution)/shard_map/ppermute | solution.py:18
  0.5 12.2 %collective-permute-start.4 = (bf16[16,32,384]{2,1,0:T(8,128)(2,1)}, bf16[16,32,384]{2,1,0:T(8,128)(2,1)S(1)}, u32[]{:S(2)}, u32[]{:S(2)}) collective-permute-start(bf16[16,32,384]{2,1,0:T(8,128)(2,1)} %own_ref.1), channel_id=1, source_target_pairs={{0,2},{1,13},{2,0},{3,15},{4,6},{5,9},{6,4},{7,11},{8,10},{9,5},{1... | collective-permute-start | bytes 1179656 | tf_op jit(solution)/shard_map/ppermute | solution.py:24
  3.0 7.9 %collective-permute-start = (s32[1,32]{1,0:T(1,128)}, s32[1,32]{1,0:T(1,128)S(1)}, u32[]{:S(2)}, u32[]{:S(2)}) collective-permute-start(s32[1,32]{1,0:T(1,128)} %list_ref.1), channel_id=1, source_target_pairs={{0,6},{1,7},{2,4},{3,5},{4,2},{5,3},{6,0},{7,1},{8,14},{9,15},{10,... | collective-permute-start | bytes 392 | tf_op jit(solution)/shard_map/ppermute | solution.py:24
  4.5 6.3 %collective-permute-start.1 = (s32[1,32]{1,0:T(1,128)}, s32[1,32]{1,0:T(1,128)S(1)}, u32[]{:S(2)}, u32[]{:S(2)}) collective-permute-start(s32[1,32]{1,0:T(1,128)} %list_ref.1), channel_id=1, source_target_pairs={{0,4},{1,5},{2,6},{3,7},{4,0},{5,1},{6,2},{7,3},{8,12},{9,13},{10,... | collective-permute-start | bytes 392 | tf_op jit(solution)/shard_map/ppermute | solution.py:24
  4.6 6.3 %collective-permute-start.2 = (s32[1,32]{1,0:T(1,128)}, s32[1,32]{1,0:T(1,128)S(1)}, u32[]{:S(2)}, u32[]{:S(2)}) collective-permute-start(s32[1,32]{1,0:T(1,128)} %list_ref.1), channel_id=1, source_target_pairs={{0,2},{1,3},{2,0},{3,1},{4,6},{5,7},{6,4},{7,5},{8,10},{9,11},{10,... | collective-permute-start | bytes 392 | tf_op jit(solution)/shard_map/ppermute | solution.py:24
  10.8 11.8 %copy-start = (f32[1,256]{1,0:T(1,128)S(1)}, f32[1,256]{1,0:T(1,128)}, u32[]{:S(2)}) copy-start(f32[1,256]{1,0:T(1,128)} %weight_ref.1) | copy-start | bytes 3076
  14.2 6.6 %collective-permute-start.5 = (bf16[4,32,384]{2,1,0:T(8,128)(2,1)S(1)}, bf16[4,32,384]{2,1,0:T(8,128)(2,1)S(1)}, u32[]{:S(2)}, u32[]{:S(2)}) collective-permute-start(bf16[4,32,384]{2,1,0:T(8,128)(2,1)S(1)} %get-tuple-element.25), channel_id=1, source_target_pairs={{0,6},{1,7},{2,4},{3,5},{4,2},{5,3},{6,0},{7,1},{8,14},{9,15},{10,... | collective-permute-start | bytes 294920 | tf_op jit(solution)/shard_map/ppermute | solution.py:24
  15.8 5.6 %collective-permute-start.6 = (bf16[4,32,384]{2,1,0:T(8,128)(2,1)S(1)}, bf16[4,32,384]{2,1,0:T(8,128)(2,1)S(1)}, u32[]{:S(2)}, u32[]{:S(2)}) collective-permute-start(bf16[4,32,384]{2,1,0:T(8,128)(2,1)S(1)} %get-tuple-element.26), channel_id=1, source_target_pairs={{0,4},{1,5},{2,6},{3,7},{4,0},{5,1},{6,2},{7,3},{8,12},{9,13},{10,... | collective-permute-start | bytes 294920 | tf_op jit(solution)/shard_map/ppermute | solution.py:24
  16.0 6.7 %collective-permute-start.7 = (bf16[4,32,384]{2,1,0:T(8,128)(2,1)S(1)}, bf16[4,32,384]{2,1,0:T(8,128)(2,1)S(1)}, u32[]{:S(2)}, u32[]{:S(2)}) collective-permute-start(bf16[4,32,384]{2,1,0:T(8,128)(2,1)S(1)} %get-tuple-element.27), channel_id=1, source_target_pairs={{0,2},{1,3},{2,0},{3,1},{4,6},{5,7},{6,4},{7,5},{8,10},{9,11},{10,... | collective-permute-start | bytes 294920 | tf_op jit(solution)/shard_map/ppermute | solution.py:24
  17.8 7.2 %collective-permute-start.8 = (s32[33]{0:T(128)S(1)}, s32[33]{0:T(128)S(1)}, u32[]{:S(2)}, u32[]{:S(2)}) collective-permute-start(s32[33]{0:T(128)S(1)} %search_lists.1.ids_ref.near_ref), channel_id=1, source_target_pairs={{0,2},{1,13},{2,0},{3,15},{4,6},{5,9},{6,4},{7,11},{8,10},{9,5},{1... | collective-permute-start | bytes 404 | tf_op jit(solution)/shard_map/ppermute | solution.py:24
  25.0 1.3 %collective-permute-start.9 = (f32[2,40,256]{2,1,0:T(8,128)S(1)}, f32[2,40,256]{2,1,0:T(8,128)S(1)}, u32[]{:S(2)}, u32[]{:S(2)}) collective-permute-start(f32[2,40,256]{2,1,0:T(8,128)S(1)} %predict.1.mine_ref), channel_id=1, source_target_pairs={{0,1},{1,0},{2,3},{3,2},{4,5},{5,4},{6,7},{7,6},{8,9},{9,8},{10,11... | collective-permute-start | bytes 245768 | tf_op jit(solution)/shard_map/ppermute | solution.py:18
  28.1 7.9 %collective-permute-start.10 = (bf16[4,32,384]{2,1,0:T(8,128)(2,1)S(1)}, bf16[4,32,384]{2,1,0:T(8,128)(2,1)S(1)}, u32[]{:S(2)}, u32[]{:S(2)}) collective-permute-start(bf16[4,32,384]{2,1,0:T(8,128)(2,1)S(1)} %get-tuple-element.30), channel_id=1, source_target_pairs={{0,6},{1,11},{2,4},{3,9},{4,2},{5,15},{6,0},{7,13},{8,14},{9,3},{1... | collective-permute-start | bytes 294920 | tf_op jit(solution)/shard_map/ppermute | solution.py:24
  29.6 6.6 %collective-permute-start.12 = (bf16[4,32,384]{2,1,0:T(8,128)(2,1)S(1)}, bf16[4,32,384]{2,1,0:T(8,128)(2,1)S(1)}, u32[]{:S(2)}, u32[]{:S(2)}) collective-permute-start(bf16[4,32,384]{2,1,0:T(8,128)(2,1)S(1)} %get-tuple-element.35), channel_id=1, source_target_pairs={{0,4},{1,9},{2,6},{3,11},{4,0},{5,13},{6,2},{7,15},{8,12},{9,1},{1... | collective-permute-start | bytes 294920 | tf_op jit(solution)/shard_map/ppermute | solution.py:24
  30.2 6.3 %collective-permute-start.13 = (bf16[4,32,384]{2,1,0:T(8,128)(2,1)S(1)}, bf16[4,32,384]{2,1,0:T(8,128)(2,1)S(1)}, u32[]{:S(2)}, u32[]{:S(2)}) collective-permute-start(bf16[4,32,384]{2,1,0:T(8,128)(2,1)S(1)} %get-tuple-element.36), channel_id=1, source_target_pairs={{0,2},{1,15},{2,0},{3,13},{4,6},{5,11},{6,4},{7,9},{8,10},{9,7},{1... | collective-permute-start | bytes 294920 | tf_op jit(solution)/shard_map/ppermute | solution.py:24
  31.7 6.7 %collective-permute-start.14 = (bf16[4,32,384]{2,1,0:T(8,128)(2,1)S(1)}, bf16[4,32,384]{2,1,0:T(8,128)(2,1)S(1)}, u32[]{:S(2)}, u32[]{:S(2)}) collective-permute-start(bf16[4,32,384]{2,1,0:T(8,128)(2,1)S(1)} %get-tuple-element.33.refs_0_), channel_id=1, source_target_pairs={{0,2},{1,13},{2,0},{3,15},{4,6},{5,9},{6,4},{7,11},{8,10},{9,5},{1... | collective-permute-start | bytes 294920 | tf_op jit(solution)/shard_map/ppermute | solution.py:24
  32.3 3.4 %collective-permute-start.11 = (s32[33]{0:T(128)S(1)}, s32[33]{0:T(128)S(1)}, u32[]{:S(2)}, u32[]{:S(2)}) collective-permute-start(s32[33]{0:T(128)S(1)} %collective-permute-done.8.far_ref), channel_id=1, source_target_pairs={{0,1},{1,0},{2,3},{3,2},{4,5},{5,4},{6,7},{7,6},{8,9},{9,8},{10,11... | collective-permute-start | bytes 404 | tf_op jit(solution)/shard_map/ppermute | solution.py:18
  35.7 3.9 %collective-permute-start.15 = (bf16[4,32,384]{2,1,0:T(8,128)(2,1)S(1)}, bf16[4,32,384]{2,1,0:T(8,128)(2,1)S(1)}, u32[]{:S(2)}, u32[]{:S(2)}) collective-permute-start(bf16[4,32,384]{2,1,0:T(8,128)(2,1)S(1)} %get-tuple-element.33.refs_0_), channel_id=1, source_target_pairs={{0,1},{1,0},{2,3},{3,2},{4,5},{5,4},{6,7},{7,6},{8,9},{9,8},{10,11... | collective-permute-start | bytes 294920 | tf_op jit(solution)/shard_map/ppermute | solution.py:18
  36.0 3.6 %collective-permute-start.16 = (bf16[4,32,384]{2,1,0:T(8,128)(2,1)S(1)}, bf16[4,32,384]{2,1,0:T(8,128)(2,1)S(1)}, u32[]{:S(2)}, u32[]{:S(2)}) collective-permute-start(bf16[4,32,384]{2,1,0:T(8,128)(2,1)S(1)} %collective-permute-done.10.refs_1_), channel_id=1, source_target_pairs={{0,1},{1,0},{2,3},{3,2},{4,5},{5,4},{6,7},{7,6},{8,9},{9,8},{10,11... | collective-permute-start | bytes 294920 | tf_op jit(solution)/shard_map/ppermute | solution.py:18
  36.2 3.4 %collective-permute-start.17 = (bf16[4,32,384]{2,1,0:T(8,128)(2,1)S(1)}, bf16[4,32,384]{2,1,0:T(8,128)(2,1)S(1)}, u32[]{:S(2)}, u32[]{:S(2)}) collective-permute-start(bf16[4,32,384]{2,1,0:T(8,128)(2,1)S(1)} %collective-permute-done.12.refs_2_), channel_id=1, source_target_pairs={{0,1},{1,0},{2,3},{3,2},{4,5},{5,4},{6,7},{7,6},{8,9},{9,8},{10,11... | collective-permute-start | bytes 294920 | tf_op jit(solution)/shard_map/ppermute | solution.py:18
  36.5 3.1 %collective-permute-start.18 = (bf16[4,32,384]{2,1,0:T(8,128)(2,1)S(1)}, bf16[4,32,384]{2,1,0:T(8,128)(2,1)S(1)}, u32[]{:S(2)}, u32[]{:S(2)}) collective-permute-start(bf16[4,32,384]{2,1,0:T(8,128)(2,1)S(1)} %collective-permute-done.13.refs_3_), channel_id=1, source_target_pairs={{0,1},{1,0},{2,3},{3,2},{4,5},{5,4},{6,7},{7,6},{8,9},{9,8},{10,11... | collective-permute-start | bytes 294920 | tf_op jit(solution)/shard_map/ppermute | solution.py:18
  38.3 1.5 %collective-permute-start.19 = (bf16[4,32,384]{2,1,0:T(8,128)(2,1)S(1)}, bf16[4,32,384]{2,1,0:T(8,128)(2,1)S(1)}, u32[]{:S(2)}, u32[]{:S(2)}) collective-permute-start(bf16[4,32,384]{2,1,0:T(8,128)(2,1)S(1)} %collective-permute-done.14.refs_4_), channel_id=1, source_target_pairs={{0,1},{1,0},{2,3},{3,2},{4,5},{5,4},{6,7},{7,6},{8,9},{9,8},{10,11... | collective-permute-start | bytes 294920 | tf_op jit(solution)/shard_map/ppermute | solution.py:18

commit v6 on v5

--- a/solution.py
+++ b/solution.py
@@ -88,20 +88,26 @@
         copy.wait()
 
 
-def stage_kernel(slots, column_ref, sens_ref, out_ref, sems):
-    for copy in column_copies(slots, column_ref, sens_ref, out_ref, sems):
+def search_lists(owner, part, capacity, blocks, own_ids_ref, lists, ids_ref):
+    for turn, list_ref in enumerate(lists):
+        find_asked(list_ref, owner, blocks, turn * capacity, ids_ref)
+    for c in range(capacity):
+        ids_ref[len(lists) * capacity + c] = own_ids_ref[part * capacity + c]
+
+
+def stage_kernel(tiles, capacity, blocks, here_ref, own_ids_ref, column_ref, *refs):
+    *lists, sens_ref, out_ref, near_ref, sems = refs
+    copies = column_copies(tiles // 2 * capacity, column_ref, sens_ref, out_ref, sems)
+    search_lists(here_ref[0], 0, capacity, blocks, own_ids_ref, lists, near_ref)
+    for copy in copies:
         copy.wait()
 
 
 def search_kernel(tiles, capacity, blocks, here_ref, own_ids_ref, *refs):
     *lists, ids_ref = refs
-    steps, tile = tiles // 2, here_ref[0]
-    slots = steps * capacity
-    for part, owner in enumerate((tile, tile ^ (tiles - 2))):
-        for turn, list_ref in enumerate(lists):
-            find_asked(list_ref, owner, blocks, part * slots + turn * capacity, ids_ref)
-        for c in range(capacity):
-            ids_ref[part * slots + (steps - 1) * capacity + c] = own_ids_ref[part * capacity + c]
+    core = here_ref[1]
+    owner = jnp.where(core == 0, here_ref[0], here_ref[0] ^ (tiles - 2))
+    search_lists(owner, core, capacity, blocks, own_ids_ref, lists, ids_ref)
 
 
 def select_kernel(capacity, here_ref, ids_ref, own_ref, mirror_ref, *refs):
@@ -117,10 +123,9 @@
         pltpu.make_async_copy(mirror_ref, dirs_ref, sem.at[0]).start()
 
     pltpu.make_async_copy(own_ref, dirs_ref, sem.at[0]).wait()
-    start = core * (len(outs) * capacity)
     for turn, out_ref in enumerate(outs):
         for c in range(capacity):
-            out_ref[c] = dirs_ref[ids_ref[start + turn * capacity + c]]
+            out_ref[c] = dirs_ref[ids_ref[turn * capacity + c]]
 
 
 def predict_kernel(capacity, live_ref, own_ref, other_ref, weight_ref, *refs):
@@ -171,11 +176,11 @@
 
 def sum_kernel(turns, capacity, here_ref, near_ref, far_ref, *refs):
     kept_ref, *chunks, out_ref = refs
-    core, slots = here_ref[1], len(chunks) * capacity
+    core = here_ref[1]
     add_chunks(
         turns,
         capacity,
-        lambda slot: jnp.where(core == 0, near_ref[slot], far_ref[slots + slot]),
+        lambda slot: jnp.where(core == 0, near_ref[slot], far_ref[slot]),
         core == 0,
         kept_ref,
         chunks,
@@ -185,11 +190,11 @@
 
 def finish_kernel(turns, capacity, here_ref, near_ref, far_ref, own_ref, *refs):
     kept_ref, *chunks, out_ref, total_ref, sems = refs
-    core, slots = here_ref[1], len(chunks) * capacity
+    core = here_ref[1]
     add_chunks(
         turns,
         capacity,
-        lambda slot: jnp.where(core == 0, far_ref[slots + slot], near_ref[slot]),
+        lambda slot: jnp.where(core == 0, far_ref[slot], near_ref[slot]),
         core != 0,
         kept_ref,
         chunks,
@@ -243,7 +248,7 @@
     chunk = jax.ShapeDtypeStruct((capacity, vecs, width), jnp.bfloat16)
     ids = pl.pallas_call(
         functools.partial(search_kernel, tiles, capacity, blocks),
-        out_shape=jax.ShapeDtypeStruct((2 * slots + 1,), jnp.int32),
+        out_shape=table,
         in_specs=[SMEM] * (1 + steps),
         out_specs=SMEM,
         compiler_params=PARAMS,
@@ -265,16 +270,16 @@
     )(here, ids, in_hbm(directions), mirrored)
     fetched = [exchange(x, {0: s, 1: s}) for s, x in zip(order[:-1], chunks)] + [chunks[-1]]
 
-    other_sens = pl.pallas_call(
-        functools.partial(stage_kernel, slots),
-        out_shape=columns,
-        in_specs=[SMEM, HBM],
-        out_specs=VMEM,
+    other_sens, near_ids = pl.pallas_call(
+        functools.partial(stage_kernel, tiles, capacity, blocks),
+        out_shape=[columns, table],
+        in_specs=[SMEM] * (2 + steps) + [HBM],
+        out_specs=[VMEM, SMEM],
         scratch_shapes=[pltpu.SemaphoreType.DMA((slots,))],
         compiler_params=PARAMS,
         cost_estimate=cost(1),
         name="stage_columns",
-    )(column, other_sens)
+    )(here, own_ids, column, *lists, other_sens)
 
     far_ids = exchange(ids, {0: 1, 1: mirror})
     partial = pl.pallas_call(
@@ -315,7 +320,7 @@
         compiler_params=PARAMS,
         cost_estimate=cost(1),
         name="sum_blocks",
-    )(here, ids, far_ids, own_grads, *returned)
+    )(here, near_ids, far_ids, own_grads, *returned)
     return pl.pallas_call(
         functools.partial(finish_kernel, turns, capacity),
         out_shape=total,
@@ -328,7 +333,7 @@
         compiler_params=PARAMS,
         cost_estimate=cost(1),
         name="finish_blocks",
-    )(here, ids, passed_ids, own_sum, other_grads, *other_returned)
+    )(here, near_ids, passed_ids, own_sum, other_grads, *other_returned)
 
 
 def solution(mesh):

time: 41.6 us -> 41.7 us (level)
  waiting for transfers between devices: 4.18 us -> 3.55 us
    ppermute x12, waiting for transfers between devices: 2.01 us -> 1.37 us  [exchange(): return lax.ppermute(x, ('tile', 'row'), pairs)]
    pallas_call x1, Pallas kernels: 2.65 us -> 3.28 us  [on_device(): pl.pallas_call(functools.partial(stage_kernel, tiles, capacity, blocks),...]
  transfers between devices with their start and end apart: 20 -> 20, of which waited for: 6 -> 5; matrix products, arithmetic and copies ran while one was open for 0% -> 0% of each run, Pallas kernels for 32% -> 33%
where the time goes in v6:
time: 41.7 us; the launch traced here: 41.4 us
  starting transfers between devices  20.6 us (49%)
  Pallas kernels  17 us (41%)
  waiting for transfers between devices  3.55 us (9%)
    ppermute x12, starting transfers between devices, exchange(): return lax.ppermute(x, ('tile', 'row'), pairs)  14 us
    ppermute x8, starting transfers between devices, swap_rows(): return lax.ppermute(x, 'row', [(0, 1), (1, 0)])  6.6 us
    pallas_call x1, Pallas kernels, on_device(): pl.pallas_call(functools.partial(plan_kernel, tiles, capacity, blocks), o...  4.27 us
    pallas_call x1, Pallas kernels, on_device(): pl.pallas_call(functools.partial(stage_kernel, tiles, capacity, blocks),...  3.28 us
    pallas_call x1, Pallas kernels, on_device(): pl.pallas_call(functools.partial(predict_kernel, capacity), out_shape=jax...  2.37 us
    ppermute x8, waiting for transfers between devices, swap_rows(): return lax.ppermute(x, 'row', [(0, 1), (1, 0)])  2.18 us
    pallas_call x1, Pallas kernels, on_device(): pl.pallas_call(functools.partial(back_kernel, capacity), out_shape=[chunk...  1.71 us
    pallas_call x1, Pallas kernels, on_device(): pl.pallas_call(functools.partial(finish_kernel, turns, capacity), out_sha...  1.63 us
  transfers between devices with their start and end apart: 20, of which 5 were waited for; matrix products, arithmetic and copies ran while one was open for 0% of the time, Pallas kernels for 33%

profile of v6, /device:TPU:0, one launch (start us, length us, event | category | flops | bytes accessed | tf_op | source)
XLA Modules:
  0.0 41.4 jit_solution(7404547393411800302)
XLA Ops:
  0.0 0.5 %collective-permute-start.3 = (bf16[256,12288]{1,0:T(8,128)(2,1)}, bf16[256,12288]{1,0:T(8,128)(2,1)}, u32[]{:S(2)}, u32[]{:S(2)}) collective-permute-start(bf16[256,12288]{1,0:T(8,128)(2,1)} %bitcast.3), channel_id=1, source_target_pairs={{0,1},{1,0},{2,3},{3,2},{4,5},{5,4},{6,7},{7,6},{8,9},{9,8},{10,11... | collective-permute-start | bytes 18874376 | tf_op jit(solution)/shard_map/ppermute | solution.py:18
  0.5 2.5 %collective-permute-start.4 = (bf16[16,32,384]{2,1,0:T(8,128)(2,1)}, bf16[16,32,384]{2,1,0:T(8,128)(2,1)S(1)}, u32[]{:S(2)}, u32[]{:S(2)}) collective-permute-start(bf16[16,32,384]{2,1,0:T(8,128)(2,1)} %own_ref.1), channel_id=1, source_target_pairs={{0,2},{1,13},{2,0},{3,15},{4,6},{5,9},{6,4},{7,11},{8,10},{9,5},{1... | collective-permute-start | bytes 1179656 | tf_op jit(solution)/shard_map/ppermute | solution.py:24
  3.0 1.5 %collective-permute-start = (s32[1,32]{1,0:T(1,128)}, s32[1,32]{1,0:T(1,128)S(1)}, u32[]{:S(2)}, u32[]{:S(2)}) collective-permute-start(s32[1,32]{1,0:T(1,128)} %list_ref.1), channel_id=1, source_target_pairs={{0,6},{1,7},{2,4},{3,5},{4,2},{5,3},{6,0},{7,1},{8,14},{9,15},{10,... | collective-permute-start | bytes 392 | tf_op jit(solution)/shard_map/ppermute | solution.py:24
  4.6 1.9 %collective-permute-start.2 = (s32[1,32]{1,0:T(1,128)}, s32[1,32]{1,0:T(1,128)S(1)}, u32[]{:S(2)}, u32[]{:S(2)}) collective-permute-start(s32[1,32]{1,0:T(1,128)} %list_ref.1), channel_id=1, source_target_pairs={{0,2},{1,3},{2,0},{3,1},{4,6},{5,7},{6,4},{7,5},{8,10},{9,11},{10,... | collective-permute-start | bytes 392 | tf_op jit(solution)/shard_map/ppermute | solution.py:24
  6.5 4.3 %plan_columns.1 = (s32[17]{0:T(128)S(1)}, s32[17]{0:T(128)S(1)}, s32[9]{0:T(128)S(1)}, bf16[256,6144]{1,0:T(8,128)(2,1)S(1)}) custom-call(s32[2]{0:T(128)S(1)} %pad_add_fusion.here_ref, s32[1,32]{1,0:T(1,128)} %list_ref.1, s32[1,32]{1,0:T(1,128)} %mask_ref.1, bf16[256,12288]{1,0:T(8,128)(2,1)} %bitcast.4), custom_call_target="tpu_custom_call" | custom-call | bytes 1 | tf_op jit(solution)/shard_map/plan_columns/pallas_call | solution.py:232
  10.8 1.5 %search_lists.1.ids_ref = s32[17]{0:T(128)S(1)} custom-call(s32[2]{0:T(128)S(1)} %pad_add_fusion.here_ref, s32[9]{0:T(128)S(1)} %get-tuple-element.23.own_ids_ref, s32[1,32]{1,0:T(1,128)S(1)} %collective-permute-done.refs_0_, s32[1,32]{1,0:T(1,128)S(1)} %collective-permute-done.1.refs_1_, s32[1,32]{1,0:T(1,128)S(1)} %collective-permute-done.2.refs_2_), custom_call_target="tpu_custom_call" | custom-call | bytes 1 | tf_op jit(solution)/shard_map/search_lists/pallas_call | solution.py:249
  12.3 1.6 %select_blocks.1 = (bf16[4,32,384]{2,1,0:T(8,128)(2,1)S(1)}, bf16[4,32,384]{2,1,0:T(8,128)(2,1)S(1)}, bf16[4,32,384]{2,1,0:T(8,128)(2,1)S(1)}, bf16[4,32,384]{2,1,0:T(8,128)(2,1)S(1)}) custom-call(s32[2]{0:T(128)S(1)} %pad_add_fusion.here_ref, s32[17]{0:T(128)S(1)} %search_lists.1.ids_ref, bf16[16,32,384]{2,1,0:T(8,128)(2,1)} %own_ref.1, ...), custom_call_target="tpu_custom_call" | custom-call | bytes 1 | tf_op jit(solution)/shard_map/select_blocks/pallas_call | solution.py:258
  13.9 1.6 %collective-permute-start.5 = (bf16[4,32,384]{2,1,0:T(8,128)(2,1)S(1)}, bf16[4,32,384]{2,1,0:T(8,128)(2,1)S(1)}, u32[]{:S(2)}, u32[]{:S(2)}) collective-permute-start(bf16[4,32,384]{2,1,0:T(8,128)(2,1)S(1)} %get-tuple-element.29), channel_id=1, source_target_pairs={{0,6},{1,7},{2,4},{3,5},{4,2},{5,3},{6,0},{7,1},{8,14},{9,15},{10,... | collective-permute-start | bytes 294920 | tf_op jit(solution)/shard_map/ppermute | solution.py:24
  15.5 0.1 collective-permute-start.6
  15.7 1.9 %collective-permute-start.7 = (bf16[4,32,384]{2,1,0:T(8,128)(2,1)S(1)}, bf16[4,32,384]{2,1,0:T(8,128)(2,1)S(1)}, u32[]{:S(2)}, u32[]{:S(2)}) collective-permute-start(bf16[4,32,384]{2,1,0:T(8,128)(2,1)S(1)} %get-tuple-element.31), channel_id=1, source_target_pairs={{0,2},{1,3},{2,0},{3,1},{4,6},{5,7},{6,4},{7,5},{8,10},{9,11},{10,... | collective-permute-start | bytes 294920 | tf_op jit(solution)/shard_map/ppermute | solution.py:24
  17.5 0.2 collective-permute-start.8
  17.7 3.3 %stage_columns.1 = (bf16[256,6144]{1,0:T(8,128)(2,1)S(1)}, s32[17]{0:T(128)S(1)}) custom-call(s32[2]{0:T(128)S(1)} %pad_add_fusion.here_ref, s32[9]{0:T(128)S(1)} %get-tuple-element.23.own_ids_ref, s32[17]{0:T(128)S(1)} %get-tuple-element.24.column_ref, s32[1,32]{1,0:T(1,128)S(1)} %collective-permute-done.refs_0_, ...), custom_call_target="tpu_custom_call" | custom-call | bytes 1 | tf_op jit(solution)/shard_map/stage_columns/pallas_call | solution.py:273
  21.0 0.2 collective-permute-done.6.refs_1_
  21.2 1.2 %collective-permute-done.7.refs_2_ = bf16[4,32,384]{2,1,0:T(8,128)(2,1)S(1)} collective-permute-done((bf16[4,32,384]{2,1,0:T(8,128)(2,1)S(1)}, bf16[4,32,384]{2,1,0:T(8,128)(2,1)S(1)}, u32[]{:S(2)}, u32[]{:S(2)}) %collective-permute-start.7) | collective-permute-done | bytes 98336 | tf_op jit(solution)/shard_map/ppermute | solution.py:24
  22.3 2.4 %predict.1.mine_ref = f32[2,40,256]{2,1,0:T(8,128)S(1)} custom-call(s32[17]{0:T(128)S(1)} %get-tuple-element.26.live_ref, bf16[256,6144]{1,0:T(8,128)(2,1)S(1)} %get-tuple-element.27.own_ref, bf16[256,6144]{1,0:T(8,128)(2,1)S(1)} %get-tuple-element.28.other_ref, f32[1,256]{1,0:T(1,128)S(1)} %copy-done, ...), custom_call_target="tpu_custom_call" | custom-call | bytes 1 | tf_op jit(solution)/shard_map/predict/pallas_call | solution.py:285
  24.7 0.2 collective-permute-start.9
  24.9 1.2 %collective-permute-done.9.theirs_ref = f32[2,40,256]{2,1,0:T(8,128)S(1)} collective-permute-done((f32[2,40,256]{2,1,0:T(8,128)S(1)}, f32[2,40,256]{2,1,0:T(8,128)S(1)}, u32[]{:S(2)}, u32[]{:S(2)}) %collective-permute-start.9) | collective-permute-done | bytes 81952 | tf_op jit(solution)/shard_map/ppermute | solution.py:18
  26.0 1.7 %back_project.1 = (bf16[4,32,384]{2,1,0:T(8,128)(2,1)S(1)}, bf16[4,32,384]{2,1,0:T(8,128)(2,1)S(1)}, bf16[4,32,384]{2,1,0:T(8,128)(2,1)S(1)}, bf16[4,32,384]{2,1,0:T(8,128)(2,1)S(1)}) custom-call(s32[17]{0:T(128)S(1)} %get-tuple-element.26.live_ref, bf16[256,6144]{1,0:T(8,128)(2,1)S(1)} %get-tuple-element.27.own_ref, ...), custom_call_target="tpu_custom_call" | custom-call | bytes 1 | tf_op jit(solution)/shard_map/back_project/pallas_call | solution.py:298
  27.8 1.9 %collective-permute-start.10 = (bf16[4,32,384]{2,1,0:T(8,128)(2,1)S(1)}, bf16[4,32,384]{2,1,0:T(8,128)(2,1)S(1)}, u32[]{:S(2)}, u32[]{:S(2)}) collective-permute-start(bf16[4,32,384]{2,1,0:T(8,128)(2,1)S(1)} %get-tuple-element.34), channel_id=1, source_target_pairs={{0,6},{1,11},{2,4},{3,9},{4,2},{5,15},{6,0},{7,13},{8,14},{9,3},{1... | collective-permute-start | bytes 294920 | tf_op jit(solution)/shard_map/ppermute | solution.py:24
  29.6 0.4 collective-permute-start.12
  30.0 1.3 %collective-permute-start.13 = (bf16[4,32,384]{2,1,0:T(8,128)(2,1)S(1)}, bf16[4,32,384]{2,1,0:T(8,128)(2,1)S(1)}, u32[]{:S(2)}, u32[]{:S(2)}) collective-permute-start(bf16[4,32,384]{2,1,0:T(8,128)(2,1)S(1)} %get-tuple-element.40), channel_id=1, source_target_pairs={{0,2},{1,15},{2,0},{3,13},{4,6},{5,11},{6,4},{7,9},{8,10},{9,7},{1... | collective-permute-start | bytes 294920 | tf_op jit(solution)/shard_map/ppermute | solution.py:24
  31.3 0.7 %collective-permute-start.14 = (bf16[4,32,384]{2,1,0:T(8,128)(2,1)S(1)}, bf16[4,32,384]{2,1,0:T(8,128)(2,1)S(1)}, u32[]{:S(2)}, u32[]{:S(2)}) collective-permute-start(bf16[4,32,384]{2,1,0:T(8,128)(2,1)S(1)} %get-tuple-element.37.refs_0_), channel_id=1, source_target_pairs={{0,2},{1,13},{2,0},{3,15},{4,6},{5,9},{6,4},{7,11},{8,10},{9,5},{1... | collective-permute-start | bytes 294920 | tf_op jit(solution)/shard_map/ppermute | solution.py:24
  32.1 2.5 %collective-permute-start.11 = (s32[17]{0:T(128)S(1)}, s32[17]{0:T(128)S(1)}, u32[]{:S(2)}, u32[]{:S(2)}) collective-permute-start(s32[17]{0:T(128)S(1)} %collective-permute-done.8.far_ref), channel_id=1, source_target_pairs={{0,1},{1,0},{2,3},{3,2},{4,5},{5,4},{6,7},{7,6},{8,9},{9,8},{10,11... | collective-permute-start | bytes 212 | tf_op jit(solution)/shard_map/ppermute | solution.py:18
  34.5 0.8 %collective-permute-done.11.far_ref = s32[17]{0:T(128)S(1)} collective-permute-done((s32[17]{0:T(128)S(1)}, s32[17]{0:T(128)S(1)}, u32[]{:S(2)}, u32[]{:S(2)}) %collective-permute-start.11) | collective-permute-done | bytes 100 | tf_op jit(solution)/shard_map/ppermute | solution.py:18
  35.3 0.3 collective-permute-start.15
  35.7 0.2 collective-permute-start.16
  35.9 0.3 collective-permute-start.17
  36.2 1.9 %collective-permute-start.18 = (bf16[4,32,384]{2,1,0:T(8,128)(2,1)S(1)}, bf16[4,32,384]{2,1,0:T(8,128)(2,1)S(1)}, u32[]{:S(2)}, u32[]{:S(2)}) collective-permute-start(bf16[4,32,384]{2,1,0:T(8,128)(2,1)S(1)} %collective-permute-done.13.refs_3_), channel_id=1, source_target_pairs={{0,1},{1,0},{2,3},{3,2},{4,5},{5,4},{6,7},{7,6},{8,9},{9,8},{10,11... | collective-permute-start | bytes 294920 | tf_op jit(solution)/shard_map/ppermute | solution.py:18
  38.0 0.8 %collective-permute-start.19 = (bf16[4,32,384]{2,1,0:T(8,128)(2,1)S(1)}, bf16[4,32,384]{2,1,0:T(8,128)(2,1)S(1)}, u32[]{:S(2)}, u32[]{:S(2)}) collective-permute-start(bf16[4,32,384]{2,1,0:T(8,128)(2,1)S(1)} %collective-permute-done.14.refs_4_), channel_id=1, source_target_pairs={{0,1},{1,0},{2,3},{3,2},{4,5},{5,4},{6,7},{7,6},{8,9},{9,8},{10,11... | collective-permute-start | bytes 294920 | tf_op jit(solution)/shard_map/ppermute | solution.py:18
  38.9 0.7 %sum_blocks.1.own_ref = f32[16,32,384]{2,1,0:T(8,128)S(1)} custom-call(s32[2]{0:T(128)S(1)} %pad_add_fusion.here_ref, s32[17]{0:T(128)S(1)} %get-tuple-element.25.near_ref, s32[17]{0:T(128)S(1)} %collective-permute-done.8.far_ref, bf16[4,32,384]{2,1,0:T(8,128)(2,1)S(1)} %get-tuple-element.37.refs_0_, ...), custom_call_target="tpu_custom_call" | custom-call | bytes 1 | tf_op jit(solution)/shard_map/sum_blocks/pallas_call | solution.py:315
  39.6 0.2 collective-permute-done.19.refs_4_
  39.8 1.6 %finish_blocks.1 = f32[16,32,384]{2,1,0:T(8,128)} custom-call(s32[2]{0:T(128)S(1)} %pad_add_fusion.here_ref, s32[17]{0:T(128)S(1)} %get-tuple-element.25.near_ref, s32[17]{0:T(128)S(1)} %collective-permute-done.11.far_ref, f32[16,32,384]{2,1,0:T(8,128)S(1)} %sum_blocks.1.own_ref, bf16[4,32,384]{2,1,0:T(8,128)(2,1)S(1)} %collective-permute-done.15.refs_0_, ...), custom_call_target="tpu_custom_call" | custom-call | bytes 1 | tf_op jit(solution)/shard_map/finish_blocks/pallas_call | solution.py:324
  (19 shorter events, 0.2 us)
Async XLA Ops:
  0.0 17.7 %collective-permute-start.3 = (bf16[256,12288]{1,0:T(8,128)(2,1)}, bf16[256,12288]{1,0:T(8,128)(2,1)}, u32[]{:S(2)}, u32[]{:S(2)}) collective-permute-start(bf16[256,12288]{1,0:T(8,128)(2,1)} %bitcast.3), channel_id=1, source_target_pairs={{0,1},{1,0},{2,3},{3,2},{4,5},{5,4},{6,7},{7,6},{8,9},{9,8},{10,11... | collective-permute-start | bytes 18874376 | tf_op jit(solution)/shard_map/ppermute | solution.py:18
  0.5 11.9 %collective-permute-start.4 = (bf16[16,32,384]{2,1,0:T(8,128)(2,1)}, bf16[16,32,384]{2,1,0:T(8,128)(2,1)S(1)}, u32[]{:S(2)}, u32[]{:S(2)}) collective-permute-start(bf16[16,32,384]{2,1,0:T(8,128)(2,1)} %own_ref.1), channel_id=1, source_target_pairs={{0,2},{1,13},{2,0},{3,15},{4,6},{5,9},{6,4},{7,11},{8,10},{9,5},{1... | collective-permute-start | bytes 1179656 | tf_op jit(solution)/shard_map/ppermute | solution.py:24
  3.0 7.8 %collective-permute-start = (s32[1,32]{1,0:T(1,128)}, s32[1,32]{1,0:T(1,128)S(1)}, u32[]{:S(2)}, u32[]{:S(2)}) collective-permute-start(s32[1,32]{1,0:T(1,128)} %list_ref.1), channel_id=1, source_target_pairs={{0,6},{1,7},{2,4},{3,5},{4,2},{5,3},{6,0},{7,1},{8,14},{9,15},{10,... | collective-permute-start | bytes 392 | tf_op jit(solution)/shard_map/ppermute | solution.py:24
  4.5 6.3 %collective-permute-start.1 = (s32[1,32]{1,0:T(1,128)}, s32[1,32]{1,0:T(1,128)S(1)}, u32[]{:S(2)}, u32[]{:S(2)}) collective-permute-start(s32[1,32]{1,0:T(1,128)} %list_ref.1), channel_id=1, source_target_pairs={{0,4},{1,5},{2,6},{3,7},{4,0},{5,1},{6,2},{7,3},{8,12},{9,13},{10,... | collective-permute-start | bytes 392 | tf_op jit(solution)/shard_map/ppermute | solution.py:24
  4.6 6.3 %collective-permute-start.2 = (s32[1,32]{1,0:T(1,128)}, s32[1,32]{1,0:T(1,128)S(1)}, u32[]{:S(2)}, u32[]{:S(2)}) collective-permute-start(s32[1,32]{1,0:T(1,128)} %list_ref.1), channel_id=1, source_target_pairs={{0,2},{1,3},{2,0},{3,1},{4,6},{5,7},{6,4},{7,5},{8,10},{9,11},{10,... | collective-permute-start | bytes 392 | tf_op jit(solution)/shard_map/ppermute | solution.py:24
  6.5 15.8 %copy-start = (f32[1,256]{1,0:T(1,128)S(1)}, f32[1,256]{1,0:T(1,128)}, u32[]{:S(2)}) copy-start(f32[1,256]{1,0:T(1,128)} %weight_ref.1) | copy-start | bytes 3076
  13.9 7.0 %collective-permute-start.5 = (bf16[4,32,384]{2,1,0:T(8,128)(2,1)S(1)}, bf16[4,32,384]{2,1,0:T(8,128)(2,1)S(1)}, u32[]{:S(2)}, u32[]{:S(2)}) collective-permute-start(bf16[4,32,384]{2,1,0:T(8,128)(2,1)S(1)} %get-tuple-element.29), channel_id=1, source_target_pairs={{0,6},{1,7},{2,4},{3,5},{4,2},{5,3},{6,0},{7,1},{8,14},{9,15},{10,... | collective-permute-start | bytes 294920 | tf_op jit(solution)/shard_map/ppermute | solution.py:24
  15.5 5.6 %collective-permute-start.6 = (bf16[4,32,384]{2,1,0:T(8,128)(2,1)S(1)}, bf16[4,32,384]{2,1,0:T(8,128)(2,1)S(1)}, u32[]{:S(2)}, u32[]{:S(2)}) collective-permute-start(bf16[4,32,384]{2,1,0:T(8,128)(2,1)S(1)} %get-tuple-element.30), channel_id=1, source_target_pairs={{0,4},{1,5},{2,6},{3,7},{4,0},{5,1},{6,2},{7,3},{8,12},{9,13},{10,... | collective-permute-start | bytes 294920 | tf_op jit(solution)/shard_map/ppermute | solution.py:24
  15.7 6.7 %collective-permute-start.7 = (bf16[4,32,384]{2,1,0:T(8,128)(2,1)S(1)}, bf16[4,32,384]{2,1,0:T(8,128)(2,1)S(1)}, u32[]{:S(2)}, u32[]{:S(2)}) collective-permute-start(bf16[4,32,384]{2,1,0:T(8,128)(2,1)S(1)} %get-tuple-element.31), channel_id=1, source_target_pairs={{0,2},{1,3},{2,0},{3,1},{4,6},{5,7},{6,4},{7,5},{8,10},{9,11},{10,... | collective-permute-start | bytes 294920 | tf_op jit(solution)/shard_map/ppermute | solution.py:24
  17.5 7.2 %collective-permute-start.8 = (s32[17]{0:T(128)S(1)}, s32[17]{0:T(128)S(1)}, u32[]{:S(2)}, u32[]{:S(2)}) collective-permute-start(s32[17]{0:T(128)S(1)} %search_lists.1.ids_ref), channel_id=1, source_target_pairs={{0,2},{1,13},{2,0},{3,15},{4,6},{5,9},{6,4},{7,11},{8,10},{9,5},{1... | collective-permute-start | bytes 212 | tf_op jit(solution)/shard_map/ppermute | solution.py:24
  24.7 1.3 %collective-permute-start.9 = (f32[2,40,256]{2,1,0:T(8,128)S(1)}, f32[2,40,256]{2,1,0:T(8,128)S(1)}, u32[]{:S(2)}, u32[]{:S(2)}) collective-permute-start(f32[2,40,256]{2,1,0:T(8,128)S(1)} %predict.1.mine_ref), channel_id=1, source_target_pairs={{0,1},{1,0},{2,3},{3,2},{4,5},{5,4},{6,7},{7,6},{8,9},{9,8},{10,11... | collective-permute-start | bytes 245768 | tf_op jit(solution)/shard_map/ppermute | solution.py:18
  27.8 7.9 %collective-permute-start.10 = (bf16[4,32,384]{2,1,0:T(8,128)(2,1)S(1)}, bf16[4,32,384]{2,1,0:T(8,128)(2,1)S(1)}, u32[]{:S(2)}, u32[]{:S(2)}) collective-permute-start(bf16[4,32,384]{2,1,0:T(8,128)(2,1)S(1)} %get-tuple-element.34), channel_id=1, source_target_pairs={{0,6},{1,11},{2,4},{3,9},{4,2},{5,15},{6,0},{7,13},{8,14},{9,3},{1... | collective-permute-start | bytes 294920 | tf_op jit(solution)/shard_map/ppermute | solution.py:24
  29.6 6.2 %collective-permute-start.12 = (bf16[4,32,384]{2,1,0:T(8,128)(2,1)S(1)}, bf16[4,32,384]{2,1,0:T(8,128)(2,1)S(1)}, u32[]{:S(2)}, u32[]{:S(2)}) collective-permute-start(bf16[4,32,384]{2,1,0:T(8,128)(2,1)S(1)} %get-tuple-element.39), channel_id=1, source_target_pairs={{0,4},{1,9},{2,6},{3,11},{4,0},{5,13},{6,2},{7,15},{8,12},{9,1},{1... | collective-permute-start | bytes 294920 | tf_op jit(solution)/shard_map/ppermute | solution.py:24
  30.0 6.1 %collective-permute-start.13 = (bf16[4,32,384]{2,1,0:T(8,128)(2,1)S(1)}, bf16[4,32,384]{2,1,0:T(8,128)(2,1)S(1)}, u32[]{:S(2)}, u32[]{:S(2)}) collective-permute-start(bf16[4,32,384]{2,1,0:T(8,128)(2,1)S(1)} %get-tuple-element.40), channel_id=1, source_target_pairs={{0,2},{1,15},{2,0},{3,13},{4,6},{5,11},{6,4},{7,9},{8,10},{9,7},{1... | collective-permute-start | bytes 294920 | tf_op jit(solution)/shard_map/ppermute | solution.py:24
  31.3 6.7 %collective-permute-start.14 = (bf16[4,32,384]{2,1,0:T(8,128)(2,1)S(1)}, bf16[4,32,384]{2,1,0:T(8,128)(2,1)S(1)}, u32[]{:S(2)}, u32[]{:S(2)}) collective-permute-start(bf16[4,32,384]{2,1,0:T(8,128)(2,1)S(1)} %get-tuple-element.37.refs_0_), channel_id=1, source_target_pairs={{0,2},{1,13},{2,0},{3,15},{4,6},{5,9},{6,4},{7,11},{8,10},{9,5},{1... | collective-permute-start | bytes 294920 | tf_op jit(solution)/shard_map/ppermute | solution.py:24
  32.1 3.3 %collective-permute-start.11 = (s32[17]{0:T(128)S(1)}, s32[17]{0:T(128)S(1)}, u32[]{:S(2)}, u32[]{:S(2)}) collective-permute-start(s32[17]{0:T(128)S(1)} %collective-permute-done.8.far_ref), channel_id=1, source_target_pairs={{0,1},{1,0},{2,3},{3,2},{4,5},{5,4},{6,7},{7,6},{8,9},{9,8},{10,11... | collective-permute-start | bytes 212 | tf_op jit(solution)/shard_map/ppermute | solution.py:18
  35.3 4.2 %collective-permute-start.15 = (bf16[4,32,384]{2,1,0:T(8,128)(2,1)S(1)}, bf16[4,32,384]{2,1,0:T(8,128)(2,1)S(1)}, u32[]{:S(2)}, u32[]{:S(2)}) collective-permute-start(bf16[4,32,384]{2,1,0:T(8,128)(2,1)S(1)} %get-tuple-element.37.refs_0_), channel_id=1, source_target_pairs={{0,1},{1,0},{2,3},{3,2},{4,5},{5,4},{6,7},{7,6},{8,9},{9,8},{10,11... | collective-permute-start | bytes 294920 | tf_op jit(solution)/shard_map/ppermute | solution.py:18
  35.7 3.9 %collective-permute-start.16 = (bf16[4,32,384]{2,1,0:T(8,128)(2,1)S(1)}, bf16[4,32,384]{2,1,0:T(8,128)(2,1)S(1)}, u32[]{:S(2)}, u32[]{:S(2)}) collective-permute-start(bf16[4,32,384]{2,1,0:T(8,128)(2,1)S(1)} %collective-permute-done.10.refs_1_), channel_id=1, source_target_pairs={{0,1},{1,0},{2,3},{3,2},{4,5},{5,4},{6,7},{7,6},{8,9},{9,8},{10,11... | collective-permute-start | bytes 294920 | tf_op jit(solution)/shard_map/ppermute | solution.py:18
  35.9 3.7 %collective-permute-start.17 = (bf16[4,32,384]{2,1,0:T(8,128)(2,1)S(1)}, bf16[4,32,384]{2,1,0:T(8,128)(2,1)S(1)}, u32[]{:S(2)}, u32[]{:S(2)}) collective-permute-start(bf16[4,32,384]{2,1,0:T(8,128)(2,1)S(1)} %collective-permute-done.12.refs_2_), channel_id=1, source_target_pairs={{0,1},{1,0},{2,3},{3,2},{4,5},{5,4},{6,7},{7,6},{8,9},{9,8},{10,11... | collective-permute-start | bytes 294920 | tf_op jit(solution)/shard_map/ppermute | solution.py:18
  36.2 3.4 %collective-permute-start.18 = (bf16[4,32,384]{2,1,0:T(8,128)(2,1)S(1)}, bf16[4,32,384]{2,1,0:T(8,128)(2,1)S(1)}, u32[]{:S(2)}, u32[]{:S(2)}) collective-permute-start(bf16[4,32,384]{2,1,0:T(8,128)(2,1)S(1)} %collective-permute-done.13.refs_3_), channel_id=1, source_target_pairs={{0,1},{1,0},{2,3},{3,2},{4,5},{5,4},{6,7},{7,6},{8,9},{9,8},{10,11... | collective-permute-start | bytes 294920 | tf_op jit(solution)/shard_map/ppermute | solution.py:18
  38.0 1.8 %collective-permute-start.19 = (bf16[4,32,384]{2,1,0:T(8,128)(2,1)S(1)}, bf16[4,32,384]{2,1,0:T(8,128)(2,1)S(1)}, u32[]{:S(2)}, u32[]{:S(2)}) collective-permute-start(bf16[4,32,384]{2,1,0:T(8,128)(2,1)S(1)} %collective-permute-done.14.refs_4_), channel_id=1, source_target_pairs={{0,1},{1,0},{2,3},{3,2},{4,5},{5,4},{6,7},{7,6},{8,9},{9,8},{10,11... | collective-permute-start | bytes 294920 | tf_op jit(solution)/shard_map/ppermute | solution.py:18

commit v7 on v6

--- a/solution.py
+++ b/solution.py
@@ -128,10 +128,10 @@
             out_ref[c] = dirs_ref[ids_ref[turn * capacity + c]]
 
 
-def predict_kernel(capacity, live_ref, own_ref, other_ref, weight_ref, *refs):
+def predict_kernel(turns, capacity, live_ref, own_ref, other_ref, weight_ref, *refs):
     *chunks, out_ref, flat_ref = refs
     vecs, width = chunks[0].shape[1:]
-    for turn, chunk_ref in enumerate(chunks):
+    for turn, chunk_ref in zip(turns, chunks):
         for c in range(capacity):
             slot = turn * capacity + c
             live = live_ref[slot].astype(jnp.float32)
@@ -221,6 +221,7 @@
     slots, mirror = steps * capacity, tiles - 2
     here = jnp.stack([lax.axis_index("tile"), lax.axis_index("row")]).astype(jnp.int32)
     order = list(reversed(range(steps)))
+    came = [0] + list(range(steps - 2, 0, -1)) + [steps - 1]
 
     own_sens = in_hbm(sensitivity[0])
     other_sens = in_hbm(swap_rows(sensitivity[0]))
@@ -283,7 +284,7 @@
 
     far_ids = exchange(ids, {0: 1, 1: mirror})
     partial = pl.pallas_call(
-        functools.partial(predict_kernel, capacity),
+        functools.partial(predict_kernel, came, capacity),
         out_shape=jax.ShapeDtypeStruct((2, vecs + 8, rows), jnp.float32),
         in_specs=[SMEM] + [VMEM] * (3 + steps),
         out_specs=VMEM,
@@ -291,7 +292,7 @@
         compiler_params=PARAMS,
         cost_estimate=cost(1),
         name="predict",
-    )(live, own_sens, other_sens, data_weight, *fetched)
+    )(live, own_sens, other_sens, data_weight, *[fetched[i] for i in came])
     partial, far_ids = lax.optimization_barrier((partial, far_ids))
     other_partial = swap_rows(partial)
 

time: 41.7 us -> 41.6 us (level)
  transfers between devices with their start and end apart: 20 -> 20, of which waited for: 5 -> 4; matrix products, arithmetic and copies ran while one was open for 0% -> 0% of each run, Pallas kernels for 33% -> 33%
where the time goes in v7:
time: 41.6 us; the launch traced here: 41.4 us
  starting transfers between devices  20.5 us (49%)
  Pallas kernels  17 us (41%)
  waiting for transfers between devices  3.63 us (9%)
    ppermute x12, starting transfers between devices, exchange(): return lax.ppermute(x, ('tile', 'row'), pairs)  14 us
    ppermute x8, starting transfers between devices, swap_rows(): return lax.ppermute(x, 'row', [(0, 1), (1, 0)])  6.56 us
    pallas_call x1, Pallas kernels, on_device(): pl.pallas_call(functools.partial(plan_kernel, tiles, capacity, blocks), o...  4.27 us
    pallas_call x1, Pallas kernels, on_device(): pl.pallas_call(functools.partial(stage_kernel, tiles, capacity, blocks),...  3.28 us
    pallas_call x1, Pallas kernels, on_device(): pl.pallas_call(functools.partial(predict_kernel, came, capacity), out_sha...  2.37 us
    ppermute x8, waiting for transfers between devices, swap_rows(): return lax.ppermute(x, 'row', [(0, 1), (1, 0)])  2.22 us
    pallas_call x1, Pallas kernels, on_device(): pl.pallas_call(functools.partial(back_kernel, capacity), out_shape=[chunk...  1.72 us
    pallas_call x1, Pallas kernels, on_device(): pl.pallas_call(functools.partial(finish_kernel, turns, capacity), out_sha...  1.63 us
  transfers between devices with their start and end apart: 20, of which 4 were waited for; matrix products, arithmetic and copies ran while one was open for 0% of the time, Pallas kernels for 33%

profile of v7, /device:TPU:0, one launch (start us, length us, event | category | flops | bytes accessed | tf_op | source)
XLA Modules:
  0.0 41.4 jit_solution(11919919876951529437)
XLA Ops:
  0.0 0.5 %collective-permute-start.3 = (bf16[256,12288]{1,0:T(8,128)(2,1)}, bf16[256,12288]{1,0:T(8,128)(2,1)}, u32[]{:S(2)}, u32[]{:S(2)}) collective-permute-start(bf16[256,12288]{1,0:T(8,128)(2,1)} %bitcast.3), channel_id=1, source_target_pairs={{0,1},{1,0},{2,3},{3,2},{4,5},{5,4},{6,7},{7,6},{8,9},{9,8},{10,11... | collective-permute-start | bytes 18874376 | tf_op jit(solution)/shard_map/ppermute | solution.py:18
  0.5 2.5 %collective-permute-start.4 = (bf16[16,32,384]{2,1,0:T(8,128)(2,1)}, bf16[16,32,384]{2,1,0:T(8,128)(2,1)S(1)}, u32[]{:S(2)}, u32[]{:S(2)}) collective-permute-start(bf16[16,32,384]{2,1,0:T(8,128)(2,1)} %own_ref.1), channel_id=1, source_target_pairs={{0,2},{1,13},{2,0},{3,15},{4,6},{5,9},{6,4},{7,11},{8,10},{9,5},{1... | collective-permute-start | bytes 1179656 | tf_op jit(solution)/shard_map/ppermute | solution.py:24
  3.0 1.5 %collective-permute-start = (s32[1,32]{1,0:T(1,128)}, s32[1,32]{1,0:T(1,128)S(1)}, u32[]{:S(2)}, u32[]{:S(2)}) collective-permute-start(s32[1,32]{1,0:T(1,128)} %list_ref.1), channel_id=1, source_target_pairs={{0,6},{1,7},{2,4},{3,5},{4,2},{5,3},{6,0},{7,1},{8,14},{9,15},{10,... | collective-permute-start | bytes 392 | tf_op jit(solution)/shard_map/ppermute | solution.py:24
  4.6 1.9 %collective-permute-start.2 = (s32[1,32]{1,0:T(1,128)}, s32[1,32]{1,0:T(1,128)S(1)}, u32[]{:S(2)}, u32[]{:S(2)}) collective-permute-start(s32[1,32]{1,0:T(1,128)} %list_ref.1), channel_id=1, source_target_pairs={{0,2},{1,3},{2,0},{3,1},{4,6},{5,7},{6,4},{7,5},{8,10},{9,11},{10,... | collective-permute-start | bytes 392 | tf_op jit(solution)/shard_map/ppermute | solution.py:24
  6.5 0.1 pad_add_fusion.here_ref
  6.5 4.3 %plan_columns.1 = (s32[17]{0:T(128)S(1)}, s32[17]{0:T(128)S(1)}, s32[9]{0:T(128)S(1)}, bf16[256,6144]{1,0:T(8,128)(2,1)S(1)}) custom-call(s32[2]{0:T(128)S(1)} %pad_add_fusion.here_ref, s32[1,32]{1,0:T(1,128)} %list_ref.1, s32[1,32]{1,0:T(1,128)} %mask_ref.1, bf16[256,12288]{1,0:T(8,128)(2,1)} %bitcast.4), custom_call_target="tpu_custom_call" | custom-call | bytes 1 | tf_op jit(solution)/shard_map/plan_columns/pallas_call | solution.py:233
  10.8 1.5 %search_lists.1.ids_ref = s32[17]{0:T(128)S(1)} custom-call(s32[2]{0:T(128)S(1)} %pad_add_fusion.here_ref, s32[9]{0:T(128)S(1)} %get-tuple-element.23.own_ids_ref, s32[1,32]{1,0:T(1,128)S(1)} %collective-permute-done.refs_0_, s32[1,32]{1,0:T(1,128)S(1)} %collective-permute-done.1.refs_1_, s32[1,32]{1,0:T(1,128)S(1)} %collective-permute-done.2.refs_2_), custom_call_target="tpu_custom_call" | custom-call | bytes 1 | tf_op jit(solution)/shard_map/search_lists/pallas_call | solution.py:250
  12.3 1.6 %select_blocks.1 = (bf16[4,32,384]{2,1,0:T(8,128)(2,1)S(1)}, bf16[4,32,384]{2,1,0:T(8,128)(2,1)S(1)}, bf16[4,32,384]{2,1,0:T(8,128)(2,1)S(1)}, bf16[4,32,384]{2,1,0:T(8,128)(2,1)S(1)}) custom-call(s32[2]{0:T(128)S(1)} %pad_add_fusion.here_ref, s32[17]{0:T(128)S(1)} %search_lists.1.ids_ref, bf16[16,32,384]{2,1,0:T(8,128)(2,1)} %own_ref.1, ...), custom_call_target="tpu_custom_call" | custom-call | bytes 1 | tf_op jit(solution)/shard_map/select_blocks/pallas_call | solution.py:259
  13.9 1.6 %collective-permute-start.5 = (bf16[4,32,384]{2,1,0:T(8,128)(2,1)S(1)}, bf16[4,32,384]{2,1,0:T(8,128)(2,1)S(1)}, u32[]{:S(2)}, u32[]{:S(2)}) collective-permute-start(bf16[4,32,384]{2,1,0:T(8,128)(2,1)S(1)} %get-tuple-element.29), channel_id=1, source_target_pairs={{0,6},{1,7},{2,4},{3,5},{4,2},{5,3},{6,0},{7,1},{8,14},{9,15},{10,... | collective-permute-start | bytes 294920 | tf_op jit(solution)/shard_map/ppermute | solution.py:24
  15.5 1.5 %collective-permute-start.6 = (bf16[4,32,384]{2,1,0:T(8,128)(2,1)S(1)}, bf16[4,32,384]{2,1,0:T(8,128)(2,1)S(1)}, u32[]{:S(2)}, u32[]{:S(2)}) collective-permute-start(bf16[4,32,384]{2,1,0:T(8,128)(2,1)S(1)} %get-tuple-element.30), channel_id=1, source_target_pairs={{0,2},{1,3},{2,0},{3,1},{4,6},{5,7},{6,4},{7,5},{8,10},{9,11},{10,... | collective-permute-start | bytes 294920 | tf_op jit(solution)/shard_map/ppermute | solution.py:24
  17.0 0.5 %collective-permute-start.7 = (bf16[4,32,384]{2,1,0:T(8,128)(2,1)S(1)}, bf16[4,32,384]{2,1,0:T(8,128)(2,1)S(1)}, u32[]{:S(2)}, u32[]{:S(2)}) collective-permute-start(bf16[4,32,384]{2,1,0:T(8,128)(2,1)S(1)} %get-tuple-element.31), channel_id=1, source_target_pairs={{0,4},{1,5},{2,6},{3,7},{4,0},{5,1},{6,2},{7,3},{8,12},{9,13},{10,... | collective-permute-start | bytes 294920 | tf_op jit(solution)/shard_map/ppermute | solution.py:24
  17.5 0.2 collective-permute-start.8
  17.7 3.3 %stage_columns.1 = (bf16[256,6144]{1,0:T(8,128)(2,1)S(1)}, s32[17]{0:T(128)S(1)}) custom-call(s32[2]{0:T(128)S(1)} %pad_add_fusion.here_ref, s32[9]{0:T(128)S(1)} %get-tuple-element.23.own_ids_ref, s32[17]{0:T(128)S(1)} %get-tuple-element.24.column_ref, s32[1,32]{1,0:T(1,128)S(1)} %collective-permute-done.refs_0_, ...), custom_call_target="tpu_custom_call" | custom-call | bytes 1 | tf_op jit(solution)/shard_map/stage_columns/pallas_call | solution.py:274
  21.0 1.4 %collective-permute-done.6.refs_1_ = bf16[4,32,384]{2,1,0:T(8,128)(2,1)S(1)} collective-permute-done((bf16[4,32,384]{2,1,0:T(8,128)(2,1)S(1)}, bf16[4,32,384]{2,1,0:T(8,128)(2,1)S(1)}, u32[]{:S(2)}, u32[]{:S(2)}) %collective-permute-start.6) | collective-permute-done | bytes 98336 | tf_op jit(solution)/shard_map/ppermute | solution.py:24
  22.4 2.4 %predict.1.mine_ref = f32[2,40,256]{2,1,0:T(8,128)S(1)} custom-call(s32[17]{0:T(128)S(1)} %get-tuple-element.26.live_ref, bf16[256,6144]{1,0:T(8,128)(2,1)S(1)} %get-tuple-element.27.own_ref, bf16[256,6144]{1,0:T(8,128)(2,1)S(1)} %get-tuple-element.28.other_ref, f32[1,256]{1,0:T(1,128)S(1)} %copy-done, ...), custom_call_target="tpu_custom_call" | custom-call | bytes 1 | tf_op jit(solution)/shard_map/predict/pallas_call | solution.py:286
  24.8 0.1 collective-permute-start.9
  24.9 1.2 %collective-permute-done.9.theirs_ref = f32[2,40,256]{2,1,0:T(8,128)S(1)} collective-permute-done((f32[2,40,256]{2,1,0:T(8,128)S(1)}, f32[2,40,256]{2,1,0:T(8,128)S(1)}, u32[]{:S(2)}, u32[]{:S(2)}) %collective-permute-start.9) | collective-permute-done | bytes 81952 | tf_op jit(solution)/shard_map/ppermute | solution.py:18
  26.1 1.7 %back_project.1 = (bf16[4,32,384]{2,1,0:T(8,128)(2,1)S(1)}, bf16[4,32,384]{2,1,0:T(8,128)(2,1)S(1)}, bf16[4,32,384]{2,1,0:T(8,128)(2,1)S(1)}, bf16[4,32,384]{2,1,0:T(8,128)(2,1)S(1)}) custom-call(s32[17]{0:T(128)S(1)} %get-tuple-element.26.live_ref, bf16[256,6144]{1,0:T(8,128)(2,1)S(1)} %get-tuple-element.27.own_ref, ...), custom_call_target="tpu_custom_call" | custom-call | bytes 1 | tf_op jit(solution)/shard_map/back_project/pallas_call | solution.py:299
  27.8 1.8 %collective-permute-start.10 = (bf16[4,32,384]{2,1,0:T(8,128)(2,1)S(1)}, bf16[4,32,384]{2,1,0:T(8,128)(2,1)S(1)}, u32[]{:S(2)}, u32[]{:S(2)}) collective-permute-start(bf16[4,32,384]{2,1,0:T(8,128)(2,1)S(1)} %get-tuple-element.34), channel_id=1, source_target_pairs={{0,6},{1,11},{2,4},{3,9},{4,2},{5,15},{6,0},{7,13},{8,14},{9,3},{1... | collective-permute-start | bytes 294920 | tf_op jit(solution)/shard_map/ppermute | solution.py:24
  29.6 0.4 collective-permute-start.12
  30.0 1.4 %collective-permute-start.13 = (bf16[4,32,384]{2,1,0:T(8,128)(2,1)S(1)}, bf16[4,32,384]{2,1,0:T(8,128)(2,1)S(1)}, u32[]{:S(2)}, u32[]{:S(2)}) collective-permute-start(bf16[4,32,384]{2,1,0:T(8,128)(2,1)S(1)} %get-tuple-element.40), channel_id=1, source_target_pairs={{0,2},{1,15},{2,0},{3,13},{4,6},{5,11},{6,4},{7,9},{8,10},{9,7},{1... | collective-permute-start | bytes 294920 | tf_op jit(solution)/shard_map/ppermute | solution.py:24
  31.4 0.7 %collective-permute-start.14 = (bf16[4,32,384]{2,1,0:T(8,128)(2,1)S(1)}, bf16[4,32,384]{2,1,0:T(8,128)(2,1)S(1)}, u32[]{:S(2)}, u32[]{:S(2)}) collective-permute-start(bf16[4,32,384]{2,1,0:T(8,128)(2,1)S(1)} %get-tuple-element.37.refs_0_), channel_id=1, source_target_pairs={{0,2},{1,13},{2,0},{3,15},{4,6},{5,9},{6,4},{7,11},{8,10},{9,5},{1... | collective-permute-start | bytes 294920 | tf_op jit(solution)/shard_map/ppermute | solution.py:24
  32.1 2.5 %collective-permute-start.11 = (s32[17]{0:T(128)S(1)}, s32[17]{0:T(128)S(1)}, u32[]{:S(2)}, u32[]{:S(2)}) collective-permute-start(s32[17]{0:T(128)S(1)} %collective-permute-done.8.far_ref), channel_id=1, source_target_pairs={{0,1},{1,0},{2,3},{3,2},{4,5},{5,4},{6,7},{7,6},{8,9},{9,8},{10,11... | collective-permute-start | bytes 212 | tf_op jit(solution)/shard_map/ppermute | solution.py:18
  34.6 0.8 %collective-permute-done.11.far_ref = s32[17]{0:T(128)S(1)} collective-permute-done((s32[17]{0:T(128)S(1)}, s32[17]{0:T(128)S(1)}, u32[]{:S(2)}, u32[]{:S(2)}) %collective-permute-start.11) | collective-permute-done | bytes 100 | tf_op jit(solution)/shard_map/ppermute | solution.py:18
  35.4 0.3 collective-permute-start.15
  35.7 0.2 collective-permute-start.16
  35.9 0.3 collective-permute-start.17
  36.2 1.8 %collective-permute-start.18 = (bf16[4,32,384]{2,1,0:T(8,128)(2,1)S(1)}, bf16[4,32,384]{2,1,0:T(8,128)(2,1)S(1)}, u32[]{:S(2)}, u32[]{:S(2)}) collective-permute-start(bf16[4,32,384]{2,1,0:T(8,128)(2,1)S(1)} %collective-permute-done.13.refs_3_), channel_id=1, source_target_pairs={{0,1},{1,0},{2,3},{3,2},{4,5},{5,4},{6,7},{7,6},{8,9},{9,8},{10,11... | collective-permute-start | bytes 294920 | tf_op jit(solution)/shard_map/ppermute | solution.py:18
  38.0 0.8 %collective-permute-start.19 = (bf16[4,32,384]{2,1,0:T(8,128)(2,1)S(1)}, bf16[4,32,384]{2,1,0:T(8,128)(2,1)S(1)}, u32[]{:S(2)}, u32[]{:S(2)}) collective-permute-start(bf16[4,32,384]{2,1,0:T(8,128)(2,1)S(1)} %collective-permute-done.14.refs_4_), channel_id=1, source_target_pairs={{0,1},{1,0},{2,3},{3,2},{4,5},{5,4},{6,7},{7,6},{8,9},{9,8},{10,11... | collective-permute-start | bytes 294920 | tf_op jit(solution)/shard_map/ppermute | solution.py:18
  38.9 0.7 %sum_blocks.1.own_ref = f32[16,32,384]{2,1,0:T(8,128)S(1)} custom-call(s32[2]{0:T(128)S(1)} %pad_add_fusion.here_ref, s32[17]{0:T(128)S(1)} %get-tuple-element.25.near_ref, s32[17]{0:T(128)S(1)} %collective-permute-done.8.far_ref, bf16[4,32,384]{2,1,0:T(8,128)(2,1)S(1)} %get-tuple-element.37.refs_0_, ...), custom_call_target="tpu_custom_call" | custom-call | bytes 1 | tf_op jit(solution)/shard_map/sum_blocks/pallas_call | solution.py:316
  39.6 0.2 collective-permute-done.19.refs_4_
  39.8 1.6 %finish_blocks.1 = f32[16,32,384]{2,1,0:T(8,128)} custom-call(s32[2]{0:T(128)S(1)} %pad_add_fusion.here_ref, s32[17]{0:T(128)S(1)} %get-tuple-element.25.near_ref, s32[17]{0:T(128)S(1)} %collective-permute-done.11.far_ref, f32[16,32,384]{2,1,0:T(8,128)S(1)} %sum_blocks.1.own_ref, bf16[4,32,384]{2,1,0:T(8,128)(2,1)S(1)} %collective-permute-done.15.refs_0_, ...), custom_call_target="tpu_custom_call" | custom-call | bytes 1 | tf_op jit(solution)/shard_map/finish_blocks/pallas_call | solution.py:325
  (19 shorter events, 0.1 us)
Async XLA Ops:
  0.0 17.7 %collective-permute-start.3 = (bf16[256,12288]{1,0:T(8,128)(2,1)}, bf16[256,12288]{1,0:T(8,128)(2,1)}, u32[]{:S(2)}, u32[]{:S(2)}) collective-permute-start(bf16[256,12288]{1,0:T(8,128)(2,1)} %bitcast.3), channel_id=1, source_target_pairs={{0,1},{1,0},{2,3},{3,2},{4,5},{5,4},{6,7},{7,6},{8,9},{9,8},{10,11... | collective-permute-start | bytes 18874376 | tf_op jit(solution)/shard_map/ppermute | solution.py:18
  0.5 11.9 %collective-permute-start.4 = (bf16[16,32,384]{2,1,0:T(8,128)(2,1)}, bf16[16,32,384]{2,1,0:T(8,128)(2,1)S(1)}, u32[]{:S(2)}, u32[]{:S(2)}) collective-permute-start(bf16[16,32,384]{2,1,0:T(8,128)(2,1)} %own_ref.1), channel_id=1, source_target_pairs={{0,2},{1,13},{2,0},{3,15},{4,6},{5,9},{6,4},{7,11},{8,10},{9,5},{1... | collective-permute-start | bytes 1179656 | tf_op jit(solution)/shard_map/ppermute | solution.py:24
  3.0 7.8 %collective-permute-start = (s32[1,32]{1,0:T(1,128)}, s32[1,32]{1,0:T(1,128)S(1)}, u32[]{:S(2)}, u32[]{:S(2)}) collective-permute-start(s32[1,32]{1,0:T(1,128)} %list_ref.1), channel_id=1, source_target_pairs={{0,6},{1,7},{2,4},{3,5},{4,2},{5,3},{6,0},{7,1},{8,14},{9,15},{10,... | collective-permute-start | bytes 392 | tf_op jit(solution)/shard_map/ppermute | solution.py:24
  4.5 6.3 %collective-permute-start.1 = (s32[1,32]{1,0:T(1,128)}, s32[1,32]{1,0:T(1,128)S(1)}, u32[]{:S(2)}, u32[]{:S(2)}) collective-permute-start(s32[1,32]{1,0:T(1,128)} %list_ref.1), channel_id=1, source_target_pairs={{0,4},{1,5},{2,6},{3,7},{4,0},{5,1},{6,2},{7,3},{8,12},{9,13},{10,... | collective-permute-start | bytes 392 | tf_op jit(solution)/shard_map/ppermute | solution.py:24
  4.6 6.3 %collective-permute-start.2 = (s32[1,32]{1,0:T(1,128)}, s32[1,32]{1,0:T(1,128)S(1)}, u32[]{:S(2)}, u32[]{:S(2)}) collective-permute-start(s32[1,32]{1,0:T(1,128)} %list_ref.1), channel_id=1, source_target_pairs={{0,2},{1,3},{2,0},{3,1},{4,6},{5,7},{6,4},{7,5},{8,10},{9,11},{10,... | collective-permute-start | bytes 392 | tf_op jit(solution)/shard_map/ppermute | solution.py:24
  6.5 15.8 %copy-start = (f32[1,256]{1,0:T(1,128)S(1)}, f32[1,256]{1,0:T(1,128)}, u32[]{:S(2)}) copy-start(f32[1,256]{1,0:T(1,128)} %weight_ref.1) | copy-start | bytes 3076
  13.9 7.0 %collective-permute-start.5 = (bf16[4,32,384]{2,1,0:T(8,128)(2,1)S(1)}, bf16[4,32,384]{2,1,0:T(8,128)(2,1)S(1)}, u32[]{:S(2)}, u32[]{:S(2)}) collective-permute-start(bf16[4,32,384]{2,1,0:T(8,128)(2,1)S(1)} %get-tuple-element.29), channel_id=1, source_target_pairs={{0,6},{1,7},{2,4},{3,5},{4,2},{5,3},{6,0},{7,1},{8,14},{9,15},{10,... | collective-permute-start | bytes 294920 | tf_op jit(solution)/shard_map/ppermute | solution.py:24
  15.5 6.9 %collective-permute-start.6 = (bf16[4,32,384]{2,1,0:T(8,128)(2,1)S(1)}, bf16[4,32,384]{2,1,0:T(8,128)(2,1)S(1)}, u32[]{:S(2)}, u32[]{:S(2)}) collective-permute-start(bf16[4,32,384]{2,1,0:T(8,128)(2,1)S(1)} %get-tuple-element.30), channel_id=1, source_target_pairs={{0,2},{1,3},{2,0},{3,1},{4,6},{5,7},{6,4},{7,5},{8,10},{9,11},{10,... | collective-permute-start | bytes 294920 | tf_op jit(solution)/shard_map/ppermute | solution.py:24
  17.0 5.3 %collective-permute-start.7 = (bf16[4,32,384]{2,1,0:T(8,128)(2,1)S(1)}, bf16[4,32,384]{2,1,0:T(8,128)(2,1)S(1)}, u32[]{:S(2)}, u32[]{:S(2)}) collective-permute-start(bf16[4,32,384]{2,1,0:T(8,128)(2,1)S(1)} %get-tuple-element.31), channel_id=1, source_target_pairs={{0,4},{1,5},{2,6},{3,7},{4,0},{5,1},{6,2},{7,3},{8,12},{9,13},{10,... | collective-permute-start | bytes 294920 | tf_op jit(solution)/shard_map/ppermute | solution.py:24
  17.5 7.2 %collective-permute-start.8 = (s32[17]{0:T(128)S(1)}, s32[17]{0:T(128)S(1)}, u32[]{:S(2)}, u32[]{:S(2)}) collective-permute-start(s32[17]{0:T(128)S(1)} %search_lists.1.ids_ref), channel_id=1, source_target_pairs={{0,2},{1,13},{2,0},{3,15},{4,6},{5,9},{6,4},{7,11},{8,10},{9,5},{1... | collective-permute-start | bytes 212 | tf_op jit(solution)/shard_map/ppermute | solution.py:24
  24.8 1.3 %collective-permute-start.9 = (f32[2,40,256]{2,1,0:T(8,128)S(1)}, f32[2,40,256]{2,1,0:T(8,128)S(1)}, u32[]{:S(2)}, u32[]{:S(2)}) collective-permute-start(f32[2,40,256]{2,1,0:T(8,128)S(1)} %predict.1.mine_ref), channel_id=1, source_target_pairs={{0,1},{1,0},{2,3},{3,2},{4,5},{5,4},{6,7},{7,6},{8,9},{9,8},{10,11... | collective-permute-start | bytes 245768 | tf_op jit(solution)/shard_map/ppermute | solution.py:18
  27.8 7.9 %collective-permute-start.10 = (bf16[4,32,384]{2,1,0:T(8,128)(2,1)S(1)}, bf16[4,32,384]{2,1,0:T(8,128)(2,1)S(1)}, u32[]{:S(2)}, u32[]{:S(2)}) collective-permute-start(bf16[4,32,384]{2,1,0:T(8,128)(2,1)S(1)} %get-tuple-element.34), channel_id=1, source_target_pairs={{0,6},{1,11},{2,4},{3,9},{4,2},{5,15},{6,0},{7,13},{8,14},{9,3},{1... | collective-permute-start | bytes 294920 | tf_op jit(solution)/shard_map/ppermute | solution.py:24
  29.6 6.3 %collective-permute-start.12 = (bf16[4,32,384]{2,1,0:T(8,128)(2,1)S(1)}, bf16[4,32,384]{2,1,0:T(8,128)(2,1)S(1)}, u32[]{:S(2)}, u32[]{:S(2)}) collective-permute-start(bf16[4,32,384]{2,1,0:T(8,128)(2,1)S(1)} %get-tuple-element.39), channel_id=1, source_target_pairs={{0,4},{1,9},{2,6},{3,11},{4,0},{5,13},{6,2},{7,15},{8,12},{9,1},{1... | collective-permute-start | bytes 294920 | tf_op jit(solution)/shard_map/ppermute | solution.py:24
  30.0 6.2 %collective-permute-start.13 = (bf16[4,32,384]{2,1,0:T(8,128)(2,1)S(1)}, bf16[4,32,384]{2,1,0:T(8,128)(2,1)S(1)}, u32[]{:S(2)}, u32[]{:S(2)}) collective-permute-start(bf16[4,32,384]{2,1,0:T(8,128)(2,1)S(1)} %get-tuple-element.40), channel_id=1, source_target_pairs={{0,2},{1,15},{2,0},{3,13},{4,6},{5,11},{6,4},{7,9},{8,10},{9,7},{1... | collective-permute-start | bytes 294920 | tf_op jit(solution)/shard_map/ppermute | solution.py:24
  31.4 6.6 %collective-permute-start.14 = (bf16[4,32,384]{2,1,0:T(8,128)(2,1)S(1)}, bf16[4,32,384]{2,1,0:T(8,128)(2,1)S(1)}, u32[]{:S(2)}, u32[]{:S(2)}) collective-permute-start(bf16[4,32,384]{2,1,0:T(8,128)(2,1)S(1)} %get-tuple-element.37.refs_0_), channel_id=1, source_target_pairs={{0,2},{1,13},{2,0},{3,15},{4,6},{5,9},{6,4},{7,11},{8,10},{9,5},{1... | collective-permute-start | bytes 294920 | tf_op jit(solution)/shard_map/ppermute | solution.py:24
  32.1 3.3 %collective-permute-start.11 = (s32[17]{0:T(128)S(1)}, s32[17]{0:T(128)S(1)}, u32[]{:S(2)}, u32[]{:S(2)}) collective-permute-start(s32[17]{0:T(128)S(1)} %collective-permute-done.8.far_ref), channel_id=1, source_target_pairs={{0,1},{1,0},{2,3},{3,2},{4,5},{5,4},{6,7},{7,6},{8,9},{9,8},{10,11... | collective-permute-start | bytes 212 | tf_op jit(solution)/shard_map/ppermute | solution.py:18
  35.4 4.2 %collective-permute-start.15 = (bf16[4,32,384]{2,1,0:T(8,128)(2,1)S(1)}, bf16[4,32,384]{2,1,0:T(8,128)(2,1)S(1)}, u32[]{:S(2)}, u32[]{:S(2)}) collective-permute-start(bf16[4,32,384]{2,1,0:T(8,128)(2,1)S(1)} %get-tuple-element.37.refs_0_), channel_id=1, source_target_pairs={{0,1},{1,0},{2,3},{3,2},{4,5},{5,4},{6,7},{7,6},{8,9},{9,8},{10,11... | collective-permute-start | bytes 294920 | tf_op jit(solution)/shard_map/ppermute | solution.py:18
  35.7 3.9 %collective-permute-start.16 = (bf16[4,32,384]{2,1,0:T(8,128)(2,1)S(1)}, bf16[4,32,384]{2,1,0:T(8,128)(2,1)S(1)}, u32[]{:S(2)}, u32[]{:S(2)}) collective-permute-start(bf16[4,32,384]{2,1,0:T(8,128)(2,1)S(1)} %collective-permute-done.10.refs_1_), channel_id=1, source_target_pairs={{0,1},{1,0},{2,3},{3,2},{4,5},{5,4},{6,7},{7,6},{8,9},{9,8},{10,11... | collective-permute-start | bytes 294920 | tf_op jit(solution)/shard_map/ppermute | solution.py:18
  35.9 3.7 %collective-permute-start.17 = (bf16[4,32,384]{2,1,0:T(8,128)(2,1)S(1)}, bf16[4,32,384]{2,1,0:T(8,128)(2,1)S(1)}, u32[]{:S(2)}, u32[]{:S(2)}) collective-permute-start(bf16[4,32,384]{2,1,0:T(8,128)(2,1)S(1)} %collective-permute-done.12.refs_2_), channel_id=1, source_target_pairs={{0,1},{1,0},{2,3},{3,2},{4,5},{5,4},{6,7},{7,6},{8,9},{9,8},{10,11... | collective-permute-start | bytes 294920 | tf_op jit(solution)/shard_map/ppermute | solution.py:18
  36.2 3.4 %collective-permute-start.18 = (bf16[4,32,384]{2,1,0:T(8,128)(2,1)S(1)}, bf16[4,32,384]{2,1,0:T(8,128)(2,1)S(1)}, u32[]{:S(2)}, u32[]{:S(2)}) collective-permute-start(bf16[4,32,384]{2,1,0:T(8,128)(2,1)S(1)} %collective-permute-done.13.refs_3_), channel_id=1, source_target_pairs={{0,1},{1,0},{2,3},{3,2},{4,5},{5,4},{6,7},{7,6},{8,9},{9,8},{10,11... | collective-permute-start | bytes 294920 | tf_op jit(solution)/shard_map/ppermute | solution.py:18
  38.0 1.8 %collective-permute-start.19 = (bf16[4,32,384]{2,1,0:T(8,128)(2,1)S(1)}, bf16[4,32,384]{2,1,0:T(8,128)(2,1)S(1)}, u32[]{:S(2)}, u32[]{:S(2)}) collective-permute-start(bf16[4,32,384]{2,1,0:T(8,128)(2,1)S(1)} %collective-permute-done.14.refs_4_), channel_id=1, source_target_pairs={{0,1},{1,0},{2,3},{3,2},{4,5},{5,4},{6,7},{7,6},{8,9},{9,8},{10,11... | collective-permute-start | bytes 294920 | tf_op jit(solution)/shard_map/ppermute | solution.py:18
